TPU v7x, 32 devices: a whole 2x2x4 slice. The times are simulated.
32 devices in a mesh: dp: 8 (over y, x, core), seq: 4 (over z).
Axes of the slice: x: 2, y: 2, z: 4, core: 2. Of those that a mesh axis runs over, the one named last changes fastest.
Arguments:
- hidden: float32 [16, 1024, 1536], P('dp', 'seq'), may hold values from -6 to 6
- out_grad: float32 [16, 1024, 1536], P('dp', 'seq'), may hold values from -6 to 6
- lengths: int32 [16], P('dp'), may hold values from 256 to 1024, as said below
- norm_gain: bfloat16 [2, 1536], P(None, ('dp', 'seq')), may hold values from 0.5 to 1.5
- in_proj: bfloat16 [2, 1536, 6448], P(None, ('dp', 'seq')), may hold values from -0.15625 to 0.15625
- conv_weight: bfloat16 [2, 4, 3328], P(None, None, ('dp', 'seq')), may hold values from -3 to 3
- gate_gain: bfloat16 [2, 3072], P(None, ('dp', 'seq')), may hold values from 0.5 to 1.5
- out_proj: bfloat16 [2, 3072, 1536], P(None, ('dp', 'seq')), may hold values from -0.109375 to 0.109375
- dt_bias: float32 [2, 48], replicated, may hold values from -9.5 to -3.5
- a_log: float32 [2, 48], replicated, may hold values from 0 to 1.5
- d_skip: float32 [2, 48], replicated, may hold values from 0.5 to 1.5
Outputs:
- result: float32 [16, 1024, 1536], P('dp', 'seq')
- grad_hidden: float32 [16, 1024, 1536], P('dp', 'seq')
- grad_norm_gain: float32 [2, 1536], P(None, ('dp', 'seq'))
- grad_in_proj: float32 [2, 1536, 6448], P(None, ('dp', 'seq'))
- grad_conv_weight: float32 [2, 4, 3328], P(None, None, ('dp', 'seq'))
- grad_gate_gain: float32 [2, 3072], P(None, ('dp', 'seq'))
- grad_out_proj: float32 [2, 3072, 1536], P(None, ('dp', 'seq'))
- grad_dt_bias: float32 [2, 48], replicated
- grad_a_log: float32 [2, 48], replicated
- grad_d_skip: float32 [2, 48], replicated
Inputs may be any that keep to these rules, and one draw needn't show every extreme that they name: Positions from lengths[b] on are padding. Among the 2 slots of each index of dp, one has length 1024 and another 256.
All inputs are finite; a program needn't handle non-finite values.
Results may differ from a plain program's by a relative error of at most 0.0084.
Values may be sent and summed in bfloat16 or wider, within the bound.
A program may use at most 448 MiB of HBM per device.

v0:
```python
import jax
import jax.numpy as jnp
from jax import lax
from jax.sharding import PartitionSpec as P

D = 1536
HEADS = 48
HEADDIM = 64
NSTATE = 128
CONV = 4
LAYERS = 2
MICRO = 2
INNER = 3072
CONVCH = 3328
PROJ = 6448


epsilon = 1e-05
exact_product = lax.Precision.HIGHEST


def passed_along(value, axis, steps):
    count = lax.axis_size(axis)
    initial, last = (max(0, -steps), min(count, count - steps))
    return lax.ppermute(value, axis, [(source, source + steps) for source in range(initial, last)])


def norm_rows(vector, gain_row):
    inverse_rms = lax.rsqrt(jnp.mean(vector * vector, axis=-1, keepdims=True) + epsilon)
    return vector * inverse_rms * gain_row


def front_part(extended, raw_step, conv_kernel, step_bias, decay_log):
    length = extended.shape[1] - conv_kernel.shape[0] + 1
    convolved = conv_kernel[0] * extended[:, 0:length]
    for offset in range(1, conv_kernel.shape[0]):
        convolved = convolved + conv_kernel[offset] * extended[:, offset : offset + length]
    activated = jax.nn.silu(convolved)
    values = activated[..., :INNER].reshape(activated.shape[0], length, HEADS, HEADDIM)
    input_map = activated[..., INNER : INNER + NSTATE]
    output_map = activated[..., INNER + NSTATE :]
    step_size = jax.nn.softplus(raw_step + step_bias)
    log_decay = -step_size * jnp.exp(decay_log)
    return (values, input_map, output_map, step_size, log_decay)


def mix_out(values, input_map, output_map, step_size, log_decay, skip_gain, state_in):
    cumulative = jnp.cumsum(log_decay, axis=1)
    length = log_decay.shape[1]
    causal = (jnp.arange(length)[:, None] >= jnp.arange(length)[None, :])[None, :, :, None]
    spread = cumulative[:, :, None, :] - cumulative[:, None, :, :]
    decays = jnp.where(causal, jnp.exp(jnp.where(causal, spread, 0.0)), 0.0)
    intersection = jnp.einsum("stn,srn->str", output_map, input_map, precision=exact_product)
    weights = decays * intersection[..., None] * step_size[:, None, :, :]
    mixture = jnp.einsum("strh,srhp->sthp", weights, values, precision=exact_product)
    carried = jnp.einsum("stn,shpn->sthp", output_map, state_in, precision=exact_product)
    return mixture + carried * jnp.exp(cumulative)[..., None] + skip_gain[:, None] * values


def state_part(values, input_map, step_size, log_decay):
    cumulative = jnp.cumsum(log_decay, axis=1)
    remaining = jnp.exp(cumulative[:, -1:, :] - cumulative) * step_size
    weighted = remaining[..., None] * values
    return jnp.einsum("srhp,srn->shpn", weighted, input_map, precision=exact_product)


def mixing(values, input_map, output_map, step_size, log_decay, skip_gain, state_in):
    mixture = mix_out(values, input_map, output_map, step_size, log_decay, skip_gain, state_in)
    total_decay = jnp.exp(jnp.sum(log_decay, axis=1))
    state_out = total_decay[..., None, None] * state_in + state_part(
        values, input_map, step_size, log_decay
    )
    return (mixture, state_out)


def gate_part(mixture, gate_in, gate_gain):
    gated = mixture.reshape(gate_in.shape) * jax.nn.silu(gate_in)
    return norm_rows(gated, gate_gain)


def outer_sum(left_rows, right_rows):
    return lax.dot_general(
        left_rows, right_rows, (((0,), (0,)), ((), ())), preferred_element_type=jnp.float32
    )


def transposed_product(left_rows, right_rows):
    return lax.dot_general(
        left_rows, right_rows, (((1,), (1,)), ((), ())), preferred_element_type=jnp.float32
    )


def pack_grads(members, leading):
    grad_norm, grad_in_weight, grad_kernel, grad_gate_gain, grad_out_weight = members
    count = 1
    for extent in leading:
        count = count * extent
    kernel_rows = jnp.transpose(grad_kernel.reshape(CONV, count, -1), (1, 0, 2))
    return (
        grad_norm.reshape(leading + (-1,)),
        grad_in_weight.reshape(leading + (8, -1)),
        kernel_rows,
        grad_gate_gain.reshape(leading + (-1,)),
        grad_out_weight.reshape(leading + (8, -1)),
    )


def unpack_grads(shares):
    return (
        shares[0].reshape(-1),
        shares[1].reshape(-1, PROJ),
        shares[2].reshape(CONV, -1),
        shares[3].reshape(-1),
        shares[4].reshape(-1, D),
    )


def body(
    hidden,
    out_grad,
    lengths,
    norm_gain,
    in_proj,
    conv_weight,
    gate_gain,
    out_proj,
    dt_bias,
    a_log,
    d_skip,
):
    seq_count = lax.axis_size("seq")
    data_count = lax.axis_size("dp")
    piece_len = hidden.shape[1]
    micro_size = hidden.shape[0] // MICRO
    positions = lax.axis_index("seq") * piece_len + jnp.arange(piece_len, dtype=jnp.int32)
    valid_all = (positions[None, :] < lengths[:, None]).astype(jnp.float32)[..., None]
    kept_layers = []
    for layer_index in range(LAYERS):
        kept_layers.append(
            (
                lax.all_gather(norm_gain[layer_index], ("dp", "seq"), axis=0, tiled=True),
                lax.all_gather(in_proj[layer_index], ("dp", "seq"), axis=0, tiled=True),
                lax.all_gather(conv_weight[layer_index], ("dp", "seq"), axis=1, tiled=True),
                lax.all_gather(gate_gain[layer_index], ("dp", "seq"), axis=0, tiled=True),
                lax.all_gather(out_proj[layer_index], ("dp", "seq"), axis=0, tiled=True),
            )
        )

    def chain_backward(total_decay, local_grad):

        def relay_back(step_index, incoming):
            return passed_along(
                (total_decay[..., None, None] * incoming + local_grad).astype(jnp.bfloat16),
                "seq",
                -1,
            ).astype(jnp.float32)

        return lax.fori_loop(0, seq_count - 1, relay_back, jnp.zeros_like(local_grad))

    def layer_backward(grad_next, valid_rows, gathered, layer_index, saved):
        gain_norm, input_weight, kernel, gain_gate, output_weight = gathered
        current, projected_rows, edge_rows, state_in, normalized_output, normalized_input = saved
        grad_branch = (valid_rows * grad_next).astype(jnp.bfloat16)
        grad_rows = grad_branch.reshape(-1, D)
        grad_normed_out = transposed_product(grad_rows, output_weight)
        gate_in = projected_rows[..., :INNER]
        conv_in = projected_rows[..., INNER : INNER + CONVCH]
        raw_step = projected_rows[..., INNER + CONVCH :]
        extended = jnp.concatenate([edge_rows, conv_in], axis=1)
        front_out, front_back = jax.vjp(
            front_part,
            extended,
            raw_step,
            kernel.astype(jnp.float32),
            dt_bias[layer_index],
            a_log[layer_index],
        )
        values, input_map, output_map, step_size, log_decay = front_out
        mix_values, mix_back = jax.vjp(
            mixing,
            values,
            input_map,
            output_map,
            step_size,
            log_decay,
            d_skip[layer_index],
            state_in,
        )
        gate_values, gate_back = jax.vjp(
            gate_part, mix_values[0], gate_in, gain_gate.astype(jnp.float32)
        )
        grad_mixture, grad_gate_in, grad_gate_gain = gate_back(
            grad_normed_out.reshape(gate_values.shape)
        )
        cumulative = jnp.cumsum(log_decay, axis=1)
        local_grad = jnp.einsum(
            "sthp,stn->shpn",
            grad_mixture * jnp.exp(cumulative)[..., None],
            output_map,
            precision=exact_product,
        )
        total_decay = jnp.exp(jnp.sum(log_decay, axis=1))
        grad_state_out = chain_backward(total_decay, local_grad)
        grad_values, grad_input_map, grad_output_map, grad_step, grad_log, grad_skip, unused = (
            mix_back((grad_mixture, grad_state_out))
        )
        grad_extended, grad_raw, grad_kernel, grad_bias, grad_decay_log = front_back(
            (grad_values, grad_input_map, grad_output_map, grad_step, grad_log)
        )
        returned = passed_along(
            grad_extended[:, : CONV - 1].astype(jnp.bfloat16), "seq", -1
        ).astype(jnp.float32)
        grad_conv_in = grad_extended[:, CONV - 1 :] + jnp.pad(
            returned, ((0, 0), (piece_len - (CONV - 1), 0), (0, 0))
        )
        grad_projected = jnp.concatenate([grad_gate_in, grad_conv_in, grad_raw], axis=-1).astype(
            jnp.bfloat16
        )
        grad_proj_rows = grad_projected.reshape(-1, PROJ)
        grad_normed = transposed_product(grad_proj_rows, input_weight).reshape(current.shape)
        norm_values, norm_back = jax.vjp(norm_rows, current, gain_norm.astype(jnp.float32))
        grad_current, grad_norm = norm_back(grad_normed)
        small_grads = (grad_norm, grad_kernel, grad_gate_gain, grad_bias, grad_decay_log, grad_skip)
        product_rows = (
            normalized_input.reshape(-1, D),
            grad_proj_rows,
            normalized_output.reshape(-1, INNER),
            grad_rows,
        )
        return (grad_next + grad_current, small_grads, product_rows)

    totals = []
    row_store = []
    for layer_index in range(LAYERS):
        totals.append(
            [
                jnp.zeros((D,), jnp.float32),
                jnp.zeros((CONV, CONVCH), jnp.float32),
                jnp.zeros((INNER,), jnp.float32),
                jnp.zeros((HEADS,), jnp.float32),
                jnp.zeros((HEADS,), jnp.float32),
                jnp.zeros((HEADS,), jnp.float32),
            ]
        )
        row_store.append([[], [], [], []])
    results = []
    grads_in = []
    for micro_index in range(MICRO):
        first_row = micro_index * micro_size
        current = hidden[first_row : first_row + micro_size]
        valid_rows = valid_all[first_row : first_row + micro_size]
        saved_all = []
        for layer_index in range(LAYERS):
            gathered = kept_layers[layer_index]
            (
                layer_gain_norm,
                layer_input_weight,
                layer_kernel,
                layer_gain_gate,
                layer_output_weight,
            ) = gathered
            layer_normalized_input = norm_rows(current, layer_gain_norm.astype(jnp.float32)).astype(
                jnp.bfloat16
            )
            layer_projected_rows = jnp.einsum(
                "yji,ip->yjp",
                layer_normalized_input,
                layer_input_weight,
                preferred_element_type=jnp.float32,
            )
            layer_gate_in = layer_projected_rows[..., :INNER]
            layer_conv_in = layer_projected_rows[..., INNER : INNER + CONVCH]
            layer_raw_step = layer_projected_rows[..., INNER + CONVCH :]
            layer_edge_rows = passed_along(layer_conv_in[:, piece_len - (CONV - 1) :], "seq", 1)
            layer_extended = jnp.concatenate([layer_edge_rows, layer_conv_in], axis=1)
            layer_values, layer_input_map, layer_output_map, layer_step_size, layer_log_decay = (
                front_part(
                    layer_extended,
                    layer_raw_step,
                    layer_kernel.astype(jnp.float32),
                    dt_bias[layer_index],
                    a_log[layer_index],
                )
            )
            layer_total_decay = jnp.exp(jnp.sum(layer_log_decay, axis=1))
            chain_total_decay = layer_total_decay
            local_state = state_part(
                layer_values, layer_input_map, layer_step_size, layer_log_decay
            )

            def relay_step(step_index, incoming):
                return passed_along(
                    chain_total_decay[..., None, None] * incoming + local_state, "seq", 1
                )

            layer_state_in = lax.fori_loop(
                0, seq_count - 1, relay_step, jnp.zeros_like(local_state)
            )
            mixture = mix_out(
                layer_values,
                layer_input_map,
                layer_output_map,
                layer_step_size,
                layer_log_decay,
                d_skip[layer_index],
                layer_state_in,
            )
            layer_normalized_output = gate_part(
                mixture, layer_gate_in, layer_gain_gate.astype(jnp.float32)
            ).astype(jnp.bfloat16)
            branch_output = jnp.einsum(
                "nrc,co->nro",
                layer_normalized_output,
                layer_output_weight,
                preferred_element_type=jnp.float32,
            )
            current, saved = (
                current + valid_rows * branch_output,
                (
                    current,
                    layer_projected_rows,
                    layer_edge_rows,
                    layer_state_in,
                    layer_normalized_output,
                    layer_normalized_input,
                ),
            )
            saved_all.append(saved)
        results.append(current)
        grad_next = out_grad[first_row : first_row + micro_size]
        for layer_index in reversed(range(LAYERS)):
            gathered = kept_layers[layer_index]
            grad_next, small_grads, product_rows = layer_backward(
                grad_next, valid_rows, gathered, layer_index, saved_all[layer_index]
            )
            totals[layer_index] = [
                running + added for running, added in zip(totals[layer_index], small_grads)
            ]
            for member in range(4):
                row_store[layer_index][member].append(product_rows[member])
        grads_in.append(grad_next)
    share_lists = [[], [], [], [], []]
    for layer_index in range(LAYERS):
        stored = [jnp.concatenate(row_store[layer_index][member], axis=0) for member in range(4)]
        grad_in_weight = outer_sum(stored[0], stored[1])
        grad_out_weight = outer_sum(stored[2], stored[3])
        layer_totals = totals[layer_index]
        members = (
            layer_totals[0],
            grad_in_weight,
            layer_totals[1],
            layer_totals[2],
            grad_out_weight,
        )
        packed = pack_grads(members, (data_count * seq_count,))
        summed = (
            lax.psum_scatter(packed[0], ("dp", "seq"), scatter_dimension=0, tiled=True),
            lax.psum_scatter(packed[1], ("dp", "seq"), scatter_dimension=0, tiled=True),
            lax.psum_scatter(packed[2], ("dp", "seq"), scatter_dimension=0, tiled=True),
            lax.psum_scatter(packed[3], ("dp", "seq"), scatter_dimension=0, tiled=True),
            lax.psum_scatter(packed[4], ("dp", "seq"), scatter_dimension=0, tiled=True),
        )
        shares = unpack_grads(summed)
        for member in range(5):
            share_lists[member].append(shares[member])
    bias_local = jnp.stack([totals[layer_index][3] for layer_index in range(LAYERS)])
    decay_local = jnp.stack([totals[layer_index][4] for layer_index in range(LAYERS)])
    skip_local = jnp.stack([totals[layer_index][5] for layer_index in range(LAYERS)])
    grad_bias, grad_decay, grad_skip = lax.psum(
        (bias_local, decay_local, skip_local), ("dp", "seq")
    )
    result = jnp.concatenate(results, axis=0)
    grad_hidden = jnp.concatenate(grads_in, axis=0)
    return (
        result,
        grad_hidden,
        jnp.stack(share_lists[0]),
        jnp.stack(share_lists[1]),
        jnp.stack(share_lists[2]),
        jnp.stack(share_lists[3]),
        jnp.stack(share_lists[4]),
        grad_bias,
        grad_decay,
        grad_skip,
    )


def solution(mesh):
    placed = (
        P("dp", "seq", None),
        P("dp", "seq", None),
        P("dp"),
        P(None, ("dp", "seq")),
        P(None, ("dp", "seq"), None),
        P(None, None, ("dp", "seq")),
        P(None, ("dp", "seq")),
        P(None, ("dp", "seq"), None),
        P(),
        P(),
        P(),
    )
    return jax.shard_map(
        body,
        mesh=mesh,
        in_specs=placed,
        out_specs=(
            P("dp", "seq", None),
            P("dp", "seq", None),
            P(None, ("dp", "seq")),
            P(None, ("dp", "seq"), None),
            P(None, None, ("dp", "seq")),
            P(None, ("dp", "seq")),
            P(None, ("dp", "seq"), None),
            P(),
            P(),
            P(),
        ),
        check_vma=False,
    )
```

profile of v0, /device:TPU:0, one launch (start us, length us, event | category | flops | bytes accessed | tf_op | source)
XLA Modules:
  0.0 3268.4 jit_solution(4492304726880197903)
XLA Ops:
  14.1 42.7 %all-reduce.65 = (bf16[1536]{0:T(1024)(128)(2,1)S(1)}, bf16[3072]{0:T(1024)(128)(2,1)S(1)}, bf16[1536]{0:T(1024)(128)(2,1)S(1)}, bf16[3072]{0:T(1024)(128)(2,1)S(1)}) all-reduce(bf16[1536]{0:T(1024)(128)(2,1)S(1)} %dynamic-update-slice, bf16[3072]{0:T(1024)(128)(2,1)S(1)} %dynamic-update-slice.1, ...), channel_id=3, replica_groups=mesh['dp'=8,'seq'=4] {'dp','seq'}, use_global_device_ids=true, to_apply=%add.52 | all-reduce | flops 9216 | bytes 36864
  56.9 102.1 %all-gather = bf16[1,4,3328]{1,0,2:T(2,128)(2,1)S(1)} all-gather(bf16[1,4,104]{1,0,2:T(2,128)(2,1)S(1)} %copy.584), channel_id=2, replica_groups=mesh['dp'=8,'seq'=4] {'dp','seq'}, dimensions={2}, use_global_device_ids=true | all-gather | bytes 27456 | tf_op jit(solution)/shard_map/all_gather | solution.py:143
  163.2 109.7 %all-gather.5 = bf16[1,4,3328]{1,0,2:T(2,128)(2,1)S(1)} all-gather(bf16[1,4,104]{1,0,2:T(2,128)(2,1)S(1)} %copy.585), channel_id=7, replica_groups=mesh['dp'=8,'seq'=4] {'dp','seq'}, dimensions={2}, use_global_device_ids=true | all-gather | bytes 27456 | tf_op jit(solution)/shard_map/all_gather | solution.py:143
  282.5 69.7 %slice_reduce_fusion.7 = (f32[3328]{0:T(1024)}, f32[3328]{0:T(1024)}, f32[3328]{0:T(1024)}, f32[3328]{0:T(1024)}) fusion(f32[1,4,3328]{1,0,2:T(1,128)S(1)} %copy-done.23), kind=kLoop, calls=%fused_computation.418 | loop fusion | bytes 106496 | tf_op jit(solution)/shard_map/slice | solution.py:35
  352.2 70.1 %slice_reduce_fusion.3 = (f32[3328]{0:T(1024)}, f32[3328]{0:T(1024)}, f32[3328]{0:T(1024)}, f32[3328]{0:T(1024)}) fusion(f32[1,4,3328]{1,0,2:T(1,128)S(1)} %copy-done.24), kind=kLoop, calls=%fused_computation.414 | loop fusion | bytes 106496 | tf_op jit(solution)/shard_map/slice | solution.py:35
  430.8 13.6 fusion.40
  446.4 14.8 fusion.43
  495.1 18.1 fusion.171
  523.0 114.6 %while.84 = (s32[]{:T(128)}, f32[1,48,64,128]{3,2,1,0:T(8,128)S(1)}, f32[1,48]{1,0:T(1,128)S(1)}, f32[1,48,64,128]{3,2,1,0:T(8,128)S(1)}, s32[]{:T(128)}) while((s32[]{:T(128)}, f32[1,48,64,128]{3,2,1,0:T(8,128)S(1)}, f32[1,48]{1,0:T(1,128)S(1)}, f32[1,48,64,128]{3,2,1,0:T(8,128)S(1)}, s32[]{:T(128)}) %tuple.397), condition=%wide.region_5.6_spmd, body=%wide.region_4.5_spmd.sunk | while | flops 786434 | bytes 11010341 | solution.py:296
  527.4 33.7 %collective-permute-done = f32[1,48,64,128]{3,2,1,0:T(8,128)S(1)} collective-permute-done((f32[1,48,64,128]{3,2,1,0:T(8,128)}, f32[1,48,64,128]{3,2,1,0:T(8,128)S(1)}, u32[]{:S(2)}, u32[]{:S(2)}) %collective-permute-start) | collective-permute-done | bytes 1572896 | tf_op jit(solution)/shard_map/while/body/eval_jaxpr/ppermute | solution.py:25
  566.8 32.8 %collective-permute-done = f32[1,48,64,128]{3,2,1,0:T(8,128)S(1)} collective-permute-done((f32[1,48,64,128]{3,2,1,0:T(8,128)}, f32[1,48,64,128]{3,2,1,0:T(8,128)S(1)}, u32[]{:S(2)}, u32[]{:S(2)}) %collective-permute-start) | collective-permute-done | bytes 1572896 | tf_op jit(solution)/shard_map/while/body/eval_jaxpr/ppermute | solution.py:25
  605.3 31.9 collective-permute-done
  643.3 14.5 fusion.215
  668.8 107.5 %while.86 = (s32[]{:T(128)}, f32[1,48,64,128]{3,2,1,0:T(8,128)S(1)}, f32[1,48]{1,0:T(1,128)S(1)}, f32[1,48,64,128]{3,2,1,0:T(8,128)S(1)}, s32[]{:T(128)}) while((s32[]{:T(128)}, f32[1,48,64,128]{3,2,1,0:T(8,128)S(1)}, f32[1,48]{1,0:T(1,128)S(1)}, f32[1,48,64,128]{3,2,1,0:T(8,128)S(1)}, s32[]{:T(128)}) %tuple.395), condition=%wide.region_19.20_spmd, body=%wide.region_18.19_spmd.sunk | while | flops 786434 | bytes 11010341 | solution.py:296
  674.5 31.0 collective-permute-done.2
  711.2 30.0 collective-permute-done.2
  747.0 29.1 collective-permute-done.2
  781.9 14.7 fusion.213
  818.4 13.1 fusion.46
  833.5 14.7 fusion.49
  883.5 18.7 fusion.170
  907.7 100.0 %while.85 = (s32[]{:T(128)}, f32[1,48,64,128]{3,2,1,0:T(8,128)S(1)}, f32[1,48]{1,0:T(1,128)S(1)}, f32[1,48,64,128]{3,2,1,0:T(8,128)S(1)}, s32[]{:T(128)}) while((s32[]{:T(128)}, f32[1,48,64,128]{3,2,1,0:T(8,128)S(1)}, f32[1,48]{1,0:T(1,128)S(1)}, f32[1,48,64,128]{3,2,1,0:T(8,128)S(1)}, s32[]{:T(128)}) %tuple.401), condition=%wide.region_12.13_spmd, body=%wide.region_11.12_spmd.sunk | while | flops 786434 | bytes 11010341 | solution.py:296
  912.1 28.8 collective-permute-done.1
  946.7 28.8 collective-permute-done.1
  981.2 26.4 collective-permute-done.1
  1013.0 14.8 fusion.214
  1040.8 100.3 %while.87 = (s32[]{:T(128)}, f32[1,48,64,128]{3,2,1,0:T(8,128)S(1)}, f32[1,48]{1,0:T(1,128)S(1)}, f32[1,48,64,128]{3,2,1,0:T(8,128)}, s32[]{:T(128)}) while((s32[]{:T(128)}, f32[1,48,64,128]{3,2,1,0:T(8,128)S(1)}, f32[1,48]{1,0:T(1,128)S(1)}, f32[1,48,64,128]{3,2,1,0:T(8,128)}, s32[]{:T(128)}) %tuple.399), condition=%wide.region_26.27_spmd, body=%wide.region_25.26_spmd.sunk | while | flops 786434 | bytes 11010341 | solution.py:296
  1047.9 27.4 collective-permute-done.3
  1082.5 27.4 collective-permute-done.3
  1117.0 23.8 collective-permute-done.3
  1146.5 15.0 fusion.212
  1177.4 13.7 multiply_reduce_fusion.21
  1196.6 63.9 %while.88 = (s32[]{:T(128)}, f32[1,48,64,128]{3,2,1,0:T(8,128)}, f32[1,48]{1,0:T(1,128)S(1)}, f32[1,48,64,128]{3,2,1,0:T(8,128)}, s32[]{:T(128)}, /*index=5*/s32[]{:T(128)}) while((s32[]{:T(128)}, f32[1,48,64,128]{3,2,1,0:T(8,128)}, f32[1,48]{1,0:T(1,128)S(1)}, f32[1,48,64,128]{3,2,1,0:T(8,128)}, s32[]{:T(128)}, ...), condition=%wide.region_35.37_spmd.clone, body=%wide.region_34.36_spmd.clone.sunk | while | flops 1966083 | bytes 9437495 | solution.py:158
  1200.5 14.9 collective-permute-done.4
  1222.2 15.9 collective-permute-done.4
  1244.9 13.2 collective-permute-done.4
  1275.8 70.3 %while.90 = (s32[]{:T(128)}, f32[1,48,64,128]{3,2,1,0:T(8,128)}, f32[1,48]{1,0:T(1,128)S(1)}, f32[1,48,64,128]{3,2,1,0:T(8,128)}, s32[]{:T(128)}, /*index=5*/s32[]{:T(128)}) while((s32[]{:T(128)}, f32[1,48,64,128]{3,2,1,0:T(8,128)}, f32[1,48]{1,0:T(1,128)S(1)}, f32[1,48,64,128]{3,2,1,0:T(8,128)}, s32[]{:T(128)}, ...), condition=%wide.region_75.77_spmd.clone, body=%wide.region_74.76_spmd.clone.sunk | while | flops 1966083 | bytes 9437495 | solution.py:158
  1279.6 17.9 collective-permute-done.6
  1304.2 19.2 collective-permute-done.6
  1330.2 13.2 collective-permute-done.6
  1376.5 25.5 fusion.69
  1444.6 12.8 bitcast_add_fusion.3
  1457.4 14.4 multiply_reduce_fusion.6
  1547.8 12.7 fusion.297
  1599.7 61.3 %while.89 = (s32[]{:T(128)}, f32[1,48,64,128]{3,2,1,0:T(8,128)S(1)}, f32[1,48]{1,0:T(1,128)S(1)}, f32[1,48,64,128]{3,2,1,0:T(8,128)S(1)}, s32[]{:T(128)}, /*index=5*/s32[]{:T(128)}) while((s32[]{:T(128)}, f32[1,48,64,128]{3,2,1,0:T(8,128)S(1)}, f32[1,48]{1,0:T(1,128)S(1)}, f32[1,48,64,128]{3,2,1,0:T(8,128)S(1)}, s32[]{:T(128)}, ...), condition=%wide.region_55.57_spmd.clone, body=%wide.region_54.56_spmd.clone.sunk | while | flops 1966083 | bytes 9437495 | solution.py:158
  1602.1 19.7 collective-permute-done.5
  1625.5 17.5 collective-permute-done.5
  1646.8 12.9 collective-permute-done.5
  1675.5 61.1 %while.91 = (s32[]{:T(128)}, f32[1,48,64,128]{3,2,1,0:T(8,128)S(1)}, f32[1,48]{1,0:T(1,128)S(1)}, f32[1,48,64,128]{3,2,1,0:T(8,128)}, s32[]{:T(128)}, /*index=5*/s32[]{:T(128)}) while((s32[]{:T(128)}, f32[1,48,64,128]{3,2,1,0:T(8,128)S(1)}, f32[1,48]{1,0:T(1,128)S(1)}, f32[1,48,64,128]{3,2,1,0:T(8,128)}, s32[]{:T(128)}, ...), condition=%wide.region_95.97_spmd.clone, body=%wide.region_94.96_spmd.clone.sunk | while | flops 1966083 | bytes 9437495 | solution.py:158
  1679.3 16.8 collective-permute-done.7
  1701.3 15.9 collective-permute-done.7
  1722.4 12.9 collective-permute-done.7
  1765.6 25.3 fusion.71
  1847.6 15.1 multiply_reduce_fusion.14
  1964.8 22.5 reshape.2747
  1999.7 22.5 reshape.2746
  2024.1 36.3 %fusion.88 = f32[1536,6448]{1,0:T(8,128)} fusion(bf16[256,48]{0,1:T(8,128)(2,1)S(1)} %bitcast.1423, bf16[256,3328]{0,1:T(8,128)(2,1)S(1)} %copy-done.113, bf16[256,3072]{0,1:T(8,128)(2,1)} %bitcast.1389, bf16[256,48]{0,1:T(8,128)(2,1)S(1)} %bitcast.1421, bf16[256,3328]{0,1:T(8,128)(2,1)S(1)} %copy-done.114, bf16[256,3072]{0,1:T(8,128)(2,1)} %bitcast.1387, ...), kind=kOutput, calls=%fused_computation.112 | convolution fusion | flops 10184589312 | bytes 47792128 | tf_op jit(solution)/shard_map/dot_general | solution.py:82
  2060.5 42.7 %reshape.2739 = f32[32,8,38688]{2,1,0:T(8,128)} reshape(f32[1536,6448]{1,0:T(8,128)} %fusion.88) | data formatting | bytes 79233024 | tf_op jit(solution)/shard_map/reshape | solution.py:101
  2105.5 38.4 %fusion.76 = f32[1536,6448]{1,0:T(8,128)} fusion(bf16[256,48]{0,1:T(8,128)(2,1)S(1)} %bitcast.1427, bf16[256,3328]{0,1:T(8,128)(2,1)S(1)} %copy-done.115, bf16[256,3072]{0,1:T(8,128)(2,1)} %bitcast.1391, bf16[256,48]{0,1:T(8,128)(2,1)S(1)} %bitcast.1425, bf16[256,3328]{0,1:T(8,128)(2,1)S(1)} %copy-done.116, bf16[256,3072]{0,1:T(8,128)(2,1)} %bitcast.1393, ...), kind=kOutput, calls=%fused_computation.100 | convolution fusion | flops 10184589312 | bytes 47792128 | tf_op jit(solution)/shard_map/dot_general | solution.py:82
  2143.9 42.8 %reshape.2738 = f32[32,8,38688]{2,1,0:T(8,128)} reshape(f32[1536,6448]{1,0:T(8,128)} %fusion.76) | data formatting | bytes 79233024 | tf_op jit(solution)/shard_map/reshape | solution.py:101
  2212.0 88.3 %reduce-scatter.11.cloned.1.call-done = f32[1,8,18432]{2,1,0:T(8,128)} async-done(((f32[32,8,18432]{2,1,0:T(8,128)}), f32[1,8,18432]{2,1,0:T(8,128)}) %reduce-scatter.11.cloned.1.call-update) | async-done | bytes 589840 | tf_op jit(solution)/shard_map/reduce_scatter | solution.py:361
  2301.6 212.1 %reduce-scatter.9.cloned.1.call-done = f32[1,8,18432]{2,1,0:T(8,128)} async-done(((f32[32,8,18432]{2,1,0:T(8,128)}), f32[1,8,18432]{2,1,0:T(8,128)}) %reduce-scatter.9.cloned.1.call-update) | async-done | bytes 589840 | tf_op jit(solution)/shard_map/reduce_scatter | solution.py:361
  2516.0 368.7 %reduce-scatter.15.cloned.1.call-done = f32[1,8,38688]{2,1,0:T(8,128)} async-done(((f32[32,8,38688]{2,1,0:T(8,128)}), f32[1,8,38688]{2,1,0:T(8,128)}) %reduce-scatter.15.cloned.1.call-update) | async-done | bytes 1238032
  2887.0 368.8 %reduce-scatter.13.cloned.1.call-done = f32[1,8,38688]{2,1,0:T(8,128)} async-done(((f32[32,8,38688]{2,1,0:T(8,128)}), f32[1,8,38688]{2,1,0:T(8,128)}) %reduce-scatter.13.cloned.1.call-update) | async-done | bytes 1238032
  (1142 shorter events, 798.5 us)
Async XLA Ops:
  7.2 49.6 %copy-start.296 = (bf16[2,4,104]{2,1,0:T(4,128)(2,1)S(1)}, bf16[2,4,104]{2,1,0:T(4,128)(2,1)}, u32[]{:S(2)}) copy-start(bf16[2,4,104]{2,1,0:T(4,128)(2,1)} %param.33) | copy-start | bytes 4996
  7.2 415.1 %all-gather.21.cloned.1.call-start = ((), (), s32[]{:S(2)}) async-start(), calls=%async_computation.9 | async-start | bytes 9732096 | tf_op jit(solution)/shard_map/all_gather | solution.py:145
  9.2 421.6 %all-gather.15.cloned.1.call-start = ((), (), s32[]{:S(2)}) async-start(), calls=%async_computation.6 | async-start | bytes 20680704 | tf_op jit(solution)/shard_map/all_gather | solution.py:142
  11.7 793.4 %all-gather.17.cloned.1.call-start = ((), (), s32[]{:S(2)}) async-start(), calls=%async_computation.7 | async-start | bytes 9732096 | tf_op jit(solution)/shard_map/all_gather | solution.py:145
  12.4 806.0 %all-gather.19.cloned.1.call-start = ((), (), s32[]{:S(2)}) async-start(), calls=%async_computation.8 | async-start | bytes 20680704 | tf_op jit(solution)/shard_map/all_gather | solution.py:142
  13.0 2193.3 %all-reduce.68.cloned.1.call-start = ((), (), s32[]{:S(2)}) async-start(), calls=%async_computation.12 | async-start | bytes 399360
  56.8 223.8 %copy-start.172 = (f32[1536]{0:T(1024)}, f32[1536]{0:T(1024)S(1)}, u32[]{:S(2)}) copy-start(f32[1536]{0:T(1024)S(1)} %convert_element_type.153) | copy-start | bytes 18436
  161.8 115.2 %copy-start.19 = (f32[2,256,1536]{2,1,0:T(8,128)S(1)}, f32[2,256,1536]{2,1,0:T(8,128)}, u32[]{:S(2)}) copy-start(f32[2,256,1536]{2,1,0:T(8,128)} %param.28) | copy-start | bytes 9437188
  278.0 186.4 %copy-start.290 = (f32[48]{0:T(128)}, f32[48]{0:T(128)S(1)}, u32[]{:S(2)}) copy-start(f32[48]{0:T(128)S(1)} %get-tuple-element.591) | copy-start | bytes 580
  278.5 185.9 %copy-start.238 = (f32[48]{0:T(128)}, f32[48]{0:T(128)S(1)}, u32[]{:S(2)}) copy-start(f32[48]{0:T(128)S(1)} %get-tuple-element.589) | copy-start | bytes 580
  282.5 69.7 %copy-start.24 = (f32[1,4,3328]{1,0,2:T(1,128)S(1)}, f32[1,4,3328]{1,0,2:T(1,128)}, u32[]{:S(2)}) copy-start(f32[1,4,3328]{1,0,2:T(1,128)} %convert_element_type.150) | copy-start | bytes 159748
  352.2 70.1 %copy-start.128 = (bf16[256,1536]{1,0:T(8,128)(2,1)S(1)}, bf16[256,1536]{1,0:T(8,128)(2,1)}, u32[]{:S(2)}) copy-start(bf16[256,1536]{1,0:T(8,128)(2,1)} %get-tuple-element.538) | copy-start | bytes 2359300
  471.4 18.6 collective-permute-start.8
  475.9 16.6 collective-permute-start.10
  480.0 300.3 %copy-start.162 = (f32[256,48]{0,1:T(8,128)}, f32[256,48]{0,1:T(8,128)S(1)}, u32[]{:S(2)}) copy-start(f32[256,48]{0,1:T(8,128)S(1)} %get-tuple-element.489) | copy-start | bytes 147460
  522.8 118.8 %copy-start.143 = (f32[256,256]{1,0:T(8,128)}, f32[256,256]{1,0:T(8,128)S(1)}, u32[]{:S(2)}) copy-start(f32[256,256]{1,0:T(8,128)S(1)} %fusion.420) | copy-start | bytes 786436
  524.4 36.7 %collective-permute-start = (f32[1,48,64,128]{3,2,1,0:T(8,128)}, f32[1,48,64,128]{3,2,1,0:T(8,128)S(1)}, u32[]{:S(2)}, u32[]{:S(2)}) collective-permute-start(f32[1,48,64,128]{3,2,1,0:T(8,128)} %multiply_add_fusion.24), channel_id=1, source_target_pairs={{0,1},{1,2},{2,3},{4,5},{5,6},{6,7},{8,9},{9,10},{10,11},{12,13},{... | collective-permute-start | bytes 4718600 | tf_op jit(solution)/shard_map/while/body/eval_jaxpr/ppermute | solution.py:25
  562.4 37.2 %collective-permute-start = (f32[1,48,64,128]{3,2,1,0:T(8,128)}, f32[1,48,64,128]{3,2,1,0:T(8,128)S(1)}, u32[]{:S(2)}, u32[]{:S(2)}) collective-permute-start(f32[1,48,64,128]{3,2,1,0:T(8,128)} %multiply_add_fusion.24), channel_id=1, source_target_pairs={{0,1},{1,2},{2,3},{4,5},{5,6},{6,7},{8,9},{9,10},{10,11},{12,13},{... | collective-permute-start | bytes 4718600 | tf_op jit(solution)/shard_map/while/body/eval_jaxpr/ppermute | solution.py:25
  601.0 36.3 %collective-permute-start = (f32[1,48,64,128]{3,2,1,0:T(8,128)}, f32[1,48,64,128]{3,2,1,0:T(8,128)S(1)}, u32[]{:S(2)}, u32[]{:S(2)}) collective-permute-start(f32[1,48,64,128]{3,2,1,0:T(8,128)} %multiply_add_fusion.24), channel_id=1, source_target_pairs={{0,1},{1,2},{2,3},{4,5},{5,6},{6,7},{8,9},{9,10},{10,11},{12,13},{... | collective-permute-start | bytes 4718600 | tf_op jit(solution)/shard_map/while/body/eval_jaxpr/ppermute | solution.py:25
  663.6 137.3 %copy-start.249 = (f32[256]{0:T(256)}, f32[256]{0:T(256)S(1)}, u32[]{:S(2)}) copy-start(f32[256]{0:T(256)S(1)} %fusion.501) | copy-start | bytes 3076
  668.6 111.7 %copy-start.145 = (f32[256,256]{1,0:T(8,128)}, f32[256,256]{1,0:T(8,128)S(1)}, u32[]{:S(2)}) copy-start(f32[256,256]{1,0:T(8,128)S(1)} %fusion.410) | copy-start | bytes 786436
  670.1 35.3 %collective-permute-start.2 = (f32[1,48,64,128]{3,2,1,0:T(8,128)}, f32[1,48,64,128]{3,2,1,0:T(8,128)S(1)}, u32[]{:S(2)}, u32[]{:S(2)}) collective-permute-start(f32[1,48,64,128]{3,2,1,0:T(8,128)} %multiply_add_fusion.26), channel_id=1, source_target_pairs={{0,1},{1,2},{2,3},{4,5},{5,6},{6,7},{8,9},{9,10},{10,11},{12,13},{... | collective-permute-start | bytes 4718600 | tf_op jit(solution)/shard_map/while/body/eval_jaxpr/ppermute | solution.py:25
  706.8 34.4 %collective-permute-start.2 = (f32[1,48,64,128]{3,2,1,0:T(8,128)}, f32[1,48,64,128]{3,2,1,0:T(8,128)S(1)}, u32[]{:S(2)}, u32[]{:S(2)}) collective-permute-start(f32[1,48,64,128]{3,2,1,0:T(8,128)} %multiply_add_fusion.26), channel_id=1, source_target_pairs={{0,1},{1,2},{2,3},{4,5},{5,6},{6,7},{8,9},{9,10},{10,11},{12,13},{... | collective-permute-start | bytes 4718600 | tf_op jit(solution)/shard_map/while/body/eval_jaxpr/ppermute | solution.py:25
  742.6 33.5 %collective-permute-start.2 = (f32[1,48,64,128]{3,2,1,0:T(8,128)}, f32[1,48,64,128]{3,2,1,0:T(8,128)S(1)}, u32[]{:S(2)}, u32[]{:S(2)}) collective-permute-start(f32[1,48,64,128]{3,2,1,0:T(8,128)} %multiply_add_fusion.26), channel_id=1, source_target_pairs={{0,1},{1,2},{2,3},{4,5},{5,6},{6,7},{8,9},{9,10},{10,11},{12,13},{... | collective-permute-start | bytes 4718600 | tf_op jit(solution)/shard_map/while/body/eval_jaxpr/ppermute | solution.py:25
  857.0 287.8 %copy-start.166 = (f32[256,48]{0,1:T(8,128)}, f32[256,48]{0,1:T(8,128)S(1)}, u32[]{:S(2)}) copy-start(f32[256,48]{0,1:T(8,128)S(1)} %get-tuple-element.477) | copy-start | bytes 147460
  860.3 18.0 collective-permute-start.9
  866.3 14.6 collective-permute-start.11
  871.6 163.1 %copy-start.160 = (f32[256,48]{0,1:T(8,128)}, f32[256,48]{0,1:T(8,128)S(1)}, u32[]{:S(2)}) copy-start(f32[256,48]{0,1:T(8,128)S(1)} %get-tuple-element.599) | copy-start | bytes 147460
  902.6 108.8 %copy-start.148 = (f32[256,256]{1,0:T(8,128)}, f32[256,256]{1,0:T(8,128)S(1)}, u32[]{:S(2)}) copy-start(f32[256,256]{1,0:T(8,128)S(1)} %fusion.415) | copy-start | bytes 786436
  909.1 31.8 collective-permute-start.1
  942.3 33.2 %collective-permute-start.1 = (f32[1,48,64,128]{3,2,1,0:T(8,128)}, f32[1,48,64,128]{3,2,1,0:T(8,128)S(1)}, u32[]{:S(2)}, u32[]{:S(2)}) collective-permute-start(f32[1,48,64,128]{3,2,1,0:T(8,128)} %multiply_add_fusion.25), channel_id=1, source_target_pairs={{0,1},{1,2},{2,3},{4,5},{5,6},{6,7},{8,9},{9,10},{10,11},{12,13},{... | collective-permute-start | bytes 4718600 | tf_op jit(solution)/shard_map/while/body/eval_jaxpr/ppermute | solution.py:25
  976.9 30.8 collective-permute-start.1
  1034.7 110.2 %copy-start.151 = (f32[256,256]{1,0:T(8,128)}, f32[256,256]{1,0:T(8,128)S(1)}, u32[]{:S(2)}) copy-start(f32[256,256]{1,0:T(8,128)S(1)} %fusion.405) | copy-start | bytes 786436
  1043.5 31.8 collective-permute-start.3
  1078.1 31.8 collective-permute-start.3
  1112.7 28.2 collective-permute-start.3
  1199.2 16.2 collective-permute-start.4
  1220.9 17.2 collective-permute-start.4
  1243.6 14.5 collective-permute-start.4
  1278.3 19.1 collective-permute-start.6
  1303.0 20.5 collective-permute-start.6
  1328.9 14.5 collective-permute-start.6
  1352.9 49.0 %copy-start.131 = (f32[256,48]{0,1:T(8,128)}, f32[256,48]{0,1:T(8,128)S(1)}, u32[]{:S(2)}) copy-start(f32[256,48]{0,1:T(8,128)S(1)} %get-tuple-element.611) | copy-start | bytes 147460
  1376.5 38.0 %copy-start.315 = (f32[48]{0:T(128)S(1)}, f32[48]{0:T(128)}, u32[]{:S(2)}) copy-start(f32[48]{0:T(128)} %get-tuple-element.349) | copy-start | bytes 580
  1432.1 39.7 %slice-start.5 = ((s8[6602752]{0:T(1024)(128)(4,1)}), s8[4194304]{0:T(1024)(128)(4,1)S(1)}, s32[]{:S(2)}) async-start(s8[6602752]{0:T(1024)(128)(4,1)} %bitcast.1338), calls=%async_computation.18 | async-start | bytes 8388608
  1500.0 24.8 collective-permute-start.14
  1511.0 19.7 collective-permute-start.12
  1600.8 21.0 collective-permute-start.5
  1624.3 18.8 collective-permute-start.5
  1645.5 14.2 collective-permute-start.5
  1678.0 18.1 collective-permute-start.7
  1700.0 17.2 collective-permute-start.7
  1721.1 14.2 collective-permute-start.7
  1742.2 48.7 %copy-start.133 = (f32[256,48]{0,1:T(8,128)}, f32[256,48]{0,1:T(8,128)S(1)}, u32[]{:S(2)}) copy-start(f32[256,48]{0,1:T(8,128)S(1)} %get-tuple-element.617) | copy-start | bytes 147460
  1822.5 40.2 %slice-start.3 = ((s8[6602752]{0:T(1024)(128)(4,1)}), s8[4194304]{0:T(1024)(128)(4,1)S(1)}, s32[]{:S(2)}) async-start(s8[6602752]{0:T(1024)(128)(4,1)} %bitcast.1336), calls=%async_computation.16 | async-start | bytes 8388608
  1890.7 27.1 collective-permute-start.15
  1901.9 21.9 collective-permute-start.13
  1953.8 346.5 %reduce-scatter.11.cloned.1.call-start = ((), (), s32[]{:S(2)}) async-start(), calls=%async_computation.5 | async-start | bytes 19464192 | tf_op jit(solution)/shard_map/reduce_scatter | solution.py:361
  1987.3 526.3 %reduce-scatter.9.cloned.1.call-start = ((), (), s32[]{:S(2)}) async-start(), calls=%async_computation.4 | async-start | bytes 19464192 | tf_op jit(solution)/shard_map/reduce_scatter | solution.py:361
  2022.2 862.4 %reduce-scatter.15.cloned.1.call-start = ((), (), s32[]{:S(2)}) async-start(), calls=%async_computation.11 | async-start | bytes 40955904
  2103.3 1152.5 %reduce-scatter.13.cloned.1.call-start = ((), (), s32[]{:S(2)}) async-start(), calls=%async_computation.10 | async-start | bytes 40955904
  2887.0 372.8 %copy-start.309 = (f32[2,48]{1,0:T(2,128)S(1)}, f32[2,48]{1,0:T(2,128)}, u32[]{:S(2)}) copy-start(f32[2,48]{1,0:T(2,128)} %get-tuple-element.975) | copy-start | bytes 1156
  2887.0 373.3 %copy-start.308 = (f32[2,48]{1,0:T(2,128)S(1)}, f32[2,48]{1,0:T(2,128)}, u32[]{:S(2)}) copy-start(f32[2,48]{1,0:T(2,128)} %get-tuple-element.976) | copy-start | bytes 1156
  2887.0 373.9 %copy-start.307 = (f32[2,48]{1,0:T(2,128)S(1)}, f32[2,48]{1,0:T(2,128)}, u32[]{:S(2)}) copy-start(f32[2,48]{1,0:T(2,128)} %get-tuple-element.977) | copy-start | bytes 1156
  (313 other events, 2619.7 us)
Sparse Core Ops, SparseCore 0:
  10.8 94.4 all-gather.20
  108.7 164.7 all-gather.14
  276.3 82.4 all-gather.16
  362.1 128.7 all-gather.18
  1953.9 131.2 all-reduce.67
  2092.6 207.6 reduce-scatter.10
  2307.9 205.7 reduce-scatter.8
  2521.2 363.3 reduce-scatter.14
  2892.2 363.5 reduce-scatter.12
where the time goes:
time: 3280 us; the launch traced here: 3270 us
  waiting for transfers between devices  1580 us (48%)
  matrix products  547 us (17%)
  local copies, waits for them, and re-layouts  422 us (13%)
  other arithmetic  359 us (11%)
  blocking collectives  254 us (8%)
  starting transfers between devices  85.9 us (3%)
    unnamed x12, waiting for transfers between devices  739 us
    ppermute x32, waiting for transfers between devices, passed_along(): lax.ppermute(value, axis, [(source, source + steps) for source in range(i...  541 us
    reduce_scatter x2, waiting for transfers between devices, body(): lax.psum_scatter(packed[4], ('dp', 'seq'), scatter_dimension=0, tiled=True)  300 us
    all_gather x2, blocking collectives, body(): lax.all_gather(conv_weight[layer_index], ('dp', 'seq'), axis=1, tiled=True)  212 us
    dot_general x12, matrix products, mix_out(): jnp.einsum('strh,srhp->sthp', weights, values, precision=exact_product)  182 us
    slice x2, local copies, waits for them, and re-layouts, front_part(): convolved = conv_kernel[0] * extended[:, 0:length]  140 us
    dot_general x4, matrix products, outer_sum(): lax.dot_general(left_rows, right_rows, (((0,), (0,)), ((), ())), preferre...  96.2 us
    ppermute x32, starting transfers between devices, passed_along(): lax.ppermute(value, axis, [(source, source + steps) for source in range(i...  85.5 us
  transfers between devices with their start and end apart: 41, of which 28 were waited for; matrix products, arithmetic and copies ran while one was open for 20% of the time, Pallas kernels for 0%

commit v1 on v0

v1 whole, which is shorter than its diff:
```python
import functools

import jax
import jax.numpy as jnp
from jax import lax
from jax.experimental import pallas as pl
from jax.experimental.pallas import tpu as pltpu
from jax.sharding import PartitionSpec as P

D = 1536
HEADS = 48
HEADDIM = 64
NSTATE = 128
CONV = 4
LAYERS = 2
INNER = 3072
CONVCH = 3328
PROJ = 6448
SLOTS = 2
SHORT = 256

LANES = 128
WIDE = 6656
BLK = 256
NB = INNER // BLK
COLS = 512
PER = BLK // HEADDIM
CHAIN = 512
PARTS = CHAIN // BLK

f32 = jnp.float32
bf16 = jnp.bfloat16
epsilon = 1e-05
VMEM_LIMIT = 58 << 20


def params(**more):
    return pltpu.CompilerParams(vmem_limit_bytes=VMEM_LIMIT, **more)


def for_rows(total, size, function):
    def step(index, carry):
        function(pl.ds(pl.multiple_of(index * size, size), size))
        return carry

    lax.fori_loop(0, total // size, step, 0)


def dot(left, right):
    return jnp.dot(left, right, preferred_element_type=f32)


def dot_nt(left, right):
    return lax.dot_general(left, right, (((1,), (1,)), ((), ())), preferred_element_type=f32)


def dot_tn(left, right):
    return lax.dot_general(left, right, (((0,), (0,)), ((), ())), preferred_element_type=f32)


def dot_exact(left, right):
    return jnp.dot(left, right, preferred_element_type=f32, precision=lax.Precision.HIGHEST)


def halves(array):
    high = array.astype(bf16)
    return high, (array - high.astype(f32)).astype(bf16)


def dot_halves(left, right, product=dot):
    left_high, left_low = left
    right_high, right_low = right
    return product(left_high, right_high) + product(left_high, right_low) + product(left_low, right_high)


def dot_member(array, member):
    high, low = halves(array)
    return dot(high, member) + dot(low, member)


def sigmoid(vector):
    return 0.5 + 0.5 * jnp.tanh(0.5 * vector)


def softplus(vector):
    return jnp.maximum(vector, 0.0) + jnp.log1p(jnp.exp(-jnp.abs(vector)))


def spread(columns):
    length = columns.shape[0]
    return jnp.concatenate(
        [jnp.broadcast_to(columns[:, j : j + 1], (length, HEADDIM)) for j in range(PER)], axis=1
    )


def heads_first(columns, block):
    return pltpu.roll(columns, lax.rem(LANES - PER * block, LANES), 1)


def load_extended(scratch, edge_ref, rows_ref):
    scratch[0:8, :] = edge_ref[0]
    scratch[8:, :] = rows_ref[0]


def convolve(scratch, taps, length):
    total = taps[0:1] * scratch[5 : 5 + length, :]
    for k in range(1, CONV):
        total = total + taps[k : k + 1] * scratch[5 + k : 5 + k + length, :]
    return total


def lower(length):
    first = lax.broadcasted_iota(jnp.int32, (length, length), 0)
    second = lax.broadcasted_iota(jnp.int32, (length, length), 1)
    return first >= second


def project_kernel(h_ref, gain_ref, w_ref, proj_ref, raw_ref, normed_ref):
    step = pl.program_id(0)
    total = h_ref.shape[0]

    @pl.when(step == 0)
    def _():
        def one(rows):
            h = h_ref[rows, :]
            inverse = lax.rsqrt(jnp.mean(h * h, axis=-1, keepdims=True) + epsilon)
            normed_ref[rows, :] = (h * inverse * gain_ref[...]).astype(bf16)

        for_rows(total, 32, one)

    product = dot(normed_ref[...], w_ref[...])
    proj_ref[...] = product

    @pl.when(step == pl.num_programs(0) - 1)
    def _():
        raw_ref[...] = product[:, COLS - 2 * LANES : COLS - LANES]


def project(h, gain_row, weight):
    total = h.shape[0]
    return pl.pallas_call(
        project_kernel,
        name="project",
        grid=(WIDE // COLS,),
        in_specs=[
            pl.BlockSpec((total, D), lambda n: (0, 0)),
            pl.BlockSpec((1, D), lambda n: (0, 0)),
            pl.BlockSpec((D, COLS), lambda n: (0, n)),
        ],
        out_specs=[
            pl.BlockSpec((total, COLS), lambda n: (0, n)),
            pl.BlockSpec((total, LANES), lambda n: (0, 0)),
            pl.BlockSpec((total, D), lambda n: (0, 0)),
        ],
        out_shape=[
            jax.ShapeDtypeStruct((total, WIDE), f32),
            jax.ShapeDtypeStruct((total, LANES), f32),
            jax.ShapeDtypeStruct((total, D), bf16),
        ],
        compiler_params=params(),
        cost_estimate=pl.CostEstimate(
            flops=2 * total * D * WIDE, bytes_accessed=2 * D * WIDE, transcendentals=0
        ),
    )(h, gain_row, weight)


def mix_kernel(
    rows_ref, edge_ref, taps_ref, maps_ref, maps_edge_ref, maps_taps_ref, raw_ref, heads_ref, skip_ref,
    y_ref, state_ref, cum_ref, step_ref, act_ref, decay_ref,
    extended, inner, cum_t, input_t,
):
    block = pl.program_id(1)
    length = rows_ref.shape[1]

    @pl.when(block == 0)
    def _():
        load_extended(extended, maps_edge_ref, maps_ref)
        convolved = convolve(extended, maps_taps_ref[...], length)
        maps = convolved * sigmoid(convolved)
        act_ref[0] = maps
        products = dot_halves(halves(maps[:, NSTATE:]), halves(maps[:, :NSTATE]), dot_nt)
        input_t[0], input_t[1] = halves(maps[:, :NSTATE].T)
        causal = lower(length)
        inner[...] = jnp.where(causal, products, 0.0)
        size = softplus(raw_ref[0] + heads_ref[0:1, :])
        decay = -size * jnp.exp(heads_ref[1:2, :])
        cum = dot_exact(causal.astype(f32), decay)
        cum_ref[0] = cum
        step_ref[0] = size
        cum_t[...] = cum.T

    load_extended(extended, edge_ref, rows_ref)
    convolved = convolve(extended, taps_ref[...], length)
    values = convolved * sigmoid(convolved)
    cum = heads_first(cum_ref[0], block)
    stepped = values * spread(heads_first(step_ref[0], block))
    low = stepped.astype(bf16)
    parts = []
    for j in range(PER):
        row = cum_t[pl.ds(block * PER + j, 1), :]
        column = cum[:, j : j + 1]
        pieces = []
        for first in range(0, length, LANES):
            end = first + LANES
            decays = jnp.exp(jnp.minimum(column[first:end] - row[:, :end], 0.0))
            weights = (inner[first:end, :end] * decays).astype(bf16)
            pieces.append(dot(weights, low[:end, j * HEADDIM : (j + 1) * HEADDIM]))
        parts.append(jnp.concatenate(pieces, axis=0))
    y_ref[0] = jnp.concatenate(parts, axis=1) + skip_ref[...] * values
    final = cum[length - 1 :, :]
    remaining = jnp.exp(final - cum)
    state_ref[0] = dot_halves((input_t[0], input_t[1]), halves(stepped * spread(remaining)))
    decay_ref[0] = jnp.broadcast_to(spread(jnp.exp(final)), (8, BLK))


def mix(proj, edge, taps, raw, heads, skip_row):
    length = proj.shape[1]
    return pl.pallas_call(
        mix_kernel,
        name="mix",
        grid=(SLOTS, NB),
        in_specs=[
            pl.BlockSpec((1, length, BLK), lambda s, b: (s, 0, NB + b)),
            pl.BlockSpec((1, 8, BLK), lambda s, b: (s, 0, b)),
            pl.BlockSpec((8, BLK), lambda s, b: (0, b)),
            pl.BlockSpec((1, length, BLK), lambda s, b: (s, 0, 2 * NB)),
            pl.BlockSpec((1, 8, BLK), lambda s, b: (s, 0, NB)),
            pl.BlockSpec((8, BLK), lambda s, b: (0, NB)),
            pl.BlockSpec((1, length, LANES), lambda s, b: (s, 0, 0)),
            pl.BlockSpec((8, LANES), lambda s, b: (0, 0)),
            pl.BlockSpec((1, BLK), lambda s, b: (0, b)),
        ],
        out_specs=[
            pl.BlockSpec((1, length, BLK), lambda s, b: (s, 0, b)),
            pl.BlockSpec((1, NSTATE, BLK), lambda s, b: (s, 0, b)),
            pl.BlockSpec((1, length, LANES), lambda s, b: (s, 0, 0)),
            pl.BlockSpec((1, length, LANES), lambda s, b: (s, 0, 0)),
            pl.BlockSpec((1, length, BLK), lambda s, b: (s, 0, 0)),
            pl.BlockSpec((1, 8, BLK), lambda s, b: (s, 0, b)),
        ],
        out_shape=[
            jax.ShapeDtypeStruct((SLOTS, length, INNER), f32),
            jax.ShapeDtypeStruct((SLOTS, NSTATE, INNER), f32),
            jax.ShapeDtypeStruct((SLOTS, length, LANES), f32),
            jax.ShapeDtypeStruct((SLOTS, length, LANES), f32),
            jax.ShapeDtypeStruct((SLOTS, length, BLK), f32),
            jax.ShapeDtypeStruct((SLOTS, 8, INNER), f32),
        ],
        scratch_shapes=[
            pltpu.VMEM((length + 8, BLK), f32),
            pltpu.VMEM((length, length), f32),
            pltpu.VMEM((LANES, length), f32),
            pltpu.VMEM((2, NSTATE, length), bf16),
        ],
        compiler_params=params(),
        cost_estimate=pl.CostEstimate(flops=6 * 10**9, bytes_accessed=10**7, transcendentals=10**7),
    )(proj, edge, taps, proj, edge, taps, raw, heads, skip_row)


def branch_kernel(
    y_ref, gate_ref, act_ref, cum_ref, state_ref, gain_ref, w_ref, h_ref, valid_ref,
    out_ref, mixture_ref, inverse_ref,
    total, squares, gated_low,
):
    block = pl.program_id(0)
    count = state_ref.shape[0]
    rows = y_ref.shape[0]
    length = rows // SLOTS

    @pl.when(block == 0)
    def _():
        total[...] = jnp.zeros_like(total)
        squares[...] = jnp.zeros_like(squares)

    for slot in range(SLOTS):
        span = slice(slot * length, (slot + 1) * length)
        mixture = y_ref[span, :]
        if slot < count:
            cum = heads_first(cum_ref[span, :], block)
            carried = dot_member(act_ref[span, NSTATE:], state_ref[slot, 0])
            mixture = mixture + carried * spread(jnp.exp(cum))
        gate = gate_ref[span, :]
        gated = mixture * gate * sigmoid(gate)
        mixture_ref[span, :] = mixture
        square = gated * gated
        squares[span, :] += square[:, :LANES] + square[:, LANES:]
        gated_low[span, :] = (gated * gain_ref[...]).astype(bf16)
    total[...] += dot(gated_low[...], w_ref[...])

    @pl.when(block == NB - 1)
    def _():
        def one(span):
            mean = jnp.sum(squares[span, :], axis=-1, keepdims=True) / INNER
            inverse = lax.rsqrt(mean + epsilon)
            inverse_ref[span, :] = jnp.broadcast_to(inverse, (32, LANES))
            factor = inverse * valid_ref[span, 0:1]
            out_ref[span, :] = h_ref[span, :] + factor * total[span, :]

        for_rows(rows, 32, one)


def branch(y, proj, act, cum, state, gain_row, weight, h, valid):
    rows = h.shape[0]
    count = state.shape[0]
    return pl.pallas_call(
        branch_kernel,
        name="branch",
        grid=(NB,),
        in_specs=[
            pl.BlockSpec((rows, BLK), lambda b: (0, b)),
            pl.BlockSpec((rows, BLK), lambda b: (0, b)),
            pl.BlockSpec((rows, BLK), lambda b: (0, 0)),
            pl.BlockSpec((rows, LANES), lambda b: (0, 0)),
            pl.BlockSpec((count, 1, NSTATE, BLK), lambda b: (0, b // PARTS, 0, b % PARTS)),
            pl.BlockSpec((1, BLK), lambda b: (0, b)),
            pl.BlockSpec((BLK, D), lambda b: (b, 0)),
            pl.BlockSpec((rows, D), lambda b: (0, 0)),
            pl.BlockSpec((rows, LANES), lambda b: (0, 0)),
        ],
        out_specs=[
            pl.BlockSpec((rows, D), lambda b: (0, 0)),
            pl.BlockSpec((rows, BLK), lambda b: (0, b)),
            pl.BlockSpec((rows, LANES), lambda b: (0, 0)),
        ],
        out_shape=[
            jax.ShapeDtypeStruct((rows, D), f32),
            jax.ShapeDtypeStruct((rows, INNER), f32),
            jax.ShapeDtypeStruct((rows, LANES), f32),
        ],
        scratch_shapes=[
            pltpu.VMEM((rows, D), f32),
            pltpu.VMEM((rows, LANES), f32),
            pltpu.VMEM((rows, BLK), bf16),
        ],
        compiler_params=params(),
        cost_estimate=pl.CostEstimate(
            flops=2 * rows * D * INNER, bytes_accessed=2 * D * INNER, transcendentals=10**6
        ),
    )(y, proj, act, cum, state, gain_row, weight, h, valid)


def unbranch_kernel(
    g_ref, valid_ref, mixture_ref, gate_ref, inverse_ref, gain_ref, w_ref,
    back_ref, mean_ref, gain_out_ref, w_out_ref,
    low, norm_low,
):
    block = pl.program_id(0)
    rows = g_ref.shape[0]

    @pl.when(block == 0)
    def _():
        def one(span):
            low[span, :] = (valid_ref[span, 0:1] * g_ref[span, :]).astype(bf16)

        for_rows(rows, 32, one)
        mean_ref[...] = jnp.zeros_like(mean_ref)

    back_ref[...] = dot_nt(low[...], w_ref[...])
    gain_out_ref[...] = jnp.zeros_like(gain_out_ref)

    def one(span):
        gate = gate_ref[span, :]
        gated = mixture_ref[span, :] * gate * sigmoid(gate)
        back = back_ref[span, :]
        unit = gated * inverse_ref[span, 0:1]
        norm_low[span, :] = (unit * gain_ref[...]).astype(bf16)
        gain_out_ref[0:1, :] += jnp.sum(back * unit, axis=0, keepdims=True)
        product = gated * back * gain_ref[...]
        mean_ref[span, :] += product[:, :LANES] + product[:, LANES:]

    for_rows(rows, 128, one)
    w_out_ref[...] = dot_tn(norm_low[...], low[...]).astype(bf16)

    @pl.when(block == NB - 1)
    def _():
        mean_ref[...] = jnp.broadcast_to(
            jnp.sum(mean_ref[...], axis=-1, keepdims=True) / INNER, mean_ref.shape
        )


def unbranch(g, valid, mixture, proj, inverse, gain_row, weight):
    rows = g.shape[0]
    return pl.pallas_call(
        unbranch_kernel,
        name="unbranch",
        grid=(NB,),
        in_specs=[
            pl.BlockSpec((rows, D), lambda b: (0, 0)),
            pl.BlockSpec((rows, LANES), lambda b: (0, 0)),
            pl.BlockSpec((rows, BLK), lambda b: (0, b)),
            pl.BlockSpec((rows, BLK), lambda b: (0, b)),
            pl.BlockSpec((rows, LANES), lambda b: (0, 0)),
            pl.BlockSpec((1, BLK), lambda b: (0, b)),
            pl.BlockSpec((BLK, D), lambda b: (b, 0)),
        ],
        out_specs=[
            pl.BlockSpec((rows, BLK), lambda b: (0, b)),
            pl.BlockSpec((rows, LANES), lambda b: (0, 0)),
            pl.BlockSpec((8, BLK), lambda b: (0, b)),
            pl.BlockSpec((BLK, D), lambda b: (b, 0)),
        ],
        out_shape=[
            jax.ShapeDtypeStruct((rows, INNER), f32),
            jax.ShapeDtypeStruct((rows, LANES), f32),
            jax.ShapeDtypeStruct((8, INNER), f32),
            jax.ShapeDtypeStruct((INNER, D), bf16),
        ],
        scratch_shapes=[pltpu.VMEM((rows, D), bf16), pltpu.VMEM((rows, BLK), bf16)],
        compiler_params=params(),
        cost_estimate=pl.CostEstimate(
            flops=4 * rows * D * INNER, bytes_accessed=4 * D * INNER, transcendentals=10**6
        ),
    )(g, valid, mixture, proj, inverse, gain_row, weight)


def ungate_kernel(
    back_ref, mixture_ref, gate_ref, inverse_ref, mean_ref, gain_ref, act_ref, cum_ref,
    dy_ref, dgate_ref, state_ref,
    output_t,
):
    block = pl.program_id(0)
    rows = back_ref.shape[0]
    length = rows // SLOTS

    @pl.when(block == 0)
    def _():
        for slot in range(state_ref.shape[0]):
            span = slice(slot * length, (slot + 1) * length)
            output_t[slot, 0], output_t[slot, 1] = halves(act_ref[span, NSTATE:].T)

    for slot in range(SLOTS):
        span = slice(slot * length, (slot + 1) * length)
        gate = gate_ref[span, :]
        curve = sigmoid(gate)
        mixture = mixture_ref[span, :]
        swish = gate * curve
        inverse = inverse_ref[span, 0:1]
        back = back_ref[span, :] * gain_ref[...]
        pull = inverse * inverse * inverse * mean_ref[span, 0:1]
        grad = inverse * back - (mixture * swish) * pull
        dy = grad * swish
        dy_ref[span, :] = dy
        dgate_ref[span, :] = (grad * mixture * curve * (1.0 + gate * (1.0 - curve))).astype(bf16)
        if slot < state_ref.shape[0]:
            grown = spread(jnp.exp(heads_first(cum_ref[span, :], block)))
            state_ref[slot] = dot_halves((output_t[slot, 0], output_t[slot, 1]), halves(dy * grown))


def ungate(back, mixture, proj, inverse, mean, gain_row, act, cum, count):
    rows = back.shape[0]
    length = rows // SLOTS
    return pl.pallas_call(
        ungate_kernel,
        name="ungate",
        grid=(NB,),
        in_specs=[
            pl.BlockSpec((rows, BLK), lambda b: (0, b)),
            pl.BlockSpec((rows, BLK), lambda b: (0, b)),
            pl.BlockSpec((rows, BLK), lambda b: (0, b)),
            pl.BlockSpec((rows, LANES), lambda b: (0, 0)),
            pl.BlockSpec((rows, LANES), lambda b: (0, 0)),
            pl.BlockSpec((1, BLK), lambda b: (0, b)),
            pl.BlockSpec((rows, BLK), lambda b: (0, 0)),
            pl.BlockSpec((rows, LANES), lambda b: (0, 0)),
        ],
        out_specs=[
            pl.BlockSpec((rows, BLK), lambda b: (0, b)),
            pl.BlockSpec((rows, BLK), lambda b: (0, b)),
            pl.BlockSpec((count, NSTATE, BLK), lambda b: (0, 0, b)),
        ],
        out_shape=[
            jax.ShapeDtypeStruct((rows, INNER), f32),
            jax.ShapeDtypeStruct((rows, WIDE), bf16),
            jax.ShapeDtypeStruct((count, NSTATE, INNER), f32),
        ],
        scratch_shapes=[pltpu.VMEM((count, 2, NSTATE, length), bf16)],
        compiler_params=params(),
        cost_estimate=pl.CostEstimate(flops=10**9, bytes_accessed=2 * 10**7, transcendentals=10**7),
    )(back, mixture, proj, inverse, mean, gain_row, act, cum)


def unmix_kernel(
    rows_ref, edge_ref, taps_ref, maps_ref, maps_edge_ref, maps_taps_ref, raw_ref, heads_ref, skip_ref,
    dy_ref, state_ref, later_ref, cum_ref, step_ref, act_ref, grads_in_ref,
    grads_ref, edge_out_ref, taps_out_ref, heads_out_ref,
    extended, inner, d_inner, cum_t, grad_ext, d_maps, d_cum, d_step, over_rows, sums,
):
    del grads_in_ref
    block = pl.program_id(1)
    length = rows_ref.shape[1]
    count = state_ref.shape[0]

    def conv_back(gradient, taps):
        grad_ext[8 : 8 + length, :] = gradient
        back = taps[0:1] * grad_ext[3 : 3 + length + 8, :]
        for k in range(1, CONV):
            back = back + taps[k : k + 1] * grad_ext[3 - k : 3 - k + length + 8, :]
        edge_out_ref[0] = back[:8]
        grads_ref[0] = back[8:].astype(bf16)
        lines = [
            jnp.sum(gradient * extended[5 + k : 5 + k + length, :], axis=0, keepdims=True)
            for k in range(CONV)
        ]
        lines.append(jnp.zeros((8 - CONV, BLK), f32))
        taps_out_ref[0] = jnp.concatenate(lines, axis=0)

    @pl.when(block == 0)
    def _():
        grad_ext[0:8, :] = jnp.zeros((8, BLK), f32)
        grad_ext[8 + length :, :] = jnp.zeros((8, BLK), f32)
        maps = act_ref[0]
        products = dot_halves(halves(maps[:, :NSTATE]), halves(maps[:, NSTATE:]), dot_nt)
        inner[...] = jnp.where(lower(length).T, products, 0.0)
        cum_t[...] = cum_ref[0].T
        d_inner[...] = jnp.zeros_like(d_inner)
        d_maps[...] = jnp.zeros_like(d_maps)
        d_cum[...] = jnp.zeros_like(d_cum)
        d_step[...] = jnp.zeros_like(d_step)
        over_rows[...] = jnp.zeros_like(over_rows)
        sums[...] = jnp.zeros_like(sums)

    @pl.when(block < NB)
    def _():
        load_extended(extended, edge_ref, rows_ref)
        convolved = convolve(extended, taps_ref[...], length)
        curve = sigmoid(convolved)
        values = convolved * curve
        cum = heads_first(cum_ref[0], block)
        size = spread(heads_first(step_ref[0], block))
        stepped = values * size
        low = stepped.astype(bf16)
        dy = dy_ref[0]
        dy_low = dy.astype(bf16)
        lane = lax.broadcasted_iota(jnp.int32, (1, LANES), 1)
        parts = []
        for j in range(PER):
            head = block * PER + j
            row = cum_t[pl.ds(head, 1), :]
            column = cum[:, j : j + 1]
            dy_head = dy_low[:, j * HEADDIM : (j + 1) * HEADDIM]
            low_head = low[:, j * HEADDIM : (j + 1) * HEADDIM]
            pieces = []
            row_sums = []
            column_sums = None
            for first in range(0, length, LANES):
                end = first + LANES
                decays = jnp.exp(jnp.minimum(row[:, first:] - column[first:end], 0.0))
                products = inner[first:end, first:]
                weights = (products * decays).astype(bf16)
                grads = dot_nt(low_head[first:end], dy_head[first:]) * decays
                d_inner[first:end, first:] += grads
                pieces.append(dot(weights, dy_head[first:]))
                moved = grads * products
                row_sums.append(jnp.sum(moved, axis=1, keepdims=True))
                found = jnp.sum(moved, axis=0, keepdims=True)
                if first:
                    found = jnp.concatenate([jnp.zeros((1, first), f32), found], axis=1)
                column_sums = found if column_sums is None else column_sums + found
            parts.append(jnp.concatenate(pieces, axis=0))
            over_rows[pl.ds(head, 1), :] = column_sums
            d_cum[...] -= jnp.where(lane == head, jnp.concatenate(row_sums, axis=0), 0.0)
        d_stepped = jnp.concatenate(parts, axis=1)
        which = lax.broadcasted_iota(jnp.int32, (BLK, LANES), 0) // HEADDIM + block * PER
        chosen = which == lax.broadcasted_iota(jnp.int32, (BLK, LANES), 1)
        member = chosen.astype(f32)
        member_low = chosen.astype(bf16)
        state = state_ref[0, 0]
        later = later_ref[0, 0]
        maps = act_ref[0]
        remaining = spread(jnp.exp(cum[length - 1 :, :] - cum))
        grown = spread(jnp.exp(cum))
        from_later = dot_member(maps[:, :NSTATE], later) * remaining
        d_stepped = d_stepped + from_later
        left = stepped * remaining
        grown_dy = dy * grown
        used = stepped * from_later
        d_cum[...] += dot_member(grown_dy * dot_member(maps[:, NSTATE:], state) - used, member_low)
        d_maps[:, :NSTATE] += dot_nt(left.astype(bf16), later)
        d_maps[:, NSTATE:] += dot_nt(grown_dy.astype(bf16), state)
        d_step[...] += dot_member(d_stepped * values, member_low)
        lines = jnp.concatenate(
            [
                jnp.sum(used, axis=0, keepdims=True),
                jnp.sum(dy * values, axis=0, keepdims=True),
                jnp.sum(later.astype(f32) * state.astype(f32), axis=0, keepdims=True),
                jnp.zeros((5, BLK), f32),
            ],
            axis=0,
        )
        sums[...] += dot_exact(lines, member)
        d_values = d_stepped * size + skip_ref[...] * dy
        conv_back(d_values * curve * (1.0 + convolved * (1.0 - curve)), taps_ref[...])

    @pl.when(block == NB)
    def _():
        load_extended(extended, maps_edge_ref, maps_ref)
        convolved = convolve(extended, maps_taps_ref[...], length)
        curve = sigmoid(convolved)
        maps = act_ref[0]
        d_both = jnp.where(lower(length).T, d_inner[...], 0.0)
        d_input = d_maps[:, :NSTATE] + dot_halves(halves(d_both), halves(maps[:, NSTATE:]))
        d_output = d_maps[:, NSTATE:] + dot_halves(halves(d_both.T), halves(maps[:, :NSTATE]))
        d_both = jnp.concatenate([d_input, d_output], axis=1)
        conv_back(d_both * curve * (1.0 + convolved * (1.0 - curve)), maps_taps_ref[...])

    @pl.when(block == NB + 1)
    def _():
        final = cum_ref[0][length - 1 :, :]
        at_end = sums[0:1, :] + jnp.exp(final) * sums[2:3, :]
        d_total = d_cum[...] + over_rows[...].T
        position = lax.broadcasted_iota(jnp.int32, (length, 1), 0)
        d_total = d_total + jnp.where(position == length - 1, at_end, 0.0)
        d_decay = dot_exact(lower(length).T.astype(f32), d_total)
        rate = jnp.exp(heads_ref[1:2, :])
        size = step_ref[0]
        d_raw = (d_step[...] - d_decay * rate) * sigmoid(raw_ref[0] + heads_ref[0:1, :])
        grads_ref[0] = jnp.concatenate([d_raw, jnp.zeros_like(d_raw)], axis=1).astype(bf16)
        heads_out_ref[0] = jnp.concatenate(
            [
                jnp.sum(d_raw, axis=0, keepdims=True),
                jnp.sum(d_decay * (-size * rate), axis=0, keepdims=True),
                sums[1:2, :],
                jnp.zeros((5, LANES), f32),
            ],
            axis=0,
        )


def unmix(proj, edge, taps, raw, heads, skip_row, dy, state, later, cum, size, act, grads):
    length = proj.shape[1]
    inside = lambda b: jnp.minimum(b, NB - 1)
    upto = lambda b: jnp.minimum(b, NB)
    return pl.pallas_call(
        unmix_kernel,
        name="unmix",
        grid=(SLOTS, NB + 2),
        in_specs=[
            pl.BlockSpec((1, length, BLK), lambda s, b: (s, 0, NB + inside(b))),
            pl.BlockSpec((1, 8, BLK), lambda s, b: (s, 0, inside(b))),
            pl.BlockSpec((8, BLK), lambda s, b: (0, inside(b))),
            pl.BlockSpec((1, length, BLK), lambda s, b: (s, 0, 2 * NB)),
            pl.BlockSpec((1, 8, BLK), lambda s, b: (s, 0, NB)),
            pl.BlockSpec((8, BLK), lambda s, b: (0, NB)),
            pl.BlockSpec((1, length, LANES), lambda s, b: (s, 0, 0)),
            pl.BlockSpec((8, LANES), lambda s, b: (0, 0)),
            pl.BlockSpec((1, BLK), lambda s, b: (0, inside(b))),
            pl.BlockSpec((1, length, BLK), lambda s, b: (s, 0, inside(b))),
            pl.BlockSpec((1, 1, NSTATE, BLK), lambda s, b: (s, inside(b) // PARTS, 0, inside(b) % PARTS)),
            pl.BlockSpec((1, 1, NSTATE, BLK), lambda s, b: (s, inside(b) // PARTS, 0, inside(b) % PARTS)),
            pl.BlockSpec((1, length, LANES), lambda s, b: (s, 0, 0)),
            pl.BlockSpec((1, length, LANES), lambda s, b: (s, 0, 0)),
            pl.BlockSpec((1, length, BLK), lambda s, b: (s, 0, 0)),
            pl.BlockSpec(memory_space=pl.ANY),
        ],
        out_specs=[
            pl.BlockSpec((1, length, BLK), lambda s, b: (s, 0, NB + b)),
            pl.BlockSpec((1, 8, BLK), lambda s, b: (s, 0, upto(b))),
            pl.BlockSpec((1, 8, BLK), lambda s, b: (s, 0, upto(b))),
            pl.BlockSpec((1, 8, LANES), lambda s, b: (s, 0, 0)),
        ],
        out_shape=[
            jax.ShapeDtypeStruct((SLOTS, length, WIDE), bf16),
            jax.ShapeDtypeStruct((SLOTS, 8, CONVCH), f32),
            jax.ShapeDtypeStruct((SLOTS, 8, CONVCH), f32),
            jax.ShapeDtypeStruct((SLOTS, 8, LANES), f32),
        ],
        input_output_aliases={15: 0},
        scratch_shapes=[
            pltpu.VMEM((length + 8, BLK), f32),
            pltpu.VMEM((length, length), f32),
            pltpu.VMEM((length, length), f32),
            pltpu.VMEM((LANES, length), f32),
            pltpu.VMEM((length + 16, BLK), f32),
            pltpu.VMEM((length, 2 * NSTATE), f32),
            pltpu.VMEM((length, LANES), f32),
            pltpu.VMEM((length, LANES), f32),
            pltpu.VMEM((LANES, length), f32),
            pltpu.VMEM((8, LANES), f32),
        ],
        compiler_params=params(),
        cost_estimate=pl.CostEstimate(flops=2 * 10**10, bytes_accessed=2 * 10**7, transcendentals=10**7),
    )(proj, edge, taps, proj, edge, taps, raw, heads, skip_row, dy, state, later, cum, size, act, grads)


def unproject_kernel(
    grads_ref, late_ref, w_ref, normed_ref, h_ref, g_ref, gain_ref,
    out_ref, gain_out_ref, w_out_ref,
    total, turned, mended,
):
    step = pl.program_id(0)
    rows = h_ref.shape[0]
    length = rows // SLOTS

    @pl.when(step == 0)
    def _():
        total[...] = jnp.zeros_like(total)
        turned[...] = normed_ref[...].T

    mended[...] = grads_ref[...]
    for slot in range(SLOTS):
        span = slice((slot + 1) * length - 16, (slot + 1) * length)
        extra = jnp.concatenate([jnp.zeros((8, COLS), f32), late_ref[slot]], axis=0)
        mended[span, :] = (grads_ref[span, :].astype(f32) + extra).astype(bf16)
    w_out_ref[...] = dot(turned[...], mended[...]).astype(bf16)
    total[...] += dot_nt(mended[...], w_ref[...])

    @pl.when(step == pl.num_programs(0) - 1)
    def _():
        gain_out_ref[...] = jnp.zeros_like(gain_out_ref)

        def one(span):
            h = h_ref[span, :]
            inverse = lax.rsqrt(jnp.mean(h * h, axis=-1, keepdims=True) + epsilon)
            back = total[span, :]
            unit = h * inverse
            gain_out_ref[0:1, :] += jnp.sum(back * unit, axis=0, keepdims=True)
            wanted = back * gain_ref[...]
            mean = jnp.mean(unit * wanted, axis=-1, keepdims=True)
            out_ref[span, :] = g_ref[span, :] + inverse * (wanted - unit * mean)

        for_rows(rows, 32, one)


def unproject(grads, late, weight, normed, h, g, gain_row):
    rows = h.shape[0]
    return pl.pallas_call(
        unproject_kernel,
        name="unproject",
        grid=(WIDE // COLS,),
        in_specs=[
            pl.BlockSpec((rows, COLS), lambda n: (0, n)),
            pl.BlockSpec((SLOTS, 8, COLS), lambda n: (0, 0, n)),
            pl.BlockSpec((D, COLS), lambda n: (0, n)),
            pl.BlockSpec((rows, D), lambda n: (0, 0)),
            pl.BlockSpec((rows, D), lambda n: (0, 0)),
            pl.BlockSpec((rows, D), lambda n: (0, 0)),
            pl.BlockSpec((1, D), lambda n: (0, 0)),
        ],
        out_specs=[
            pl.BlockSpec((rows, D), lambda n: (0, 0)),
            pl.BlockSpec((8, D), lambda n: (0, 0)),
            pl.BlockSpec((D, COLS), lambda n: (0, n)),
        ],
        out_shape=[
            jax.ShapeDtypeStruct((rows, D), f32),
            jax.ShapeDtypeStruct((8, D), f32),
            jax.ShapeDtypeStruct((D, WIDE), bf16),
        ],
        scratch_shapes=[
            pltpu.VMEM((rows, D), f32),
            pltpu.VMEM((D, rows), bf16),
            pltpu.VMEM((rows, COLS), bf16),
        ],
        compiler_params=params(),
        cost_estimate=pl.CostEstimate(
            flops=4 * rows * D * WIDE, bytes_accessed=4 * D * WIDE, transcendentals=0
        ),
    )(grads, late, weight, normed, h, g, gain_row)


MESH = pl.DeviceIdType.MESH
DP_BITS = {"core": 1, "x": 2, "y": 4}
STEPS = ("z1", "z2", "x", "y", "core")


def place():
    dp, z = lax.axis_index("dp"), lax.axis_index("seq")
    return {"y": dp // 4, "x": lax.rem(dp // 2, 2), "core": lax.rem(dp, 2), "z": z, "dp": dp}


def partner(here, step):
    if step == "z1":
        return (here["dp"], here["z"] + 1 - 2 * lax.rem(here["z"], 2))
    if step == "z2":
        return (here["dp"], here["z"] + 2 - 4 * (here["z"] // 2))
    return (here["dp"] + DP_BITS[step] * (1 - 2 * here[step]), here["z"])


def greet(here):
    barrier = pltpu.get_barrier_semaphore()
    for step in STEPS:
        pl.semaphore_signal(barrier, inc=1, device_id=partner(here, step), device_id_type=MESH)
    pl.semaphore_wait(barrier, len(STEPS))


def pieces_of(shapes, split):
    jobs = []
    for index, (rows, columns) in enumerate(shapes):
        parts, colours = split[index]
        height, width = rows // parts, columns // colours
        for part in range(parts):
            for colour in range(colours):
                jobs.append((index, part, colour, part * height, height, colour * width, width))
    waves = []
    for job in jobs:
        if job[2] == 0:
            waves.append([])
        waves[-1].append(job)
    return jobs, waves


def gather_kernel(shapes, split, *refs):
    count = len(shapes)
    shards, wholes = refs[:count], refs[count : 2 * count]
    local_sems, send_sems, recv_sems = refs[2 * count :]
    here = place()
    greet(here)
    jobs, waves = pieces_of(shapes, split)
    own = [
        pltpu.make_async_copy(
            shards[i], wholes[i].at[here["y"], here["x"], here["core"], here["z"]], local_sems.at[i]
        )
        for i in range(count)
    ]
    for copy in own:
        copy.start()

    def make(job, stage):
        index, _, colour, top, height, left, width = job
        order = ("z1", "z2", "x", "y", "core") if colour == 0 else ("z1", "z2", "y", "x", "core")
        done = order[:stage]
        axis = lambda name: slice(None) if name in done else here[name]
        depth = here["z"]
        if "z2" in done:
            depth = slice(None)
        elif "z1" in done:
            depth = pl.ds(here["z"] // 2 * 2, 2)
        rows, columns = pl.ds(top, height), pl.ds(left, width)
        target = wholes[index].at[axis("y"), axis("x"), axis("core"), depth, rows, columns]
        source = shards[index].at[rows, columns] if stage == 0 else target
        number = jobs.index(job)
        return pltpu.make_async_remote_copy(
            src_ref=source,
            dst_ref=target,
            send_sem=send_sems.at[number, stage],
            recv_sem=recv_sems.at[number, stage],
            device_id=partner(here, order[stage]),
            device_id_type=MESH,
        )

    stages = len(STEPS)
    for tick in range(len(waves) + stages):
        if tick == 1:
            for copy in own:
                copy.wait()
        for stage in reversed(range(stages + 1)):
            wave = tick - stage
            if not 0 <= wave < len(waves):
                continue
            for job in waves[wave]:
                if stage:
                    make(job, stage - 1).wait()
                if stage < stages:
                    make(job, stage).start()


def gather(shards, split, identity):
    shapes = tuple(shard.shape for shard in shards)
    jobs, _ = pieces_of(shapes, split)
    count = len(shards)
    wholes = pl.pallas_call(
        functools.partial(gather_kernel, shapes, split),
        name="gather",
        in_specs=[pl.BlockSpec(memory_space=pl.ANY)] * count,
        out_specs=[pl.BlockSpec(memory_space=pl.ANY)] * count,
        out_shape=[jax.ShapeDtypeStruct((2, 2, 2, 4) + s.shape, s.dtype) for s in shards],
        scratch_shapes=[
            pltpu.SemaphoreType.DMA((count,)),
            pltpu.SemaphoreType.DMA((len(jobs), len(STEPS))),
            pltpu.SemaphoreType.DMA((len(jobs), len(STEPS))),
        ],
        compiler_params=params(collective_id=identity, has_side_effects=True),
    )(*shards)
    return [whole.reshape((-1,) + whole.shape[4:]) for whole in wholes]


def reduce_kernel(shapes, split, *refs):
    count = len(shapes)
    jobs, waves = pieces_of(shapes, split)
    number = len(jobs)
    partials, heads_in = refs[:count], refs[count]
    totals, heads_out = refs[count + 1 : 2 * count + 1], refs[2 * count + 1]
    rest = refs[2 * count + 2 :]
    kept = rest[:number]
    landed = rest[number : 6 * number]
    heads_landed, local_sems, send_sems, recv_sems, head_send, head_recv = rest[6 * number :]
    here = place()
    greet(here)
    y, x, core, z = here["y"], here["x"], here["core"], here["z"]
    half, odd = z // 2, lax.rem(z, 2)
    stages = len(STEPS)

    def order(job):
        return ("core", "y", "x", "z2", "z1") if job[2] == 0 else ("core", "x", "y", "z2", "z1")

    def area(job, stage, mine):
        pick = lambda value: value if mine else 1 - value
        if stage == 1:
            return (pick(y), slice(None), slice(None)) if job[2] == 0 else (slice(None), pick(x), slice(None))
        if stage == 2:
            return (y, pick(x), slice(None)) if job[2] == 0 else (pick(y), x, slice(None))
        if stage == 3:
            return (y, x, pl.ds(pick(half) * 2, 2))
        return (y, x, half * 2 + pick(odd))

    def load(job):
        index, _, _, top, height, left, width = job
        place_in = partials[index].at[:, :, core, :, pl.ds(top, height), pl.ds(left, width)]
        k = jobs.index(job)
        return pltpu.make_async_copy(place_in, kept[k], local_sems.at[k])

    def make(job, stage):
        index, _, _, top, height, left, width = job
        k = jobs.index(job)
        if stage == 0:
            source = partials[index].at[:, :, 1 - core, :, pl.ds(top, height), pl.ds(left, width)]
        else:
            source = kept[k].at[area(job, stage, False)]
        return pltpu.make_async_remote_copy(
            src_ref=source,
            dst_ref=landed[stage * number + k],
            send_sem=send_sems.at[k, stage],
            recv_sem=recv_sems.at[k, stage],
            device_id=partner(here, order(job)[stage]),
            device_id_type=MESH,
        )

    def add(job, stage, mine):
        k = jobs.index(job)
        into, came = kept[k], landed[(stage - 1) * number + k]
        pick = lambda value: value if mine else 1 - value
        first = job[2] == 0

        def accumulate(target, source):
            into[target] = (into[target].astype(f32) + came[source].astype(f32)).astype(into.dtype)

        if stage == 1:
            def one(i, carry):
                a, b = i // 4, lax.rem(i, 4)
                where = (pick(y), a, b) if first else (a, pick(x), b)
                accumulate(where, where)
                return carry

            lax.fori_loop(0, 8, one, 0)
        elif stage == 2:
            def one(b, carry):
                if first:
                    accumulate((y, pick(x), b), (pick(x), b))
                else:
                    accumulate((pick(y), x, b), (pick(y), b))
                return carry

            lax.fori_loop(0, 4, one, 0)
        elif stage == 3:
            for b in range(2):
                accumulate((y, x, pick(half) * 2 + b), (pick(half) * 2 + b,))
        else:
            accumulate((y, x, half * 2 + pick(odd)), (pick(odd),))

    def finish(job):
        index, _, _, top, height, left, width = job
        k = jobs.index(job)
        summed = kept[k][y, x, z].astype(f32) + landed[4 * number + k][...].astype(f32)
        totals[index][top : top + height, left : left + width] = summed

    def heads_copy(stage):
        return pltpu.make_async_remote_copy(
            src_ref=heads_out,
            dst_ref=heads_landed.at[stage],
            send_sem=head_send.at[stage],
            recv_sem=head_recv.at[stage],
            device_id=partner(here, STEPS[stage]),
            device_id_type=MESH,
        )

    heads_out[...] = heads_in[...]
    for tick in range(len(waves) + stages):
        if tick < stages:
            heads_copy(tick).start()
        for stage in reversed(range(stages + 1)):
            wave = tick - stage
            if not 0 <= wave < len(waves):
                continue
            for job in waves[wave]:
                if stage == 0:
                    make(job, 0).start()
                    load(job).start()
                    continue
                if stage == 1:
                    load(job).wait()
                make(job, stage - 1).wait()
                if stage == stages:
                    finish(job)
                else:
                    add(job, stage, False)
                    make(job, stage).start()
                    add(job, stage, True)
        if tick < stages:
            heads_copy(tick).wait()
            heads_out[...] = heads_out[...] + heads_landed[tick]


def reduce(partials, heads, split, identity):
    shapes = tuple(partial.shape[1:] for partial in partials)
    jobs, _ = pieces_of(shapes, split)
    count = len(partials)
    kept, landed = [], [[] for _ in range(5)]
    for index, _, colour, _, height, _, width in jobs:
        kind = partials[index].dtype
        kept.append(pltpu.VMEM((2, 2, 4, height, width), kind))
        for stage, lead in enumerate(((2, 2, 4), (2, 4), (4,), (2,), ())):
            landed[stage].append(pltpu.VMEM(lead + (height, width), kind))
    tile = pltpu.SemaphoreType.DMA((len(jobs), 5))
    return pl.pallas_call(
        functools.partial(reduce_kernel, shapes, split),
        name="reduce",
        in_specs=[pl.BlockSpec(memory_space=pl.ANY)] * count + [pl.BlockSpec(memory_space=pltpu.VMEM)],
        out_specs=[pl.BlockSpec(memory_space=pltpu.VMEM)] * (count + 1),
        out_shape=[jax.ShapeDtypeStruct(s, f32) for s in shapes] + [jax.ShapeDtypeStruct(heads.shape, f32)],
        scratch_shapes=kept
        + sum(landed, [])
        + [
            pltpu.VMEM((5,) + heads.shape, f32),
            pltpu.SemaphoreType.DMA((len(jobs),)),
            tile,
            tile,
            pltpu.SemaphoreType.DMA((5,)),
            pltpu.SemaphoreType.DMA((5,)),
        ],
        compiler_params=params(collective_id=identity, has_side_effects=True),
    )(*[partial.reshape((2, 2, 2, 4) + partial.shape[1:]) for partial in partials], heads)


def chain_kernel(steps, last, local_ref, decay_ref, state_ref, send_ref, send_sems, recv_sems):
    dp, me = lax.axis_index("dp"), lax.axis_index("seq")
    slots = local_ref.shape[0]
    receives = me > 0 if steps > 0 else me < last
    sends = me < last if steps > 0 else me > 0
    barrier = pltpu.get_barrier_semaphore()

    @pl.when(receives)
    def _():
        pl.semaphore_signal(barrier, inc=1, device_id=(dp, me - steps), device_id_type=MESH)

    @pl.when(sends)
    def _():
        pl.semaphore_wait(barrier, 1)

    def make(slot, part):
        columns = pl.ds(part * CHAIN, CHAIN)
        return pltpu.make_async_remote_copy(
            src_ref=send_ref.at[slot, part],
            dst_ref=state_ref.at[slot, part],
            send_sem=send_sems.at[slot, part],
            recv_sem=recv_sems.at[slot, part],
            device_id=(dp, me + steps),
            device_id_type=MESH,
        )

    parts = [(slot, part) for slot in range(slots) for part in range(INNER // CHAIN)]

    @pl.when(jnp.logical_not(receives))
    def _():
        state_ref[...] = jnp.zeros_like(state_ref)

    for slot, part in parts:
        @pl.when(receives)
        def _():
            make(slot, part).wait_recv()

        @pl.when(sends)
        def _():
            decay = decay_ref[slot, 0:1, part * CHAIN : (part + 1) * CHAIN]
            local = local_ref[slot, :, part * CHAIN : (part + 1) * CHAIN]
            send_ref[slot, part] = (decay * state_ref[slot, part].astype(f32) + local).astype(bf16)
            make(slot, part).start()

    for slot, part in parts:
        @pl.when(sends)
        def _():
            make(slot, part).wait_send()


def chained(local, decay, steps, identity):
    slots = local.shape[0]
    parts = INNER // CHAIN
    shape = (slots, parts, NSTATE, CHAIN)
    return pl.pallas_call(
        functools.partial(chain_kernel, steps, lax.axis_size("seq") - 1),
        name="chain",
        in_specs=[pl.BlockSpec(memory_space=pltpu.VMEM)] * 2,
        out_specs=pl.BlockSpec(memory_space=pltpu.VMEM),
        out_shape=jax.ShapeDtypeStruct(shape, bf16),
        scratch_shapes=[
            pltpu.VMEM(shape, bf16),
            pltpu.SemaphoreType.DMA((slots, parts)),
            pltpu.SemaphoreType.DMA((slots, parts)),
        ],
        compiler_params=params(collective_id=identity, has_side_effects=True),
    )(local, decay)


def passed_along(value, steps):
    count = lax.axis_size("seq")
    initial, last = (max(0, -steps), min(count, count - steps))
    return lax.ppermute(value, "seq", [(source, source + steps) for source in range(initial, last)])


def all_slots(state):
    missing = SLOTS - state.shape[0]
    if missing:
        state = jnp.concatenate([state, jnp.zeros((missing,) + state.shape[1:], state.dtype)], axis=0)
    return state


def padded_rows(array, rows):
    return jnp.pad(array, ((0, rows - array.shape[0]), (0, 0)))


def pack_small(norm_gain, conv_weight, gate_gain):
    pieces = [norm_gain, conv_weight.reshape(LAYERS, -1), gate_gain]
    flat = jnp.concatenate(pieces, axis=1).reshape(-1)
    size = flat.shape[0]
    tiles = -(-size // (16 * LANES)) * 16
    return jnp.pad(flat, (0, tiles * LANES - size)).reshape(tiles, LANES)


def unpack_small(everything, norm_gain, conv_weight, gate_gain):
    count = everything.shape[0]
    size = LAYERS * (norm_gain.shape[1] + conv_weight.shape[1] * conv_weight.shape[2] + gate_gain.shape[1])
    everything = everything.reshape(count, -1)[:, :size].reshape(count, LAYERS, -1)
    everything = jnp.swapaxes(everything, 0, 1).astype(f32)
    first = norm_gain.shape[1]
    second = first + conv_weight.shape[1] * conv_weight.shape[2]
    norm = everything[..., :first].reshape(LAYERS, -1)
    conv = everything[..., first:second].reshape(LAYERS, count, CONV, -1)
    conv = jnp.swapaxes(conv, 1, 2).reshape(LAYERS, CONV, -1)
    gate = everything[..., second:].reshape(LAYERS, -1)
    return norm, conv, gate


def share_small(norm, conv, gate):
    count = lax.axis_size("dp") * lax.axis_size("seq")
    conv = jnp.swapaxes(conv.reshape(LAYERS, CONV, count, -1), 1, 2).reshape(LAYERS, count, -1)
    pieces = [norm.reshape(LAYERS, count, -1), conv, gate.reshape(LAYERS, count, -1)]
    flat = jnp.swapaxes(jnp.concatenate(pieces, axis=-1), 0, 1).reshape(count, -1)
    size = flat.shape[1]
    tiles = -(-size // (16 * LANES)) * 16
    return jnp.pad(flat, ((0, 0), (0, tiles * LANES - size))).reshape(count, tiles, LANES)


def own_small(mine, norm_gain, conv_weight, gate_gain):
    first = norm_gain.shape[1]
    second = first + conv_weight.shape[1] * conv_weight.shape[2]
    width = second + gate_gain.shape[1]
    mine = mine.reshape(-1)[: LAYERS * width].reshape(LAYERS, width)
    return mine[:, :first], mine[:, first:second].reshape(LAYERS, CONV, -1), mine[:, second:]


def body(
    hidden,
    out_grad,
    lengths,
    norm_gain,
    in_proj,
    conv_weight,
    gate_gain,
    out_proj,
    dt_bias,
    a_log,
    d_skip,
):
    length = hidden.shape[1]
    rows = SLOTS * length
    count = 1 if length >= SHORT else SLOTS
    swap = lengths[0] < lengths[1]

    def ordered(array):
        return jnp.where(swap, array[::-1], array)

    positions = lax.axis_index("seq") * length + jnp.arange(length, dtype=jnp.int32)
    valid = (positions[None, :] < ordered(lengths)[:, None]).astype(f32).reshape(rows, 1)
    valid = jnp.broadcast_to(valid, (rows, LANES))
    wide_in = jnp.pad(in_proj, ((0, 0), (0, 0), (0, WIDE - PROJ)))
    small_mesh = lax.axis_size("dp") == 8 and lax.axis_size("seq") == 4
    packed = pack_small(norm_gain, conv_weight, gate_gain)
    if small_mesh:
        shards, split = [packed], [(1, 1)]
        for layer in range(LAYERS):
            shards += [wide_in[layer], out_proj[layer]]
            split += [(3, 2), (3, 2)]
        everything, *wholes = gather(shards, split, 2 * LAYERS)
        wholes = [whole.reshape(-1, whole.shape[-1]) for whole in wholes]
    else:
        everything = lax.all_gather(packed, ("dp", "seq"), axis=0, tiled=False)
        wholes = [
            lax.all_gather(shard, ("dp", "seq"), axis=0, tiled=True)
            for layer in range(LAYERS)
            for shard in (wide_in[layer], out_proj[layer])
        ]
    weights_in, weights_out = wholes[0::2], wholes[1::2]
    norm_all, conv_all, gate_all = unpack_small(everything, norm_gain, conv_weight, gate_gain)
    h = ordered(hidden).reshape(rows, D)
    kept = []
    for layer in range(LAYERS):
        gain_row = norm_all[layer].reshape(1, D)
        gate_row = gate_all[layer].reshape(1, INNER)
        taps = padded_rows(conv_all[layer], 8)
        heads = padded_rows(
            jnp.pad(
                jnp.stack([dt_bias[layer], a_log[layer]]), ((0, 0), (0, LANES - HEADS))
            ),
            8,
        )
        skip_row = jnp.repeat(d_skip[layer], HEADDIM).reshape(1, INNER)
        proj, raw, normed = project(h, gain_row, weights_in[layer])
        cube = proj.reshape(SLOTS, length, WIDE)
        raw = raw.reshape(SLOTS, length, LANES)
        edge = passed_along(cube[:, length - (CONV - 1) :, INNER : INNER + CONVCH], 1)
        edge = jnp.pad(edge.astype(f32), ((0, 0), (8 - (CONV - 1), 0), (0, 0)))
        y, local, cum, size, act, decay = mix(cube, edge, taps, raw, heads, skip_row)
        state = chained(local[:count], decay[:count], 1, layer)
        flat = lambda array: array.reshape(rows, -1)
        h_next, mixture, inverse = branch(
            flat(y), proj, flat(act), flat(cum), state, gate_row, weights_out[layer], h, valid
        )
        kept.append(
            (h, gain_row, gate_row, taps, heads, skip_row, proj, raw, normed, edge, cum, size, act,
             decay, state, mixture, inverse)
        )
        h = h_next
    result = ordered(h.reshape(SLOTS, length, D))

    g = ordered(out_grad).reshape(rows, D)
    small = [None] * LAYERS
    partials = [None] * LAYERS
    for layer in reversed(range(LAYERS)):
        (h, gain_row, gate_row, taps, heads, skip_row, proj, raw, normed, edge, cum, size, act,
         decay, state, mixture, inverse) = kept[layer]
        cube = proj.reshape(SLOTS, length, WIDE)
        flat = lambda array: array.reshape(rows, -1)
        back, mean, grad_gate, partial_out = unbranch(
            g, valid, mixture, proj, inverse, gate_row, weights_out[layer]
        )
        dy, grads, local = ungate(
            back, mixture, proj, inverse, mean, gate_row, flat(act), flat(cum), count
        )
        later = chained(local, decay[:count], -1, LAYERS + layer)
        shaped = lambda array: array.reshape(SLOTS, length, -1)
        grads, edge_grad, grad_taps, grad_heads = unmix(
            cube, edge, taps, raw, heads, skip_row, shaped(dy), all_slots(state), all_slots(later),
            cum, size, act, shaped(grads),
        )
        late = passed_along(edge_grad[:, 8 - (CONV - 1) :].astype(bf16), -1).astype(f32)
        late = jnp.pad(late, ((0, 0), (8 - (CONV - 1), 0), (INNER, WIDE - INNER - CONVCH)))
        g, grad_norm, partial_in = unproject(
            flat(grads), late, weights_in[layer], normed, h, g, gain_row
        )
        small[layer] = (
            grad_norm[0], jnp.sum(grad_taps, axis=0)[:CONV], grad_gate[0],
            jnp.sum(grad_heads, axis=0)[:3, :HEADS],
        )
        partials[layer] = (partial_in, partial_out)
    grad_hidden = ordered(g.reshape(SLOTS, length, D))
    stacked = [jnp.stack([small[layer][member] for layer in range(LAYERS)]) for member in range(4)]
    shares = share_small(*stacked[:3])
    head_sums = jnp.pad(stacked[3].reshape(-1, HEADS), ((0, 8 - 3 * LAYERS), (0, LANES - HEADS)))
    grads_in, grads_out = [None] * LAYERS, [None] * LAYERS
    if small_mesh:
        cut = lambda partial: partial.reshape(lax.axis_size("dp") * lax.axis_size("seq"), -1, partial.shape[-1])
        for layer in reversed(range(LAYERS)):
            sent, split = [cut(partial) for partial in partials[layer]], [(3, 2), (3, 2)]
            if layer == 0:
                sent, split = sent + [shares], split + [(1, 1)]
            grads_in[layer], grads_out[layer], *others = reduce(sent, head_sums, split, 2 * LAYERS + 1 + layer)
        mine, head_sums = others
    else:
        for layer in range(LAYERS):
            grads_in[layer], grads_out[layer] = [
                lax.psum_scatter(partial, ("dp", "seq"), scatter_dimension=0, tiled=True)
                for partial in partials[layer]
            ]
        mine = lax.psum_scatter(shares, ("dp", "seq"), scatter_dimension=0, tiled=True)
        head_sums = lax.psum(head_sums, ("dp", "seq"))
    grad_norm, grad_conv, grad_gate = own_small(mine, norm_gain, conv_weight, gate_gain)
    grad_heads = head_sums[: 3 * LAYERS, :HEADS].reshape(LAYERS, 3, HEADS)
    return (
        result,
        grad_hidden,
        grad_norm,
        jnp.stack(grads_in)[..., :PROJ].astype(f32),
        grad_conv,
        grad_gate,
        jnp.stack(grads_out).astype(f32),
        grad_heads[:, 0],
        grad_heads[:, 1],
        grad_heads[:, 2],
    )


def solution(mesh):
    tokens = P("dp", "seq", None)
    every = ("dp", "seq")
    weights = (P(None, every), P(None, every, None), P(None, None, every), P(None, every), P(None, every, None))
    return jax.shard_map(
        body,
        mesh=mesh,
        in_specs=(tokens, tokens, P("dp")) + weights + (P(), P(), P()),
        out_specs=(tokens, tokens) + weights + (P(), P(), P()),
        check_vma=False,
    )
```

time: 3280 us -> 1380 us (0.42)
  waiting for transfers between devices: 1580 us -> 0.72 us
  Pallas kernels: 0 us -> 1290 us
  matrix products: 547 us -> 0 us
  local copies, waits for them, and re-layouts: 422 us -> 48.7 us
  other arithmetic: 359 us -> 17.9 us
  blocking collectives: 254 us -> 0 us
  starting transfers between devices: 85.9 us -> 12.3 us
    pallas_call x0 -> x21, Pallas kernels: none -> 1290 us  [the longest x1 343 us: gather(): pl.pallas_call(functools.partial(gather_kernel, shapes, split), name='gat...]
    unnamed x12 -> x0, waiting for transfers between devices: 739 us -> none
    dot_general x68 -> x0, matrix products: 547 us -> none  [the longest x12 182 us: mix_out(): jnp.einsum('strh,srhp->sthp', weights, values, precision=exact_product)]
    ppermute x32 -> x4, waiting for transfers between devices: 541 us -> 0.72 us  [passed_along(): lax.ppermute(value, 'seq', [(source, source + steps) for source in range(...]
    reduce_scatter x2 -> x0, waiting for transfers between devices: 300 us -> none  [body(): lax.psum_scatter(packed[4], ('dp', 'seq'), scatter_dimension=0, tiled=True)]
    all_gather x2 -> x0, blocking collectives: 212 us -> none  [body(): lax.all_gather(conv_weight[layer_index], ('dp', 'seq'), axis=1, tiled=True)]
    slice x31 -> x29, local copies, waits for them, and re-layouts: 179 us -> 21.2 us  [the longest x4 7.69 us: body(): state = chained(local[:count], decay[:count], 1, layer)]
    reshape x11 -> x13, local copies, waits for them, and re-layouts: 131 us -> 5.13 us  [the longest x2 1.77 us: unpack_small(): conv = everything[..., first:second].reshape(LAYERS, count, CONV, -1)]
  transfers between devices with their start and end apart: 41 -> 4, of which waited for: 28 -> 2; matrix products, arithmetic and copies ran while one was open for 20% -> 1% of each run, Pallas kernels for 0% -> 11%
where the time goes in v1:
time: 1380 us; the launch traced here: 1370 us
  Pallas kernels  1290 us (93%)
  local copies, waits for them, and re-layouts  48.7 us (4%)
  other arithmetic  17.9 us (1%)
    pallas_call x1, Pallas kernels, gather(): pl.pallas_call(functools.partial(gather_kernel, shapes, split), name='gat...  343 us
    pallas_call x2, Pallas kernels, reduce(): pl.pallas_call(functools.partial(reduce_kernel, shapes, split), name='red...  306 us
    pallas_call x2, Pallas kernels, unmix(): pl.pallas_call(unmix_kernel, name='unmix', grid=(SLOTS, NB + 2), in_specs...  190 us
    pallas_call x4, Pallas kernels, chained(): pl.pallas_call(functools.partial(chain_kernel, steps, lax.axis_size('seq'...  105 us
    pallas_call x2, Pallas kernels, unproject(): pl.pallas_call(unproject_kernel, name='unproject', grid=(WIDE // COLS,),...  72.7 us
    pallas_call x2, Pallas kernels, mix(): pl.pallas_call(mix_kernel, name='mix', grid=(SLOTS, NB), in_specs=[pl.Blo...  71.1 us
    pallas_call x2, Pallas kernels, unbranch(): pl.pallas_call(unbranch_kernel, name='unbranch', grid=(NB,), in_specs=[pl...  69.2 us
    pallas_call x2, Pallas kernels, project(): pl.pallas_call(project_kernel, name='project', grid=(WIDE // COLS,), in_s...  48.1 us
  transfers between devices with their start and end apart: 4, of which 2 were waited for; matrix products, arithmetic and copies ran while one was open for 1% of the time, Pallas kernels for 11%

profile of v1, /device:TPU:0, one launch (start us, length us, event | category | flops | bytes accessed | tf_op | source)
XLA Modules:
  0.0 1369.2 jit_solution(11053697486647832521)
XLA Ops:
  0.7 2.5 fusion.1
  3.2 1.9 slice_bitcast_fusion
  6.0 343.2 %gather.1 = (bf16[2,2,2,4,16,128]{5,4,3,2,1,0:T(8,128)(2,1)}, bf16[2,2,2,4,48,6656]{5,4,3,2,1,0:T(8,128)(2,1)}, bf16[2,2,2,4,96,1536]{5,4,3,2,1,0:T(8,128)(2,1)}...) custom-call(bf16[16,128]{1,0:T(8,128)(2,1)} %pad_bitcast_fusion.1.refs_0_, ...), custom_call_target="tpu_custom_call" | custom-call | tf_op jit(solution)/shard_map/gather/pallas_call | solution.py:861
  349.2 0.9 copy.42
  353.0 2.0 reverse_select_fusion.3
  355.0 24.1 %project.2 = (f32[512,6656]{1,0:T(8,128)}, f32[512,128]{1,0:T(8,128)}, bf16[512,1536]{1,0:T(8,128)(2,1)}) custom-call(f32[512,1536]{1,0:T(8,128)} %bitcast.95, f32[1,1536]{1,0:T(1,128)} %slice.167.gain_ref, bf16[1536,6656]{1,0:T(8,128)(2,1)} %bitcast.139), custom_call_target="tpu_custom_call" | custom-call | flops 10468982784 | bytes 20447232 | tf_op jit(solution)/shard_map/project/pallas_call | solution.py:141
  379.1 1.6 slice.210
  380.7 1.9 collective-permute-start
  382.9 0.8 reshape.173
  383.8 0.9 copy.43
  386.2 0.7 reshape_reshape.38.skip_ref
  386.9 2.0 reverse_select_fusion.1
  389.1 0.7 slice.177.gain_ref
  391.2 1.6 pad.61.edge_ref.maps_edge_ref
  392.8 35.5 %mix.2 = (f32[2,256,3072]{2,1,0:T(8,128)}, f32[2,128,3072]{2,1,0:T(8,128)}, f32[2,256,128]{2,1,0:T(8,128)}, f32[2,256,128]{2,1,0:T(8,128)}, f32[2,256,256]{2,1,0:T(8,128)}, /*index=5*/f32[2,8,3072]{2,1,0:T(8,128)}) custom-call(f32[2,256,6656]{2,1,0:T(8,128)} %bitcast.84, f32[2,8,3328]{2,1,0:T(8,128)} %pad.61.edge_ref.maps_edge_ref, ...), custom_call_target="tpu_custom_call" | custom-call | flops 6000000000 | bytes 10000000 | tf_op jit(solution)/shard_map/mix/pallas_call | solution.py:218
  428.4 1.5 slice.175.decay_ref
  429.9 2.8 slice.174.local_ref
  432.7 20.1 %chain.4.state_ref = bf16[1,6,128,512]{3,2,1,0:T(8,128)(2,1)} custom-call(f32[1,128,3072]{2,1,0:T(8,128)} %slice.174.local_ref, f32[1,8,3072]{2,1,0:T(8,128)} %slice.175.decay_ref), custom_call_target="tpu_custom_call" | custom-call | tf_op jit(solution)/shard_map/chain/pallas_call | solution.py:1088
  452.8 0.8 broadcast_in_dim.14.valid_ref
  453.6 23.4 %branch.2 = (f32[512,1536]{1,0:T(8,128)}, f32[512,3072]{1,0:T(8,128)}, f32[512,128]{1,0:T(8,128)}) custom-call(f32[512,3072]{1,0:T(8,128)} %bitcast.104, f32[512,6656]{1,0:T(8,128)} %get-tuple-element.75.gate_ref, f32[512,256]{1,0:T(8,128)} %bitcast.110, f32[512,128]{1,0:T(8,128)} %bitcast.116, bf16[1,6,128,512]{3,2,1,0:T(8,128)(2,1)} %chain.4.state_ref, ...), custom_call_target="tpu_custom_call" | custom-call | flops 4831838208 | bytes 9437184 | tf_op jit(solution)/shard_map/branch/pallas_call | solution.py:305
  477.0 24.0 %project.3 = (f32[512,6656]{1,0:T(8,128)}, f32[512,128]{1,0:T(8,128)}, bf16[512,1536]{1,0:T(8,128)(2,1)}) custom-call(f32[512,1536]{1,0:T(8,128)} %get-tuple-element.83.h_ref, f32[1,1536]{1,0:T(1,128)} %slice.179.gain_ref, bf16[1536,6656]{1,0:T(8,128)(2,1)} %bitcast.141), custom_call_target="tpu_custom_call" | custom-call | flops 10468982784 | bytes 20447232 | tf_op jit(solution)/shard_map/project/pallas_call | solution.py:141
  501.0 1.0 slice.215
  502.0 7.4 collective-permute-start.1
  511.6 0.7 pad.65.edge_ref.maps_edge_ref
  512.3 35.6 %mix.3 = (f32[2,256,3072]{2,1,0:T(8,128)}, f32[2,128,3072]{2,1,0:T(8,128)}, f32[2,256,128]{2,1,0:T(8,128)}, f32[2,256,128]{2,1,0:T(8,128)}, f32[2,256,256]{2,1,0:T(8,128)}, /*index=5*/f32[2,8,3072]{2,1,0:T(8,128)}) custom-call(f32[2,256,6656]{2,1,0:T(8,128)} %bitcast.89, f32[2,8,3328]{2,1,0:T(8,128)} %pad.65.edge_ref.maps_edge_ref, ...), custom_call_target="tpu_custom_call" | custom-call | flops 6000000000 | bytes 10000000 | tf_op jit(solution)/shard_map/mix/pallas_call | solution.py:218
  547.9 2.8 slice.185.local_ref
  551.3 22.9 %chain.5.state_ref = bf16[1,6,128,512]{3,2,1,0:T(8,128)(2,1)} custom-call(f32[1,128,3072]{2,1,0:T(8,128)} %slice.185.local_ref, f32[1,8,3072]{2,1,0:T(8,128)} %slice.186.decay_ref), custom_call_target="tpu_custom_call" | custom-call | tf_op jit(solution)/shard_map/chain/pallas_call | solution.py:1088
  574.2 23.5 %branch.3 = (f32[512,1536]{1,0:T(8,128)}, f32[512,3072]{1,0:T(8,128)}, f32[512,128]{1,0:T(8,128)}) custom-call(f32[512,3072]{1,0:T(8,128)} %bitcast.105, f32[512,6656]{1,0:T(8,128)} %get-tuple-element.85.gate_ref, f32[512,256]{1,0:T(8,128)} %bitcast.112, f32[512,128]{1,0:T(8,128)} %bitcast.118, bf16[1,6,128,512]{3,2,1,0:T(8,128)(2,1)} %chain.5.state_ref, ...), custom_call_target="tpu_custom_call" | custom-call | flops 4831838208 | bytes 9437184 | tf_op jit(solution)/shard_map/branch/pallas_call | solution.py:305
  597.7 34.6 %unbranch.2 = (f32[512,3072]{1,0:T(8,128)}, f32[512,128]{1,0:T(8,128)}, f32[8,3072]{1,0:T(8,128)}, bf16[3072,1536]{1,0:T(8,128)(2,1)}) custom-call(f32[512,1536]{1,0:T(8,128)} %bitcast.106, f32[512,128]{1,0:T(8,128)} %broadcast_in_dim.14.valid_ref, f32[512,3072]{1,0:T(8,128)} %get-tuple-element.94.mixture_ref, f32[512,6656]{1,0:T(8,128)} %get-tuple-element.85.gate_ref, ...), custom_call_target="tpu_custom_call" | custom-call | flops 9663676416 | bytes 18874368 | tf_op jit(solution)/shard_map/unbranch/pallas_call | solution.py:383
  632.3 17.5 %ungate.2 = (f32[512,3072]{1,0:T(8,128)}, bf16[512,6656]{1,0:T(8,128)(2,1)}, f32[1,128,3072]{2,1,0:T(8,128)}) custom-call(f32[512,3072]{1,0:T(8,128)} %get-tuple-element.96.back_ref, f32[512,3072]{1,0:T(8,128)} %get-tuple-element.94.mixture_ref, f32[512,6656]{1,0:T(8,128)} %get-tuple-element.85.gate_ref, f32[512,128]{1,0:T(8,128)} %get-tuple-element.95.inverse_ref, ...), custom_call_target="tpu_custom_call" | custom-call | flops 1000000000 | bytes 20000000 | tf_op jit(solution)/shard_map/ungate/pallas_call | solution.py:452
  649.8 36.4 %chain.6 = bf16[1,6,128,512]{3,2,1,0:T(8,128)(2,1)} custom-call(f32[1,128,3072]{2,1,0:T(8,128)} %get-tuple-element.99.local_ref, f32[1,8,3072]{2,1,0:T(8,128)} %slice.186.decay_ref), custom_call_target="tpu_custom_call" | custom-call | tf_op jit(solution)/shard_map/chain/pallas_call | solution.py:1088
  686.2 1.3 concatenate.20.state_ref
  687.5 2.4 concatenate.21.later_ref
  689.9 94.9 %unmix.2 = (bf16[2,256,6656]{2,1,0:T(8,128)(2,1)}, f32[2,8,3328]{2,1,0:T(8,128)}, f32[2,8,3328]{2,1,0:T(8,128)}, f32[2,8,128]{2,1,0:T(8,128)}) custom-call(f32[2,256,6656]{2,1,0:T(8,128)} %bitcast.91, f32[2,8,3328]{2,1,0:T(8,128)} %pad.65.edge_ref.maps_edge_ref, f32[8,3328]{1,0:T(8,128)} %pad.66.taps_ref.maps_taps_ref, ...), custom_call_target="tpu_custom_call", output_to_operand_aliasing={{0}: (15, {})} | custom-call | flops 20000000000 | bytes 20000000 | tf_op jit(solution)/shard_map/unmix/pallas_call | solution.py:633
  784.8 1.0 slice.249
  785.8 1.5 collective-permute-start.2
  787.3 1.3 concatenate.22.state_ref
  788.6 0.7 reduce_sum.39
  789.3 1.0 reduce_sum.37
  790.4 0.9 slice.196
  791.8 0.8 pad_convert_fusion.1.late_ref
  792.6 36.3 %unproject.2 = (f32[512,1536]{1,0:T(8,128)}, f32[8,1536]{1,0:T(8,128)}, bf16[1536,6656]{1,0:T(8,128)(2,1)}) custom-call(bf16[512,6656]{1,0:T(8,128)(2,1)} %bitcast.144, f32[2,8,6656]{2,1,0:T(8,128)} %pad_convert_fusion.1.late_ref, bf16[1536,6656]{1,0:T(8,128)(2,1)} %bitcast.142, bf16[512,1536]{1,0:T(8,128)(2,1)} %get-tuple-element.104.normed_ref, ...), custom_call_target="tpu_custom_call" | custom-call | flops 20937965568 | bytes 40894464 | tf_op jit(solution)/shard_map/unproject/pallas_call | solution.py:726
  828.9 34.6 %unbranch.3 = (f32[512,3072]{1,0:T(8,128)}, f32[512,128]{1,0:T(8,128)}, f32[8,3072]{1,0:T(8,128)}, bf16[3072,1536]{1,0:T(8,128)(2,1)}) custom-call(f32[512,1536]{1,0:T(8,128)} %get-tuple-element.105.g_ref, f32[512,128]{1,0:T(8,128)} %broadcast_in_dim.14.valid_ref, f32[512,3072]{1,0:T(8,128)} %get-tuple-element.106.mixture_ref, ...), custom_call_target="tpu_custom_call" | custom-call | flops 9663676416 | bytes 18874368 | tf_op jit(solution)/shard_map/unbranch/pallas_call | solution.py:383
  863.5 17.3 %ungate.3 = (f32[512,3072]{1,0:T(8,128)}, bf16[512,6656]{1,0:T(8,128)(2,1)}, f32[1,128,3072]{2,1,0:T(8,128)}) custom-call(f32[512,3072]{1,0:T(8,128)} %get-tuple-element.108.back_ref, f32[512,3072]{1,0:T(8,128)} %get-tuple-element.106.mixture_ref, f32[512,6656]{1,0:T(8,128)} %get-tuple-element.75.gate_ref, f32[512,128]{1,0:T(8,128)} %get-tuple-element.107.inverse_ref, ...), custom_call_target="tpu_custom_call" | custom-call | flops 1000000000 | bytes 20000000 | tf_op jit(solution)/shard_map/ungate/pallas_call | solution.py:452
  880.9 25.4 %chain.7 = bf16[1,6,128,512]{3,2,1,0:T(8,128)(2,1)} custom-call(f32[1,128,3072]{2,1,0:T(8,128)} %get-tuple-element.111.local_ref, f32[1,8,3072]{2,1,0:T(8,128)} %slice.175.decay_ref), custom_call_target="tpu_custom_call" | custom-call | tf_op jit(solution)/shard_map/chain/pallas_call | solution.py:1088
  906.3 2.4 concatenate.23.later_ref
  908.7 94.9 %unmix.3 = (bf16[2,256,6656]{2,1,0:T(8,128)(2,1)}, f32[2,8,3328]{2,1,0:T(8,128)}, f32[2,8,3328]{2,1,0:T(8,128)}, f32[2,8,128]{2,1,0:T(8,128)}) custom-call(f32[2,256,6656]{2,1,0:T(8,128)} %bitcast.86, f32[2,8,3328]{2,1,0:T(8,128)} %pad.61.edge_ref.maps_edge_ref, f32[8,3328]{1,0:T(8,128)} %pad.62.taps_ref.maps_taps_ref, ...), custom_call_target="tpu_custom_call", output_to_operand_aliasing={{0}: (15, {})} | custom-call | flops 20000000000 | bytes 20000000 | tf_op jit(solution)/shard_map/unmix/pallas_call | solution.py:633
  1003.6 0.7 reduce_sum.38
  1004.3 1.0 slice.248
  1005.2 1.5 collective-permute-start.3
  1006.8 1.0 reduce_sum.36
  1007.9 0.9 slice.195
  1009.5 0.8 slice.192
  1010.6 154.3 %reduce.19 = (f32[48,6656]{1,0:T(8,128)}, f32[96,1536]{1,0:T(8,128)}, f32[8,128]{1,0:T(8,128)}) custom-call(bf16[2,2,2,4,48,6656]{5,4,3,2,1,0:T(8,128)(2,1)} %bitcast.93, bf16[2,2,2,4,96,1536]{5,4,3,2,1,0:T(8,128)(2,1)} %bitcast.102, f32[8,128]{1,0:T(8,128)} %pad.74.refs_3_.refs_2_), custom_call_target="tpu_custom_call" | custom-call | tf_op jit(solution)/shard_map/reduce/pallas_call | solution.py:1014
  1164.9 0.8 pad_convert_fusion.late_ref
  1165.7 36.4 %unproject.3 = (f32[512,1536]{1,0:T(8,128)}, f32[8,1536]{1,0:T(8,128)}, bf16[1536,6656]{1,0:T(8,128)(2,1)}) custom-call(bf16[512,6656]{1,0:T(8,128)(2,1)} %bitcast.146, f32[2,8,6656]{2,1,0:T(8,128)} %pad_convert_fusion.late_ref, bf16[1536,6656]{1,0:T(8,128)(2,1)} %bitcast.140, bf16[512,1536]{1,0:T(8,128)(2,1)} %get-tuple-element.116.normed_ref, ...), custom_call_target="tpu_custom_call" | custom-call | flops 20937965568 | bytes 40894464 | tf_op jit(solution)/shard_map/unproject/pallas_call | solution.py:726
  1202.1 0.8 slice.191
  1203.4 0.8 copy.39
  1204.2 151.8 %reduce.18 = (f32[48,6656]{1,0:T(8,128)}, f32[96,1536]{1,0:T(8,128)}, f32[16,128]{1,0:T(8,128)}, f32[8,128]{1,0:T(8,128)}) custom-call(bf16[2,2,2,4,48,6656]{5,4,3,2,1,0:T(8,128)(2,1)} %bitcast.94, bf16[2,2,2,4,96,1536]{5,4,3,2,1,0:T(8,128)(2,1)} %bitcast.103, f32[2,2,2,4,16,128]{5,4,3,2,1,0:T(8,128)} %bitcast.120, f32[8,128]{1,0:T(8,128)} %pad.74.refs_3_.refs_2_), custom_call_target="tpu_custom_call" | custom-call | tf_op jit(solution)/shard_map/reduce/pallas_call | solution.py:1014
  1356.0 0.8 reshape.198
  1358.8 0.7 reshape.200
  1360.0 2.3 pad_maximum_fusion.1
  1362.3 3.1 pad_maximum_fusion
  1365.4 3.4 reverse_select_fusion
  (94 shorter events, 13.5 us)
Async XLA Ops:
  0.6 4.5 copy-start.10
  0.7 4.6 copy-start.15
  0.7 4.6 copy-start.14
  0.7 350.5 %copy-start.9 = (s32[2]{0:T(128)S(1)}, s32[2]{0:T(128)}, u32[]{:S(2)}) copy-start(s32[2]{0:T(128)} %param.13) | copy-start | bytes 28
  0.7 352.3 %copy-start.2 = (f32[2,256,1536]{2,1,0:T(8,128)S(1)}, f32[2,256,1536]{2,1,0:T(8,128)}, u32[]{:S(2)}) copy-start(f32[2,256,1536]{2,1,0:T(8,128)} %param.11) | copy-start | bytes 9437188
  355.0 29.8 %copy-start.11 = (f32[2,48]{1,0:T(2,128)S(1)}, f32[2,48]{1,0:T(2,128)}, u32[]{:S(2)}) copy-start(f32[2,48]{1,0:T(2,128)} %param.19) | copy-start | bytes 1156
  355.0 29.9 %copy-start.12 = (f32[2,48]{1,0:T(2,128)S(1)}, f32[2,48]{1,0:T(2,128)}, u32[]{:S(2)}) copy-start(f32[2,48]{1,0:T(2,128)} %param.20) | copy-start | bytes 1156
  355.0 31.1 %copy-start.13 = (f32[2,48]{1,0:T(2,128)S(1)}, f32[2,48]{1,0:T(2,128)}, u32[]{:S(2)}) copy-start(f32[2,48]{1,0:T(2,128)} %param.21) | copy-start | bytes 1156
  355.0 31.9 %copy-start.3 = (f32[2,256,1536]{2,1,0:T(8,128)S(1)}, f32[2,256,1536]{2,1,0:T(8,128)}, u32[]{:S(2)}) copy-start(f32[2,256,1536]{2,1,0:T(8,128)} %param.12) | copy-start | bytes 9437188
  380.7 10.5 collective-permute-start
  502.0 9.6 collective-permute-start.1
  547.9 2.8 copy-start.8
  632.3 53.9 %copy-start.1 = (bf16[1,6,128,512]{3,2,1,0:T(8,128)(2,1)S(1)}, bf16[1,6,128,512]{3,2,1,0:T(8,128)(2,1)}, u32[]{:S(2)}) copy-start(bf16[1,6,128,512]{3,2,1,0:T(8,128)(2,1)} %chain.5.state_ref) | copy-start | bytes 2359300
  689.9 97.4 %copy-start = (bf16[1,6,128,512]{3,2,1,0:T(8,128)(2,1)S(1)}, bf16[1,6,128,512]{3,2,1,0:T(8,128)(2,1)}, u32[]{:S(2)}) copy-start(bf16[1,6,128,512]{3,2,1,0:T(8,128)(2,1)} %chain.4.state_ref) | copy-start | bytes 2359300
  785.8 6.0 collective-permute-start.2
  1005.2 159.7 %collective-permute-start.3 = (bf16[2,3,3328]{2,1,0:T(4,128)(2,1)S(1)}, bf16[2,3,3328]{2,1,0:T(4,128)(2,1)S(1)}, u32[]{:S(2)}, u32[]{:S(2)}) collective-permute-start(bf16[2,3,3328]{2,1,0:T(4,128)(2,1)S(1)} %slice.248), channel_id=1, source_target_pairs={{1,0},{2,1},{3,2},{5,4},{6,5},{7,6},{9,8},{10,9},{11,10},{13,12},{... | collective-permute-start | bytes 119816 | tf_op jit(solution)/shard_map/ppermute | solution.py:1106
  1204.2 155.8 %copy-start.7 = (f32[96,1536]{1,0:T(8,128)S(1)}, f32[96,1536]{1,0:T(8,128)}, u32[]{:S(2)}) copy-start(f32[96,1536]{1,0:T(8,128)} %get-tuple-element.134) | copy-start | bytes 1769476
  1204.2 158.1 %copy-start.6 = (f32[48,6656]{1,0:T(8,128)S(1)}, f32[48,6656]{1,0:T(8,128)}, u32[]{:S(2)}) copy-start(f32[48,6656]{1,0:T(8,128)} %get-tuple-element.132) | copy-start | bytes 3833860
  1360.0 5.4 copy-start.4
  1360.0 5.4 copy-start.5

commit v2 on v1

--- a/solution.py
+++ b/solution.py
@@ -20,7 +20,7 @@
 SHORT = 256
 
 LANES = 128
-WIDE = 6656
+TAIL = 3584
 BLK = 256
 NB = INNER // BLK
 COLS = 512
@@ -34,6 +34,56 @@
 VMEM_LIMIT = 58 << 20
 
 
+def launch(
+    kernel, name, grid, in_specs, out_specs, out_shape, args, scratch=(), cost=None, carry=None, identity=None,
+    along=False, remote=False,
+):
+    options = {"compiler_params": params()}
+    if cost is not None:
+        options["cost_estimate"] = pl.CostEstimate(flops=cost[0], bytes_accessed=cost[1], transcendentals=cost[2])
+    if carry is not None or remote:
+        options["compiler_params"] = params(collective_id=identity, has_side_effects=True)
+    if carry is None:
+        return pl.pallas_call(
+            kernel, name=name, grid=grid, in_specs=in_specs, out_specs=out_specs, out_shape=out_shape,
+            scratch_shapes=list(scratch), **options,
+        )(*args)
+    sizes = [len(in_specs), len(carry.in_specs), len(out_specs), len(carry.out_specs), len(scratch)]
+    if carry.aliases:
+        options["input_output_aliases"] = {sizes[0] + i: sizes[2] + o for i, o in carry.aliases.items()}
+
+    def wrapped(*refs):
+        groups, at = [], 0
+        for size in sizes:
+            groups.append(refs[at : at + size])
+            at += size
+        step, total = 0, 1
+        for axis, extent in enumerate(grid):
+            step, total = step * extent + pl.program_id(axis), total * extent
+        ticks = carry.ticks(groups[1], groups[3], refs[at:], along)
+        plan = {}
+        for number, tick in enumerate(ticks[:-1]):
+            plan.setdefault(number * total // (len(ticks) - 1), []).append(tick)
+        for moment, members in plan.items():
+            @pl.when(step == moment)
+            def _(members=members):
+                for member in members:
+                    member()
+
+        kernel(*groups[0], *groups[2], *groups[4])
+
+        @pl.when(step == total - 1)
+        def _():
+            ticks[-1]()
+
+    found = pl.pallas_call(
+        wrapped, name=name, grid=grid, in_specs=list(in_specs) + carry.in_specs,
+        out_specs=list(out_specs) + carry.out_specs, out_shape=list(out_shape) + carry.out_shape,
+        scratch_shapes=list(scratch) + carry.scratch, **options,
+    )(*args, *carry.args)
+    return list(found[: sizes[2]]) + [carry.results(found[sizes[2] :])]
+
+
 def params(**more):
     return pltpu.CompilerParams(vmem_limit_bytes=VMEM_LIMIT, **more)
 
@@ -136,32 +186,52 @@
         raw_ref[...] = product[:, COLS - 2 * LANES : COLS - LANES]
 
 
-def project(h, gain_row, weight):
+def project(h, gain_row, weight, carry=None, identity=None):
     total = h.shape[0]
-    return pl.pallas_call(
+    return launch(
         project_kernel,
-        name="project",
-        grid=(WIDE // COLS,),
-        in_specs=[
+        "project",
+        (TAIL // COLS,),
+        [
             pl.BlockSpec((total, D), lambda n: (0, 0)),
             pl.BlockSpec((1, D), lambda n: (0, 0)),
             pl.BlockSpec((D, COLS), lambda n: (0, n)),
         ],
-        out_specs=[
+        [
             pl.BlockSpec((total, COLS), lambda n: (0, n)),
             pl.BlockSpec((total, LANES), lambda n: (0, 0)),
             pl.BlockSpec((total, D), lambda n: (0, 0)),
         ],
-        out_shape=[
-            jax.ShapeDtypeStruct((total, WIDE), f32),
+        [
+            jax.ShapeDtypeStruct((total, TAIL), f32),
             jax.ShapeDtypeStruct((total, LANES), f32),
             jax.ShapeDtypeStruct((total, D), bf16),
         ],
-        compiler_params=params(),
-        cost_estimate=pl.CostEstimate(
-            flops=2 * total * D * WIDE, bytes_accessed=2 * D * WIDE, transcendentals=0
-        ),
-    )(h, gain_row, weight)
+        (h, gain_row, weight),
+        cost=(2 * total * D * TAIL, 2 * D * TAIL, 0),
+        carry=carry,
+        identity=identity,
+    )
+
+
+def project_gate_kernel(normed_ref, w_ref, gate_ref):
+    gate_ref[...] = dot(normed_ref[...], w_ref[...])
+
+
+def project_gate(normed, weight, carry=None, identity=None):
+    total = normed.shape[0]
+    return launch(
+        project_gate_kernel,
+        "project_gate",
+        (INNER // COLS,),
+        [pl.BlockSpec((total, D), lambda n: (0, 0)), pl.BlockSpec((D, COLS), lambda n: (0, n))],
+        [pl.BlockSpec((total, COLS), lambda n: (0, n))],
+        [jax.ShapeDtypeStruct((total, INNER), f32)],
+        (normed, weight),
+        cost=(2 * total * D * INNER, 2 * D * INNER, 0),
+        carry=carry,
+        identity=identity,
+    )
 
 
 def mix_kernel(
@@ -213,24 +283,24 @@
     decay_ref[0] = jnp.broadcast_to(spread(jnp.exp(final)), (8, BLK))
 
 
-def mix(proj, edge, taps, raw, heads, skip_row):
+def mix(proj, edge, taps, raw, heads, skip_row, carry=None, identity=None):
     length = proj.shape[1]
-    return pl.pallas_call(
+    return launch(
         mix_kernel,
-        name="mix",
-        grid=(SLOTS, NB),
-        in_specs=[
-            pl.BlockSpec((1, length, BLK), lambda s, b: (s, 0, NB + b)),
+        "mix",
+        (SLOTS, NB),
+        [
+            pl.BlockSpec((1, length, BLK), lambda s, b: (s, 0, b)),
             pl.BlockSpec((1, 8, BLK), lambda s, b: (s, 0, b)),
             pl.BlockSpec((8, BLK), lambda s, b: (0, b)),
-            pl.BlockSpec((1, length, BLK), lambda s, b: (s, 0, 2 * NB)),
+            pl.BlockSpec((1, length, BLK), lambda s, b: (s, 0, NB)),
             pl.BlockSpec((1, 8, BLK), lambda s, b: (s, 0, NB)),
             pl.BlockSpec((8, BLK), lambda s, b: (0, NB)),
             pl.BlockSpec((1, length, LANES), lambda s, b: (s, 0, 0)),
             pl.BlockSpec((8, LANES), lambda s, b: (0, 0)),
             pl.BlockSpec((1, BLK), lambda s, b: (0, b)),
         ],
-        out_specs=[
+        [
             pl.BlockSpec((1, length, BLK), lambda s, b: (s, 0, b)),
             pl.BlockSpec((1, NSTATE, BLK), lambda s, b: (s, 0, b)),
             pl.BlockSpec((1, length, LANES), lambda s, b: (s, 0, 0)),
@@ -238,7 +308,7 @@
             pl.BlockSpec((1, length, BLK), lambda s, b: (s, 0, 0)),
             pl.BlockSpec((1, 8, BLK), lambda s, b: (s, 0, b)),
         ],
-        out_shape=[
+        [
             jax.ShapeDtypeStruct((SLOTS, length, INNER), f32),
             jax.ShapeDtypeStruct((SLOTS, NSTATE, INNER), f32),
             jax.ShapeDtypeStruct((SLOTS, length, LANES), f32),
@@ -246,15 +316,17 @@
             jax.ShapeDtypeStruct((SLOTS, length, BLK), f32),
             jax.ShapeDtypeStruct((SLOTS, 8, INNER), f32),
         ],
-        scratch_shapes=[
+        (proj, edge, taps, proj, edge, taps, raw, heads, skip_row),
+        scratch=[
             pltpu.VMEM((length + 8, BLK), f32),
             pltpu.VMEM((length, length), f32),
             pltpu.VMEM((LANES, length), f32),
             pltpu.VMEM((2, NSTATE, length), bf16),
         ],
-        compiler_params=params(),
-        cost_estimate=pl.CostEstimate(flops=6 * 10**9, bytes_accessed=10**7, transcendentals=10**7),
-    )(proj, edge, taps, proj, edge, taps, raw, heads, skip_row)
+        cost=(6 * 10**9, 10**7, 10**7),
+        carry=carry,
+        identity=identity,
+    )
 
 
 def branch_kernel(
@@ -299,14 +371,14 @@
         for_rows(rows, 32, one)
 
 
-def branch(y, proj, act, cum, state, gain_row, weight, h, valid):
+def branch(y, gate, act, cum, state, gain_row, weight, h, valid, carry=None, identity=None):
     rows = h.shape[0]
     count = state.shape[0]
-    return pl.pallas_call(
+    return launch(
         branch_kernel,
-        name="branch",
-        grid=(NB,),
-        in_specs=[
+        "branch",
+        (NB,),
+        [
             pl.BlockSpec((rows, BLK), lambda b: (0, b)),
             pl.BlockSpec((rows, BLK), lambda b: (0, b)),
             pl.BlockSpec((rows, BLK), lambda b: (0, 0)),
@@ -317,26 +389,26 @@
             pl.BlockSpec((rows, D), lambda b: (0, 0)),
             pl.BlockSpec((rows, LANES), lambda b: (0, 0)),
         ],
-        out_specs=[
+        [
             pl.BlockSpec((rows, D), lambda b: (0, 0)),
             pl.BlockSpec((rows, BLK), lambda b: (0, b)),
             pl.BlockSpec((rows, LANES), lambda b: (0, 0)),
         ],
-        out_shape=[
+        [
             jax.ShapeDtypeStruct((rows, D), f32),
             jax.ShapeDtypeStruct((rows, INNER), f32),
             jax.ShapeDtypeStruct((rows, LANES), f32),
         ],
-        scratch_shapes=[
+        (y, gate, act, cum, state, gain_row, weight, h, valid),
+        scratch=[
             pltpu.VMEM((rows, D), f32),
             pltpu.VMEM((rows, LANES), f32),
             pltpu.VMEM((rows, BLK), bf16),
         ],
-        compiler_params=params(),
-        cost_estimate=pl.CostEstimate(
-            flops=2 * rows * D * INNER, bytes_accessed=2 * D * INNER, transcendentals=10**6
-        ),
-    )(y, proj, act, cum, state, gain_row, weight, h, valid)
+        cost=(2 * rows * D * INNER, 2 * D * INNER, 10**6),
+        carry=carry,
+        identity=identity,
+    )
 
 
 def unbranch_kernel(
@@ -378,13 +450,13 @@
         )
 
 
-def unbranch(g, valid, mixture, proj, inverse, gain_row, weight):
+def unbranch(g, valid, mixture, gate, inverse, gain_row, weight, carry=None, identity=None):
     rows = g.shape[0]
-    return pl.pallas_call(
+    return launch(
         unbranch_kernel,
-        name="unbranch",
-        grid=(NB,),
-        in_specs=[
+        "unbranch",
+        (NB,),
+        [
             pl.BlockSpec((rows, D), lambda b: (0, 0)),
             pl.BlockSpec((rows, LANES), lambda b: (0, 0)),
             pl.BlockSpec((rows, BLK), lambda b: (0, b)),
@@ -393,24 +465,24 @@
             pl.BlockSpec((1, BLK), lambda b: (0, b)),
             pl.BlockSpec((BLK, D), lambda b: (b, 0)),
         ],
-        out_specs=[
+        [
             pl.BlockSpec((rows, BLK), lambda b: (0, b)),
             pl.BlockSpec((rows, LANES), lambda b: (0, 0)),
             pl.BlockSpec((8, BLK), lambda b: (0, b)),
             pl.BlockSpec((BLK, D), lambda b: (b, 0)),
         ],
-        out_shape=[
+        [
             jax.ShapeDtypeStruct((rows, INNER), f32),
             jax.ShapeDtypeStruct((rows, LANES), f32),
             jax.ShapeDtypeStruct((8, INNER), f32),
             jax.ShapeDtypeStruct((INNER, D), bf16),
         ],
-        scratch_shapes=[pltpu.VMEM((rows, D), bf16), pltpu.VMEM((rows, BLK), bf16)],
-        compiler_params=params(),
-        cost_estimate=pl.CostEstimate(
-            flops=4 * rows * D * INNER, bytes_accessed=4 * D * INNER, transcendentals=10**6
-        ),
-    )(g, valid, mixture, proj, inverse, gain_row, weight)
+        (g, valid, mixture, gate, inverse, gain_row, weight),
+        scratch=[pltpu.VMEM((rows, D), bf16), pltpu.VMEM((rows, BLK), bf16)],
+        cost=(4 * rows * D * INNER, 4 * D * INNER, 10**6),
+        carry=carry,
+        identity=identity,
+    )
 
 
 def ungate_kernel(
@@ -446,14 +518,14 @@
             state_ref[slot] = dot_halves((output_t[slot, 0], output_t[slot, 1]), halves(dy * grown))
 
 
-def ungate(back, mixture, proj, inverse, mean, gain_row, act, cum, count):
+def ungate(back, mixture, gate, inverse, mean, gain_row, act, cum, count, carry=None, identity=None):
     rows = back.shape[0]
     length = rows // SLOTS
-    return pl.pallas_call(
+    return launch(
         ungate_kernel,
-        name="ungate",
-        grid=(NB,),
-        in_specs=[
+        "ungate",
+        (NB,),
+        [
             pl.BlockSpec((rows, BLK), lambda b: (0, b)),
             pl.BlockSpec((rows, BLK), lambda b: (0, b)),
             pl.BlockSpec((rows, BLK), lambda b: (0, b)),
@@ -463,29 +535,30 @@
             pl.BlockSpec((rows, BLK), lambda b: (0, 0)),
             pl.BlockSpec((rows, LANES), lambda b: (0, 0)),
         ],
-        out_specs=[
+        [
             pl.BlockSpec((rows, BLK), lambda b: (0, b)),
             pl.BlockSpec((rows, BLK), lambda b: (0, b)),
             pl.BlockSpec((count, NSTATE, BLK), lambda b: (0, 0, b)),
         ],
-        out_shape=[
+        [
             jax.ShapeDtypeStruct((rows, INNER), f32),
-            jax.ShapeDtypeStruct((rows, WIDE), bf16),
+            jax.ShapeDtypeStruct((rows, INNER), bf16),
             jax.ShapeDtypeStruct((count, NSTATE, INNER), f32),
         ],
-        scratch_shapes=[pltpu.VMEM((count, 2, NSTATE, length), bf16)],
-        compiler_params=params(),
-        cost_estimate=pl.CostEstimate(flops=10**9, bytes_accessed=2 * 10**7, transcendentals=10**7),
-    )(back, mixture, proj, inverse, mean, gain_row, act, cum)
+        (back, mixture, gate, inverse, mean, gain_row, act, cum),
+        scratch=[pltpu.VMEM((count, 2, NSTATE, length), bf16)],
+        cost=(10**9, 2 * 10**7, 10**7),
+        carry=carry,
+        identity=identity,
+    )
 
 
 def unmix_kernel(
     rows_ref, edge_ref, taps_ref, maps_ref, maps_edge_ref, maps_taps_ref, raw_ref, heads_ref, skip_ref,
-    dy_ref, state_ref, later_ref, cum_ref, step_ref, act_ref, grads_in_ref,
+    dy_ref, state_ref, later_ref, cum_ref, step_ref, act_ref,
     grads_ref, edge_out_ref, taps_out_ref, heads_out_ref,
     extended, inner, d_inner, cum_t, grad_ext, d_maps, d_cum, d_step, over_rows, sums,
 ):
-    del grads_in_ref
     block = pl.program_id(1)
     length = rows_ref.shape[1]
     count = state_ref.shape[0]
@@ -626,19 +699,19 @@
         )
 
 
-def unmix(proj, edge, taps, raw, heads, skip_row, dy, state, later, cum, size, act, grads):
+def unmix(proj, edge, taps, raw, heads, skip_row, dy, state, later, cum, size, act, carry=None, identity=None):
     length = proj.shape[1]
     inside = lambda b: jnp.minimum(b, NB - 1)
     upto = lambda b: jnp.minimum(b, NB)
-    return pl.pallas_call(
+    return launch(
         unmix_kernel,
-        name="unmix",
-        grid=(SLOTS, NB + 2),
-        in_specs=[
-            pl.BlockSpec((1, length, BLK), lambda s, b: (s, 0, NB + inside(b))),
+        "unmix",
+        (SLOTS, NB + 2),
+        [
+            pl.BlockSpec((1, length, BLK), lambda s, b: (s, 0, inside(b))),
             pl.BlockSpec((1, 8, BLK), lambda s, b: (s, 0, inside(b))),
             pl.BlockSpec((8, BLK), lambda s, b: (0, inside(b))),
-            pl.BlockSpec((1, length, BLK), lambda s, b: (s, 0, 2 * NB)),
+            pl.BlockSpec((1, length, BLK), lambda s, b: (s, 0, NB)),
             pl.BlockSpec((1, 8, BLK), lambda s, b: (s, 0, NB)),
             pl.BlockSpec((8, BLK), lambda s, b: (0, NB)),
             pl.BlockSpec((1, length, LANES), lambda s, b: (s, 0, 0)),
@@ -650,22 +723,21 @@
             pl.BlockSpec((1, length, LANES), lambda s, b: (s, 0, 0)),
             pl.BlockSpec((1, length, LANES), lambda s, b: (s, 0, 0)),
             pl.BlockSpec((1, length, BLK), lambda s, b: (s, 0, 0)),
-            pl.BlockSpec(memory_space=pl.ANY),
-        ],
-        out_specs=[
-            pl.BlockSpec((1, length, BLK), lambda s, b: (s, 0, NB + b)),
+        ],
+        [
+            pl.BlockSpec((1, length, BLK), lambda s, b: (s, 0, b)),
             pl.BlockSpec((1, 8, BLK), lambda s, b: (s, 0, upto(b))),
             pl.BlockSpec((1, 8, BLK), lambda s, b: (s, 0, upto(b))),
             pl.BlockSpec((1, 8, LANES), lambda s, b: (s, 0, 0)),
         ],
-        out_shape=[
-            jax.ShapeDtypeStruct((SLOTS, length, WIDE), bf16),
+        [
+            jax.ShapeDtypeStruct((SLOTS, length, TAIL), bf16),
             jax.ShapeDtypeStruct((SLOTS, 8, CONVCH), f32),
             jax.ShapeDtypeStruct((SLOTS, 8, CONVCH), f32),
             jax.ShapeDtypeStruct((SLOTS, 8, LANES), f32),
         ],
-        input_output_aliases={15: 0},
-        scratch_shapes=[
+        (proj, edge, taps, proj, edge, taps, raw, heads, skip_row, dy, state, later, cum, size, act),
+        scratch=[
             pltpu.VMEM((length + 8, BLK), f32),
             pltpu.VMEM((length, length), f32),
             pltpu.VMEM((length, length), f32),
@@ -677,13 +749,54 @@
             pltpu.VMEM((LANES, length), f32),
             pltpu.VMEM((8, LANES), f32),
         ],
-        compiler_params=params(),
-        cost_estimate=pl.CostEstimate(flops=2 * 10**10, bytes_accessed=2 * 10**7, transcendentals=10**7),
-    )(proj, edge, taps, proj, edge, taps, raw, heads, skip_row, dy, state, later, cum, size, act, grads)
+        cost=(2 * 10**10, 2 * 10**7, 10**7),
+        carry=carry,
+        identity=identity,
+    )
+
+
+def unproject_gate_kernel(grads_ref, w_ref, normed_ref, back_ref, w_out_ref, turned):
+    step = pl.program_id(0)
+
+    @pl.when(step == 0)
+    def _():
+        turned[...] = normed_ref[...].T
+
+    w_out_ref[...] = dot(turned[...], grads_ref[...]).astype(bf16)
+    product = dot_nt(grads_ref[...], w_ref[...])
+
+    @pl.when(step == 0)
+    def _():
+        back_ref[...] = product
+
+    @pl.when(step > 0)
+    def _():
+        back_ref[...] += product
+
+
+def unproject_gate(grads, weight, normed, carry=None, identity=None):
+    rows = normed.shape[0]
+    return launch(
+        unproject_gate_kernel,
+        "unproject_gate",
+        (INNER // COLS,),
+        [
+            pl.BlockSpec((rows, COLS), lambda n: (0, n)),
+            pl.BlockSpec((D, COLS), lambda n: (0, n)),
+            pl.BlockSpec((rows, D), lambda n: (0, 0)),
+        ],
+        [pl.BlockSpec((rows, D), lambda n: (0, 0)), pl.BlockSpec((D, COLS), lambda n: (0, n))],
+        [jax.ShapeDtypeStruct((rows, D), f32), jax.ShapeDtypeStruct((D, INNER), bf16)],
+        (grads, weight, normed),
+        scratch=[pltpu.VMEM((D, rows), bf16)],
+        cost=(4 * rows * D * INNER, 4 * D * INNER, 0),
+        carry=carry,
+        identity=identity,
+    )
 
 
 def unproject_kernel(
-    grads_ref, late_ref, w_ref, normed_ref, h_ref, g_ref, gain_ref,
+    grads_ref, late_ref, w_ref, normed_ref, h_ref, g_ref, gain_ref, back_ref,
     out_ref, gain_out_ref, w_out_ref,
     total, turned, mended,
 ):
@@ -693,7 +806,7 @@
 
     @pl.when(step == 0)
     def _():
-        total[...] = jnp.zeros_like(total)
+        total[...] = back_ref[...]
         turned[...] = normed_ref[...].T
 
     mended[...] = grads_ref[...]
@@ -721,13 +834,13 @@
         for_rows(rows, 32, one)
 
 
-def unproject(grads, late, weight, normed, h, g, gain_row):
+def unproject(grads, late, weight, normed, h, g, gain_row, back, carry=None, identity=None):
     rows = h.shape[0]
-    return pl.pallas_call(
+    return launch(
         unproject_kernel,
-        name="unproject",
-        grid=(WIDE // COLS,),
-        in_specs=[
+        "unproject",
+        (TAIL // COLS,),
+        [
             pl.BlockSpec((rows, COLS), lambda n: (0, n)),
             pl.BlockSpec((SLOTS, 8, COLS), lambda n: (0, 0, n)),
             pl.BlockSpec((D, COLS), lambda n: (0, n)),
@@ -735,30 +848,32 @@
             pl.BlockSpec((rows, D), lambda n: (0, 0)),
             pl.BlockSpec((rows, D), lambda n: (0, 0)),
             pl.BlockSpec((1, D), lambda n: (0, 0)),
-        ],
-        out_specs=[
+            pl.BlockSpec((rows, D), lambda n: (0, 0)),
+        ],
+        [
             pl.BlockSpec((rows, D), lambda n: (0, 0)),
             pl.BlockSpec((8, D), lambda n: (0, 0)),
             pl.BlockSpec((D, COLS), lambda n: (0, n)),
         ],
-        out_shape=[
+        [
             jax.ShapeDtypeStruct((rows, D), f32),
             jax.ShapeDtypeStruct((8, D), f32),
-            jax.ShapeDtypeStruct((D, WIDE), bf16),
-        ],
-        scratch_shapes=[
+            jax.ShapeDtypeStruct((D, TAIL), bf16),
+        ],
+        (grads, late, weight, normed, h, g, gain_row, back),
+        scratch=[
             pltpu.VMEM((rows, D), f32),
             pltpu.VMEM((D, rows), bf16),
             pltpu.VMEM((rows, COLS), bf16),
         ],
-        compiler_params=params(),
-        cost_estimate=pl.CostEstimate(
-            flops=4 * rows * D * WIDE, bytes_accessed=4 * D * WIDE, transcendentals=0
-        ),
-    )(grads, late, weight, normed, h, g, gain_row)
+        cost=(4 * rows * D * TAIL, 4 * D * TAIL, 0),
+        carry=carry,
+        identity=identity,
+    )
 
 
 MESH = pl.DeviceIdType.MESH
+ANY = pl.BlockSpec(memory_space=pl.ANY)
 DP_BITS = {"core": 1, "x": 2, "y": 4}
 STEPS = ("z1", "z2", "x", "y", "core")
 
@@ -773,215 +888,288 @@
         return (here["dp"], here["z"] + 1 - 2 * lax.rem(here["z"], 2))
     if step == "z2":
         return (here["dp"], here["z"] + 2 - 4 * (here["z"] // 2))
+    if step == "middle":
+        return (here["dp"], 3 - here["z"])
     return (here["dp"] + DP_BITS[step] * (1 - 2 * here[step]), here["z"])
 
 
-def greet(here):
+def greet(here, along=False):
+    peers = STEPS + ("middle",) if along else STEPS
     barrier = pltpu.get_barrier_semaphore()
-    for step in STEPS:
+    for step in peers:
         pl.semaphore_signal(barrier, inc=1, device_id=partner(here, step), device_id_type=MESH)
-    pl.semaphore_wait(barrier, len(STEPS))
-
-
-def pieces_of(shapes, split):
-    jobs = []
-    for index, (rows, columns) in enumerate(shapes):
-        parts, colours = split[index]
-        height, width = rows // parts, columns // colours
-        for part in range(parts):
-            for colour in range(colours):
-                jobs.append((index, part, colour, part * height, height, colour * width, width))
-    waves = []
-    for job in jobs:
-        if job[2] == 0:
-            waves.append([])
-        waves[-1].append(job)
-    return jobs, waves
-
-
-def gather_kernel(shapes, split, *refs):
-    count = len(shapes)
-    shards, wholes = refs[:count], refs[count : 2 * count]
-    local_sems, send_sems, recv_sems = refs[2 * count :]
-    here = place()
-    greet(here)
-    jobs, waves = pieces_of(shapes, split)
-    own = [
-        pltpu.make_async_copy(
-            shards[i], wholes[i].at[here["y"], here["x"], here["core"], here["z"]], local_sems.at[i]
-        )
-        for i in range(count)
-    ]
-    for copy in own:
-        copy.start()
-
-    def make(job, stage):
-        index, _, colour, top, height, left, width = job
-        order = ("z1", "z2", "x", "y", "core") if colour == 0 else ("z1", "z2", "y", "x", "core")
-        done = order[:stage]
-        axis = lambda name: slice(None) if name in done else here[name]
-        depth = here["z"]
-        if "z2" in done:
-            depth = slice(None)
-        elif "z1" in done:
-            depth = pl.ds(here["z"] // 2 * 2, 2)
-        rows, columns = pl.ds(top, height), pl.ds(left, width)
-        target = wholes[index].at[axis("y"), axis("x"), axis("core"), depth, rows, columns]
-        source = shards[index].at[rows, columns] if stage == 0 else target
-        number = jobs.index(job)
-        return pltpu.make_async_remote_copy(
-            src_ref=source,
-            dst_ref=target,
-            send_sem=send_sems.at[number, stage],
-            recv_sem=recv_sems.at[number, stage],
-            device_id=partner(here, order[stage]),
-            device_id_type=MESH,
-        )
-
-    stages = len(STEPS)
-    for tick in range(len(waves) + stages):
-        if tick == 1:
-            for copy in own:
-                copy.wait()
-        for stage in reversed(range(stages + 1)):
-            wave = tick - stage
-            if not 0 <= wave < len(waves):
-                continue
-            for job in waves[wave]:
-                if stage:
-                    make(job, stage - 1).wait()
-                if stage < stages:
-                    make(job, stage).start()
-
-
-def gather(shards, split, identity):
-    shapes = tuple(shard.shape for shard in shards)
-    jobs, _ = pieces_of(shapes, split)
-    count = len(shards)
-    wholes = pl.pallas_call(
-        functools.partial(gather_kernel, shapes, split),
-        name="gather",
-        in_specs=[pl.BlockSpec(memory_space=pl.ANY)] * count,
-        out_specs=[pl.BlockSpec(memory_space=pl.ANY)] * count,
-        out_shape=[jax.ShapeDtypeStruct((2, 2, 2, 4) + s.shape, s.dtype) for s in shards],
-        scratch_shapes=[
-            pltpu.SemaphoreType.DMA((count,)),
-            pltpu.SemaphoreType.DMA((len(jobs), len(STEPS))),
-            pltpu.SemaphoreType.DMA((len(jobs), len(STEPS))),
-        ],
-        compiler_params=params(collective_id=identity, has_side_effects=True),
-    )(*shards)
-    return [whole.reshape((-1,) + whole.shape[4:]) for whole in wholes]
-
-
-def reduce_kernel(shapes, split, *refs):
-    count = len(shapes)
-    jobs, waves = pieces_of(shapes, split)
-    number = len(jobs)
-    partials, heads_in = refs[:count], refs[count]
-    totals, heads_out = refs[count + 1 : 2 * count + 1], refs[2 * count + 1]
-    rest = refs[2 * count + 2 :]
-    kept = rest[:number]
-    landed = rest[number : 6 * number]
-    heads_landed, local_sems, send_sems, recv_sems, head_send, head_recv = rest[6 * number :]
-    here = place()
-    greet(here)
-    y, x, core, z = here["y"], here["x"], here["core"], here["z"]
-    half, odd = z // 2, lax.rem(z, 2)
-    stages = len(STEPS)
-
-    def order(job):
-        return ("core", "y", "x", "z2", "z1") if job[2] == 0 else ("core", "x", "y", "z2", "z1")
-
-    def area(job, stage, mine):
-        pick = lambda value: value if mine else 1 - value
-        if stage == 1:
-            return (pick(y), slice(None), slice(None)) if job[2] == 0 else (slice(None), pick(x), slice(None))
-        if stage == 2:
-            return (y, pick(x), slice(None)) if job[2] == 0 else (pick(y), x, slice(None))
-        if stage == 3:
-            return (y, x, pl.ds(pick(half) * 2, 2))
-        return (y, x, half * 2 + pick(odd))
-
-    def load(job):
-        index, _, _, top, height, left, width = job
-        place_in = partials[index].at[:, :, core, :, pl.ds(top, height), pl.ds(left, width)]
-        k = jobs.index(job)
-        return pltpu.make_async_copy(place_in, kept[k], local_sems.at[k])
-
-    def make(job, stage):
-        index, _, _, top, height, left, width = job
-        k = jobs.index(job)
-        if stage == 0:
-            source = partials[index].at[:, :, 1 - core, :, pl.ds(top, height), pl.ds(left, width)]
-        else:
-            source = kept[k].at[area(job, stage, False)]
-        return pltpu.make_async_remote_copy(
-            src_ref=source,
-            dst_ref=landed[stage * number + k],
-            send_sem=send_sems.at[k, stage],
-            recv_sem=recv_sems.at[k, stage],
-            device_id=partner(here, order(job)[stage]),
-            device_id_type=MESH,
-        )
-
-    def add(job, stage, mine):
-        k = jobs.index(job)
-        into, came = kept[k], landed[(stage - 1) * number + k]
-        pick = lambda value: value if mine else 1 - value
-        first = job[2] == 0
-
-        def accumulate(target, source):
-            into[target] = (into[target].astype(f32) + came[source].astype(f32)).astype(into.dtype)
-
-        if stage == 1:
-            def one(i, carry):
-                a, b = i // 4, lax.rem(i, 4)
-                where = (pick(y), a, b) if first else (a, pick(x), b)
-                accumulate(where, where)
-                return carry
-
-            lax.fori_loop(0, 8, one, 0)
-        elif stage == 2:
-            def one(b, carry):
-                if first:
-                    accumulate((y, pick(x), b), (pick(x), b))
-                else:
-                    accumulate((pick(y), x, b), (pick(y), b))
-                return carry
-
-            lax.fori_loop(0, 4, one, 0)
-        elif stage == 3:
-            for b in range(2):
-                accumulate((y, x, pick(half) * 2 + b), (pick(half) * 2 + b,))
-        else:
-            accumulate((y, x, half * 2 + pick(odd)), (pick(odd),))
-
-    def finish(job):
-        index, _, _, top, height, left, width = job
-        k = jobs.index(job)
-        summed = kept[k][y, x, z].astype(f32) + landed[4 * number + k][...].astype(f32)
-        totals[index][top : top + height, left : left + width] = summed
-
-    def heads_copy(stage):
-        return pltpu.make_async_remote_copy(
-            src_ref=heads_out,
-            dst_ref=heads_landed.at[stage],
-            send_sem=head_send.at[stage],
-            recv_sem=head_recv.at[stage],
-            device_id=partner(here, STEPS[stage]),
-            device_id_type=MESH,
-        )
-
-    heads_out[...] = heads_in[...]
-    for tick in range(len(waves) + stages):
-        if tick < stages:
-            heads_copy(tick).start()
-        for stage in reversed(range(stages + 1)):
-            wave = tick - stage
-            if not 0 <= wave < len(waves):
-                continue
-            for job in waves[wave]:
+    pl.semaphore_wait(barrier, len(peers))
+
+
+class Exchange:
+    def __init__(self, shapes, split, pace):
+        self.shapes, self.pace = shapes, pace
+        self.jobs, self.waves = [], []
+        for index, (rows, columns) in enumerate(shapes):
+            parts, pieces = split[index]
+            height, width = rows // parts, columns // pieces
+            for part in range(parts):
+                for piece in range(pieces):
+                    if piece % 2 == 0:
+                        self.waves.append([])
+                    job = (index, piece % 2, part * height, height, piece * width, width)
+                    self.jobs.append(job)
+                    self.waves[-1].append(job)
+
+    def plan(self):
+        last = len(self.waves) - 1 + self.pace * len(STEPS)
+        ticks = [[] for _ in range(last + 1)]
+        for stage in reversed(range(len(STEPS) + 1)):
+            for wave, jobs in enumerate(self.waves):
+                ticks[wave + self.pace * stage] += [(stage, job) for job in jobs]
+        return ticks
+
+
+class Gather(Exchange):
+    def __init__(self, shards, split, pace):
+        super().__init__(tuple(shard.shape for shard in shards), split, pace)
+        self.shards, self.wholes = list(shards), {}
+        self.entries = self.plan()
+
+    def done(self, index):
+        return max(t for t, entries in enumerate(self.entries) for _, job in entries if job[0] == index)
+
+    def whole(self, index):
+        found = self.wholes[index]
+        return found.reshape(-1, found.shape[-1])
+
+    def until(self, last):
+        first = getattr(self, "reached", 0)
+        self.reached = last + 1
+        return Run(self, first, last)
+
+
+class Run:
+    def __init__(self, gather, first, last):
+        self.gather = gather
+        self.entries = gather.entries[first : last + 1]
+        live = sorted({job[0] for entries in self.entries for stage, job in entries if stage < len(STEPS)})
+        self.live = live
+        self.fresh = [index for index in live if index not in gather.wholes]
+        self.old = [index for index in live if index in gather.wholes]
+        needed = {job[0] for entries in self.entries for stage, job in entries if stage == 0}
+        self.sources = sorted(needed | set(self.fresh))
+        self.args = [gather.shards[i] for i in self.sources] + [gather.wholes[i] for i in self.old]
+        self.in_specs = [ANY] * len(self.args)
+        self.out_specs = [ANY] * len(live)
+        self.out_shape = [
+            jax.ShapeDtypeStruct((2, 2, 2, 4) + gather.shapes[i], gather.shards[i].dtype) for i in live
+        ]
+        self.aliases = {len(self.sources) + k: live.index(i) for k, i in enumerate(self.old)}
+        self.started = [
+            (stage, job) for entries in self.entries for stage, job in entries if stage < len(STEPS)
+        ]
+        self.scratch = [
+            pltpu.SemaphoreType.DMA((max(1, len(self.fresh)),)),
+            pltpu.SemaphoreType.DMA((len(self.started),)),
+            pltpu.SemaphoreType.DMA((len(self.started),)),
+        ]
+
+    def results(self, wholes):
+        for index, whole in zip(self.live, wholes):
+            self.gather.wholes[index] = whole
+        return None
+
+    def ticks(self, ins, outs, scratch, along=False):
+        local_sems, send_sems, recv_sems = scratch
+        here = place()
+        shards = dict(zip(self.sources, ins))
+        wholes = dict(zip(self.live, outs))
+        own = [
+            pltpu.make_async_copy(
+                shards[i], wholes[i].at[here["y"], here["x"], here["core"], here["z"]], local_sems.at[k]
+            )
+            for k, i in enumerate(self.fresh)
+        ]
+
+        def make(stage, job):
+            index, colour, top, height, left, width = job
+            order = ("z1", "z2", "x", "y", "core") if colour == 0 else ("z1", "z2", "y", "x", "core")
+            done = order[:stage]
+            axis = lambda name: slice(None) if name in done else here[name]
+            depth = here["z"]
+            if "z2" in done:
+                depth = slice(None)
+            elif "z1" in done:
+                depth = pl.ds(here["z"] // 2 * 2, 2)
+            rows, columns = pl.ds(top, height), pl.ds(left, width)
+            target = wholes[index].at[axis("y"), axis("x"), axis("core"), depth, rows, columns]
+            source = shards[index].at[rows, columns] if stage == 0 else target
+            number = self.started.index((stage, job))
+            return pltpu.make_async_remote_copy(
+                src_ref=source,
+                dst_ref=target,
+                send_sem=send_sems.at[number],
+                recv_sem=recv_sems.at[number],
+                device_id=partner(here, order[stage]),
+                device_id_type=MESH,
+            )
+
+        ended = set()
+
+        def steps(number, entries):
+            actions = []
+            if number == 0:
+                actions.append(lambda: greet(here, along))
+                actions += [copy.start for copy in own]
+            if number == 1:
+                actions += [copy.wait for copy in own]
+            for stage, job in entries:
+                before = (stage - 1, job)
+                if before in self.started:
+                    actions.append(lambda before=before: make(*before).wait())
+                    ended.add(before)
+                if stage < len(STEPS):
+                    actions.append(lambda stage=stage, job=job: make(stage, job).start())
+            return actions
+
+        lists = [steps(number, entries) for number, entries in enumerate(self.entries)]
+        last = [lambda key=key: make(*key).wait() for key in self.started if key not in ended]
+        if len(lists) == 1:
+            last = [copy.wait for copy in own] + last
+        lists.append(last)
+
+        def run(actions):
+            for action in actions:
+                action()
+
+        return [functools.partial(run, actions) for actions in lists]
+
+
+class Reduce(Exchange):
+    def __init__(self, partials, split, pace=2, heads=None):
+        super().__init__(tuple(partial.shape[1:] for partial in partials), split, pace)
+        self.heads = heads is not None
+        self.aliases = {}
+        self.args = [partial.reshape((2, 2, 2, 4) + partial.shape[1:]) for partial in partials]
+        count, number = len(partials), len(self.jobs)
+        self.in_specs = [ANY] * count
+        outs = list(self.shapes)
+        if self.heads:
+            self.args.append(heads)
+            self.in_specs.append(pl.BlockSpec(heads.shape, lambda *_: (0, 0)))
+            outs.append(heads.shape)
+        self.out_specs = [pl.BlockSpec(shape, lambda *_: (0, 0)) for shape in outs]
+        self.out_shape = [jax.ShapeDtypeStruct(shape, f32) for shape in outs]
+        kept, landed = [], [[] for _ in STEPS]
+        for index, _, _, height, _, width in self.jobs:
+            kind = partials[index].dtype
+            kept.append(pltpu.VMEM((2, 2, 4, height, width), kind))
+            for stage, lead in enumerate(((2, 2, 4), (2, 4), (4,), (2,), ())):
+                landed[stage].append(pltpu.VMEM(lead + (height, width), kind))
+        tile = pltpu.SemaphoreType.DMA((number, len(STEPS)))
+        self.scratch = kept + sum(landed, []) + [pltpu.SemaphoreType.DMA((number,)), tile, tile]
+        if self.heads:
+            line = pltpu.SemaphoreType.DMA((len(STEPS),))
+            self.scratch += [pltpu.VMEM((len(STEPS),) + heads.shape, f32), line, line]
+
+    def results(self, totals):
+        return list(totals)
+
+    def ticks(self, partials, totals, scratch, along=False):
+        jobs, number, stages = self.jobs, len(self.jobs), len(STEPS)
+        kept, landed = scratch[:number], scratch[number : 6 * number]
+        local_sems, send_sems, recv_sems = scratch[6 * number : 6 * number + 3]
+        here = place()
+        y, x, core, z = here["y"], here["x"], here["core"], here["z"]
+        half, odd = z // 2, lax.rem(z, 2)
+
+        def order(job):
+            return ("core", "y", "x", "z2", "z1") if job[1] == 0 else ("core", "x", "y", "z2", "z1")
+
+        def leaving(job, stage):
+            if stage == 1:
+                return (1 - y, slice(None), slice(None)) if job[1] == 0 else (slice(None), 1 - x, slice(None))
+            if stage == 2:
+                return (y, 1 - x, slice(None)) if job[1] == 0 else (1 - y, x, slice(None))
+            if stage == 3:
+                return (y, x, pl.ds((1 - half) * 2, 2))
+            return (y, x, half * 2 + 1 - odd)
+
+        def cut(job, side):
+            index, _, top, height, left, width = job
+            return partials[index].at[:, :, side, :, pl.ds(top, height), pl.ds(left, width)]
+
+        def load(job):
+            k = jobs.index(job)
+            return pltpu.make_async_copy(cut(job, core), kept[k], local_sems.at[k])
+
+        def make(job, stage):
+            k = jobs.index(job)
+            return pltpu.make_async_remote_copy(
+                src_ref=cut(job, 1 - core) if stage == 0 else kept[k].at[leaving(job, stage)],
+                dst_ref=landed[stage * number + k],
+                send_sem=send_sems.at[k, stage],
+                recv_sem=recv_sems.at[k, stage],
+                device_id=partner(here, order(job)[stage]),
+                device_id_type=MESH,
+            )
+
+        def add(job, stage, mine):
+            k = jobs.index(job)
+            into, came = kept[k], landed[(stage - 1) * number + k]
+            pick = lambda value: value if mine else 1 - value
+            first = job[1] == 0
+
+            def accumulate(target, source):
+                into[target] = (into[target].astype(f32) + came[source].astype(f32)).astype(into.dtype)
+
+            if stage == 1:
+                def one(i, carry):
+                    a, b = i // 4, lax.rem(i, 4)
+                    where = (pick(y), a, b) if first else (a, pick(x), b)
+                    accumulate(where, where)
+                    return carry
+
+                lax.fori_loop(0, 8, one, 0)
+            elif stage == 2:
+                def one(b, carry):
+                    if first:
+                        accumulate((y, pick(x), b), (pick(x), b))
+                    else:
+                        accumulate((pick(y), x, b), (pick(y), b))
+                    return carry
+
+                lax.fori_loop(0, 4, one, 0)
+            elif stage == 3:
+                for b in range(2):
+                    accumulate((y, x, pick(half) * 2 + b), (pick(half) * 2 + b,))
+            else:
+                accumulate((y, x, half * 2 + pick(odd)), (pick(odd),))
+
+        def finish(job):
+            index, _, top, height, left, width = job
+            k = jobs.index(job)
+            summed = kept[k][y, x, z].astype(f32) + landed[4 * number + k][...].astype(f32)
+            totals[index][top : top + height, left : left + width] = summed
+
+        def heads_copy(stage):
+            heads_landed, head_send, head_recv = scratch[6 * number + 3 :]
+            return pltpu.make_async_remote_copy(
+                src_ref=totals[-1],
+                dst_ref=heads_landed.at[stage],
+                send_sem=head_send.at[stage],
+                recv_sem=head_recv.at[stage],
+                device_id=partner(here, STEPS[stage]),
+                device_id_type=MESH,
+            )
+
+        def tick(moment, entries):
+            if moment == 0:
+                greet(here, along)
+                if self.heads:
+                    totals[-1][...] = partials[-1][...]
+            if self.heads and 0 < moment <= stages:
+                heads_copy(moment - 1).wait()
+                totals[-1][...] = totals[-1][...] + scratch[6 * number + 3][moment - 1]
+            if self.heads and moment < stages:
+                heads_copy(moment).start()
+            for stage, job in entries:
                 if stage == 0:
                     make(job, 0).start()
                     load(job).start()
@@ -995,109 +1183,115 @@
                     add(job, stage, False)
                     make(job, stage).start()
                     add(job, stage, True)
-        if tick < stages:
-            heads_copy(tick).wait()
-            heads_out[...] = heads_out[...] + heads_landed[tick]
-
-
-def reduce(partials, heads, split, identity):
-    shapes = tuple(partial.shape[1:] for partial in partials)
-    jobs, _ = pieces_of(shapes, split)
-    count = len(partials)
-    kept, landed = [], [[] for _ in range(5)]
-    for index, _, colour, _, height, _, width in jobs:
-        kind = partials[index].dtype
-        kept.append(pltpu.VMEM((2, 2, 4, height, width), kind))
-        for stage, lead in enumerate(((2, 2, 4), (2, 4), (4,), (2,), ())):
-            landed[stage].append(pltpu.VMEM(lead + (height, width), kind))
-    tile = pltpu.SemaphoreType.DMA((len(jobs), 5))
-    return pl.pallas_call(
-        functools.partial(reduce_kernel, shapes, split),
-        name="reduce",
-        in_specs=[pl.BlockSpec(memory_space=pl.ANY)] * count + [pl.BlockSpec(memory_space=pltpu.VMEM)],
-        out_specs=[pl.BlockSpec(memory_space=pltpu.VMEM)] * (count + 1),
-        out_shape=[jax.ShapeDtypeStruct(s, f32) for s in shapes] + [jax.ShapeDtypeStruct(heads.shape, f32)],
-        scratch_shapes=kept
-        + sum(landed, [])
-        + [
-            pltpu.VMEM((5,) + heads.shape, f32),
-            pltpu.SemaphoreType.DMA((len(jobs),)),
-            tile,
-            tile,
-            pltpu.SemaphoreType.DMA((5,)),
-            pltpu.SemaphoreType.DMA((5,)),
-        ],
+
+        return [functools.partial(tick, moment, entries) for moment, entries in enumerate(self.plan())]
+
+
+def alone(exchange, name, identity):
+    ins, outs = len(exchange.in_specs), len(exchange.out_specs)
+
+    def kernel(*refs):
+        for tick in exchange.ticks(refs[:ins], refs[ins : ins + outs], refs[ins + outs :]):
+            tick()
+
+    found = pl.pallas_call(
+        kernel,
+        name=name,
+        grid=(1,),
+        in_specs=exchange.in_specs,
+        out_specs=exchange.out_specs,
+        out_shape=exchange.out_shape,
+        scratch_shapes=exchange.scratch,
+        input_output_aliases=exchange.aliases,
         compiler_params=params(collective_id=identity, has_side_effects=True),
-    )(*[partial.reshape((2, 2, 2, 4) + partial.shape[1:]) for partial in partials], heads)
-
-
-def chain_kernel(steps, last, local_ref, decay_ref, state_ref, send_ref, send_sems, recv_sems):
+    )(*exchange.args)
+    return exchange.results(found)
+
+
+def chain_kernel(steps, last, alone, local_ref, decay_ref, state_ref, landed, send_ref, send_sems, recv_sems):
     dp, me = lax.axis_index("dp"), lax.axis_index("seq")
-    slots = local_ref.shape[0]
+    number = pl.program_id(0)
+    total = landed.shape[0]
     receives = me > 0 if steps > 0 else me < last
     sends = me < last if steps > 0 else me > 0
-    barrier = pltpu.get_barrier_semaphore()
-
-    @pl.when(receives)
-    def _():
-        pl.semaphore_signal(barrier, inc=1, device_id=(dp, me - steps), device_id_type=MESH)
-
-    @pl.when(sends)
-    def _():
-        pl.semaphore_wait(barrier, 1)
-
-    def make(slot, part):
-        columns = pl.ds(part * CHAIN, CHAIN)
+
+    def make(part):
         return pltpu.make_async_remote_copy(
-            src_ref=send_ref.at[slot, part],
-            dst_ref=state_ref.at[slot, part],
-            send_sem=send_sems.at[slot, part],
-            recv_sem=recv_sems.at[slot, part],
+            src_ref=send_ref.at[part],
+            dst_ref=landed.at[part],
+            send_sem=send_sems.at[part],
+            recv_sem=recv_sems.at[part],
             device_id=(dp, me + steps),
             device_id_type=MESH,
         )
 
-    parts = [(slot, part) for slot in range(slots) for part in range(INNER // CHAIN)]
-
-    @pl.when(jnp.logical_not(receives))
-    def _():
-        state_ref[...] = jnp.zeros_like(state_ref)
-
-    for slot, part in parts:
-        @pl.when(receives)
+    if alone:
+        @pl.when(number == 0)
         def _():
-            make(slot, part).wait_recv()
-
-        @pl.when(sends)
-        def _():
-            decay = decay_ref[slot, 0:1, part * CHAIN : (part + 1) * CHAIN]
-            local = local_ref[slot, :, part * CHAIN : (part + 1) * CHAIN]
-            send_ref[slot, part] = (decay * state_ref[slot, part].astype(f32) + local).astype(bf16)
-            make(slot, part).start()
-
-    for slot, part in parts:
-        @pl.when(sends)
-        def _():
-            make(slot, part).wait_send()
-
-
-def chained(local, decay, steps, identity):
-    slots = local.shape[0]
-    parts = INNER // CHAIN
-    shape = (slots, parts, NSTATE, CHAIN)
-    return pl.pallas_call(
-        functools.partial(chain_kernel, steps, lax.axis_size("seq") - 1),
-        name="chain",
-        in_specs=[pl.BlockSpec(memory_space=pltpu.VMEM)] * 2,
-        out_specs=pl.BlockSpec(memory_space=pltpu.VMEM),
-        out_shape=jax.ShapeDtypeStruct(shape, bf16),
-        scratch_shapes=[
-            pltpu.VMEM(shape, bf16),
-            pltpu.SemaphoreType.DMA((slots, parts)),
-            pltpu.SemaphoreType.DMA((slots, parts)),
-        ],
-        compiler_params=params(collective_id=identity, has_side_effects=True),
-    )(local, decay)
+            chain_greet(steps, last, pltpu.get_barrier_semaphore())
+
+    @pl.when(jnp.logical_and(number < total, receives))
+    def _():
+        make(number).wait_recv()
+        state_ref[0] = landed[number]
+
+    @pl.when(jnp.logical_and(number < total, jnp.logical_not(receives)))
+    def _():
+        state_ref[0] = jnp.zeros(state_ref.shape[1:], bf16)
+
+    @pl.when(jnp.logical_and(number < total, sends))
+    def _():
+        decay = decay_ref[0, 0:1, :]
+        send_ref[number] = (decay * state_ref[0].astype(f32) + local_ref[0]).astype(bf16)
+        make(number).start()
+
+    @pl.when(jnp.logical_and(number == total, sends))
+    def _():
+        for part in range(total):
+            make(part).wait_send()
+
+
+def chain_greet(steps, last, barrier):
+    dp, me = lax.axis_index("dp"), lax.axis_index("seq")
+    receives = me > 0 if steps > 0 else me < last
+    sends = me < last if steps > 0 else me > 0
+
+    @pl.when(receives)
+    def _():
+        pl.semaphore_signal(barrier, inc=1, device_id=(dp, me - steps), device_id_type=MESH)
+
+    @pl.when(sends)
+    def _():
+        pl.semaphore_wait(barrier, 1)
+
+
+def chained(local, decay, slots, steps, identity, carry=None):
+    pieces = INNER // CHAIN
+    total = slots * pieces
+    last = lax.axis_size("seq") - 1
+    piece = lambda n: jnp.minimum(n, total - 1)
+    return launch(
+        functools.partial(chain_kernel, steps, last, carry is None),
+        "chain",
+        (total + 1,),
+        [
+            pl.BlockSpec((1, NSTATE, CHAIN), lambda n: (piece(n) // pieces, 0, piece(n) % pieces)),
+            pl.BlockSpec((1, 8, CHAIN), lambda n: (piece(n) // pieces, 0, piece(n) % pieces)),
+        ],
+        [pl.BlockSpec((1, NSTATE, CHAIN), lambda n: (piece(n), 0, 0))],
+        [jax.ShapeDtypeStruct((total, NSTATE, CHAIN), bf16)],
+        (local, decay),
+        scratch=[
+            pltpu.VMEM((total, NSTATE, CHAIN), bf16),
+            pltpu.VMEM((total, NSTATE, CHAIN), bf16),
+            pltpu.SemaphoreType.DMA((total,)),
+            pltpu.SemaphoreType.DMA((total,)),
+        ],
+        carry=carry,
+        identity=identity,
+        along=True,
+        remote=True,
+    )
 
 
 def passed_along(value, steps):
@@ -1111,6 +1305,14 @@
     if missing:
         state = jnp.concatenate([state, jnp.zeros((missing,) + state.shape[1:], state.dtype)], axis=0)
     return state
+
+
+def spaced(first, last, weights):
+    marks, sum_so_far = [], 0
+    for weight in weights:
+        sum_so_far += weight
+        marks.append(first + (last - first) * sum_so_far // sum(weights))
+    return marks
 
 
 def padded_rows(array, rows):
@@ -1181,24 +1383,28 @@
     positions = lax.axis_index("seq") * length + jnp.arange(length, dtype=jnp.int32)
     valid = (positions[None, :] < ordered(lengths)[:, None]).astype(f32).reshape(rows, 1)
     valid = jnp.broadcast_to(valid, (rows, LANES))
-    wide_in = jnp.pad(in_proj, ((0, 0), (0, 0), (0, WIDE - PROJ)))
-    small_mesh = lax.axis_size("dp") == 8 and lax.axis_size("seq") == 4
+    gates = in_proj[..., :INNER]
+    tails = jnp.pad(in_proj[..., INNER:], ((0, 0), (0, 0), (0, TAIL - (PROJ - INNER))))
+    ours = lax.axis_size("dp") == 8 and lax.axis_size("seq") == 4
     packed = pack_small(norm_gain, conv_weight, gate_gain)
-    if small_mesh:
-        shards, split = [packed], [(1, 1)]
-        for layer in range(LAYERS):
-            shards += [wide_in[layer], out_proj[layer]]
-            split += [(3, 2), (3, 2)]
-        everything, *wholes = gather(shards, split, 2 * LAYERS)
-        wholes = [whole.reshape(-1, whole.shape[-1]) for whole in wholes]
+    shards = [packed]
+    for layer in range(LAYERS):
+        shards += [tails[layer], gates[layer], out_proj[layer]]
+    ids = iter(range(100))
+    if ours:
+        moving = Gather(shards, [(1, 1)] + [(3, 2)] * (3 * LAYERS), 1)
+        tail_done, gate_done, out_done = [[moving.done(1 + 3 * layer + k) for layer in range(LAYERS)] for k in range(3)]
+        end = len(moving.entries) - 1
+        run = lambda last: moving.until(min(last, end)) if min(last, end) >= moving.reached else None
+        alone(moving.until(tail_done[0]), "gather", next(ids))
+        everything = moving.wholes[0].reshape((-1,) + packed.shape)
+        whole = moving.whole
     else:
-        everything = lax.all_gather(packed, ("dp", "seq"), axis=0, tiled=False)
-        wholes = [
-            lax.all_gather(shard, ("dp", "seq"), axis=0, tiled=True)
-            for layer in range(LAYERS)
-            for shard in (wide_in[layer], out_proj[layer])
-        ]
-    weights_in, weights_out = wholes[0::2], wholes[1::2]
+        gathered = [lax.all_gather(shard, ("dp", "seq"), axis=0, tiled=True) for shard in shards]
+        everything = gathered[0].reshape((-1,) + packed.shape)
+        whole = lambda index: gathered[index]
+        run = lambda last: None
+        tail_done = gate_done = out_done = [0] * LAYERS
     norm_all, conv_all, gate_all = unpack_small(everything, norm_gain, conv_weight, gate_gain)
     h = ordered(hidden).reshape(rows, D)
     kept = []
@@ -1213,20 +1419,25 @@
             8,
         )
         skip_row = jnp.repeat(d_skip[layer], HEADDIM).reshape(1, INNER)
-        proj, raw, normed = project(h, gain_row, weights_in[layer])
-        cube = proj.reshape(SLOTS, length, WIDE)
+        base = 1 + 3 * layer
+        more = tail_done[layer + 1] if layer + 1 < LAYERS else out_done[layer]
+        marks = spaced(tail_done[layer], out_done[layer], (1, 3, 2)) + spaced(out_done[layer], more, (1, 2))
+        proj, raw, normed, *_ = project(h, gain_row, whole(base), run(marks[0]), next(ids))
+        cube = proj.reshape(SLOTS, length, TAIL)
         raw = raw.reshape(SLOTS, length, LANES)
-        edge = passed_along(cube[:, length - (CONV - 1) :, INNER : INNER + CONVCH], 1)
-        edge = jnp.pad(edge.astype(f32), ((0, 0), (8 - (CONV - 1), 0), (0, 0)))
-        y, local, cum, size, act, decay = mix(cube, edge, taps, raw, heads, skip_row)
-        state = chained(local[:count], decay[:count], 1, layer)
+        edge = passed_along(cube[:, length - (CONV - 1) :, :CONVCH], 1)
+        edge = jnp.pad(edge, ((0, 0), (8 - (CONV - 1), 0), (0, 0)))
+        y, local, cum, size, act, decay, *_ = mix(cube, edge, taps, raw, heads, skip_row, run(marks[1]), next(ids))
+        state, *_ = chained(local, decay, count, 1, next(ids), run(marks[2]))
+        state = state.reshape(count, -1, NSTATE, CHAIN)
+        gate, *_ = project_gate(normed, whole(base + 1), run(marks[3]), next(ids))
         flat = lambda array: array.reshape(rows, -1)
-        h_next, mixture, inverse = branch(
-            flat(y), proj, flat(act), flat(cum), state, gate_row, weights_out[layer], h, valid
+        h_next, mixture, inverse, *_ = branch(
+            flat(y), gate, flat(act), flat(cum), state, gate_row, whole(base + 2), h, valid, run(marks[4]), next(ids)
         )
         kept.append(
-            (h, gain_row, gate_row, taps, heads, skip_row, proj, raw, normed, edge, cum, size, act,
-             decay, state, mixture, inverse)
+            (h, gain_row, gate_row, taps, heads, skip_row, proj, gate, raw, normed, edge, cum, size, act,
+             decay, state, mixture, inverse, whole(base), whole(base + 1), whole(base + 2))
         )
         h = h_next
     result = ordered(h.reshape(SLOTS, length, D))
@@ -1234,52 +1445,62 @@
     g = ordered(out_grad).reshape(rows, D)
     small = [None] * LAYERS
     partials = [None] * LAYERS
+    totals = [[None] * 3 for _ in range(LAYERS)]
+    waiting = None
+    cut = lambda partial: partial.reshape(lax.axis_size("dp") * lax.axis_size("seq"), -1, partial.shape[-1])
+
+    def summing(arrays):
+        if not ours or arrays[0] is None:
+            return None
+        return Reduce([cut(array) for array in arrays], [(3, 2)] * len(arrays))
+
     for layer in reversed(range(LAYERS)):
-        (h, gain_row, gate_row, taps, heads, skip_row, proj, raw, normed, edge, cum, size, act,
-         decay, state, mixture, inverse) = kept[layer]
-        cube = proj.reshape(SLOTS, length, WIDE)
+        (h, gain_row, gate_row, taps, heads, skip_row, proj, gate, raw, normed, edge, cum, size, act,
+         decay, state, mixture, inverse, weight_tail, weight_gate, weight_out) = kept[layer]
+        cube = proj.reshape(SLOTS, length, TAIL)
         flat = lambda array: array.reshape(rows, -1)
-        back, mean, grad_gate, partial_out = unbranch(
-            g, valid, mixture, proj, inverse, gate_row, weights_out[layer]
+        shaped = lambda array: array.reshape(SLOTS, length, -1)
+        back, mean, grad_gate, partial_out, *sums = unbranch(
+            g, valid, mixture, gate, inverse, gate_row, weight_out, summing([waiting]), next(ids)
         )
-        dy, grads, local = ungate(
-            back, mixture, proj, inverse, mean, gate_row, flat(act), flat(cum), count
+        if waiting is not None and ours:
+            totals[layer + 1][0] = sums[0][0]
+        dy, grads, local = ungate(back, mixture, gate, inverse, mean, gate_row, flat(act), flat(cum), count)
+        back, partial_gate = unproject_gate(grads, weight_gate, normed)
+        later, *_ = chained(local, decay, count, -1, next(ids))
+        later = later.reshape(count, -1, NSTATE, CHAIN)
+        grads, edge_grad, grad_taps, grad_heads, *sums = unmix(
+            cube, edge, taps, raw, heads, skip_row, shaped(dy), all_slots(state), all_slots(later),
+            cum, size, act, summing([partial_gate, partial_out]), next(ids),
         )
-        later = chained(local, decay[:count], -1, LAYERS + layer)
-        shaped = lambda array: array.reshape(SLOTS, length, -1)
-        grads, edge_grad, grad_taps, grad_heads = unmix(
-            cube, edge, taps, raw, heads, skip_row, shaped(dy), all_slots(state), all_slots(later),
-            cum, size, act, shaped(grads),
-        )
+        if ours:
+            totals[layer][1], totals[layer][2] = sums[0]
         late = passed_along(edge_grad[:, 8 - (CONV - 1) :].astype(bf16), -1).astype(f32)
-        late = jnp.pad(late, ((0, 0), (8 - (CONV - 1), 0), (INNER, WIDE - INNER - CONVCH)))
-        g, grad_norm, partial_in = unproject(
-            flat(grads), late, weights_in[layer], normed, h, g, gain_row
-        )
+        late = jnp.pad(late, ((0, 0), (8 - (CONV - 1), 0), (0, TAIL - CONVCH)))
+        g, grad_norm, waiting = unproject(flat(grads), late, weight_tail, normed, h, g, gain_row, back)
+        partials[layer] = (waiting, partial_gate, partial_out)
         small[layer] = (
             grad_norm[0], jnp.sum(grad_taps, axis=0)[:CONV], grad_gate[0],
             jnp.sum(grad_heads, axis=0)[:3, :HEADS],
         )
-        partials[layer] = (partial_in, partial_out)
     grad_hidden = ordered(g.reshape(SLOTS, length, D))
     stacked = [jnp.stack([small[layer][member] for layer in range(LAYERS)]) for member in range(4)]
     shares = share_small(*stacked[:3])
     head_sums = jnp.pad(stacked[3].reshape(-1, HEADS), ((0, 8 - 3 * LAYERS), (0, LANES - HEADS)))
-    grads_in, grads_out = [None] * LAYERS, [None] * LAYERS
-    if small_mesh:
-        cut = lambda partial: partial.reshape(lax.axis_size("dp") * lax.axis_size("seq"), -1, partial.shape[-1])
-        for layer in reversed(range(LAYERS)):
-            sent, split = [cut(partial) for partial in partials[layer]], [(3, 2), (3, 2)]
-            if layer == 0:
-                sent, split = sent + [shares], split + [(1, 1)]
-            grads_in[layer], grads_out[layer], *others = reduce(sent, head_sums, split, 2 * LAYERS + 1 + layer)
-        mine, head_sums = others
+    if ours:
+        totals[0][0], mine, head_sums = alone(
+            Reduce([cut(waiting), shares], [(3, 2), (1, 1)], heads=head_sums), "reduce", next(ids)
+        )
     else:
-        for layer in range(LAYERS):
-            grads_in[layer], grads_out[layer] = [
-                lax.psum_scatter(partial, ("dp", "seq"), scatter_dimension=0, tiled=True)
-                for partial in partials[layer]
+        totals = [
+            [
+                lax.optimization_barrier(
+                    lax.psum_scatter(partial, ("dp", "seq"), scatter_dimension=0, tiled=True)
+                ).astype(f32)
+                for partial in members
             ]
+            for members in partials
+        ]
         mine = lax.psum_scatter(shares, ("dp", "seq"), scatter_dimension=0, tiled=True)
         head_sums = lax.psum(head_sums, ("dp", "seq"))
     grad_norm, grad_conv, grad_gate = own_small(mine, norm_gain, conv_weight, gate_gain)
@@ -1288,10 +1509,10 @@
         result,
         grad_hidden,
         grad_norm,
-        jnp.stack(grads_in)[..., :PROJ].astype(f32),
+        jnp.stack([jnp.concatenate([gate, tail[:, : PROJ - INNER]], axis=1) for tail, gate, _ in totals]),
         grad_conv,
         grad_gate,
-        jnp.stack(grads_out).astype(f32),
+        jnp.stack([members[2] for members in totals]),
         grad_heads[:, 0],
         grad_heads[:, 1],
         grad_heads[:, 2],

time: 1380 us -> 1140 us (0.83)
  Pallas kernels: 1290 us -> 1050 us
    pallas_call x21 -> x24, Pallas kernels: 1290 us -> 1050 us  [the longest x11 591 us: launch(): pl.pallas_call(wrapped, name=name, grid=grid, in_specs=list(in_specs) + c...]
  transfers between devices with their start and end apart: 4 -> 4, of which waited for: 2 -> 1; matrix products, arithmetic and copies ran while one was open for 1% -> 2% of each run, Pallas kernels for 11% -> 0%
where the time goes in v2:
time: 1140 us; the launch traced here: 1120 us
  Pallas kernels  1050 us (92%)
  local copies, waits for them, and re-layouts  44.7 us (4%)
  other arithmetic  16.4 us (1%)
    pallas_call x11, Pallas kernels, launch(): pl.pallas_call(wrapped, name=name, grid=grid, in_specs=list(in_specs) + c...  591 us
    pallas_call x11, Pallas kernels, launch(): pl.pallas_call(kernel, name=name, grid=grid, in_specs=in_specs, out_specs...  255 us
    pallas_call x2, Pallas kernels, alone(): pl.pallas_call(kernel, name=name, grid=(1,), in_specs=exchange.in_specs,...  203 us
  transfers between devices with their start and end apart: 4, of which 1 were waited for; matrix products, arithmetic and copies ran while one was open for 2% of the time, Pallas kernels for 0%

profile of v2, /device:TPU:0, one launch (start us, length us, event | category | flops | bytes accessed | tf_op | source)
XLA Modules:
  0.0 1124.0 jit_solution(11983669871880788624)
XLA Ops:
  0.7 2.1 slice_bitcast_fusion.1
  2.8 1.9 slice_bitcast_fusion
  4.7 0.9 fusion.1
  6.4 128.2 %gather.1 = (bf16[2,2,2,4,16,128]{5,4,3,2,1,0:T(8,128)(2,1)}, bf16[2,2,2,4,48,3584]{5,4,3,2,1,0:T(8,128)(2,1)}, bf16[2,2,2,4,48,3072]{5,4,3,2,1,0:T(8,128)(2,1)}, bf16[2,2,2,4,96,1536]{5,4,3,2,1,0:T(8,128)(2,1)}) custom-call(bf16[16,128]{1,0:T(8,128)(2,1)} %pad_bitcast_fusion.1.refs_0_, bf16[48,3584]{1,0:T(8,128)(2,1)} %get-tuple-element.195.refs_1_, ...), custom_call_target="tpu_custom_call" | custom-call | tf_op jit(solution)/shard_map/gather/pallas_call | solution.py:1197
  134.6 0.9 copy.55
  138.4 2.0 reverse_select_fusion.3
  140.4 19.7 %project.2 = (f32[512,3584]{1,0:T(8,128)}, f32[512,128]{1,0:T(8,128)}, bf16[512,1536]{1,0:T(8,128)(2,1)}, bf16[2,2,2,4,48,3072]{5,4,3,2,1,0:T(8,128)(2,1)}, bf16[2,2,2,4,96,1536]{5,4,3,2,1,0:T(8,128)(2,1)}) custom-call(f32[512,1536]{1,0:T(8,128)} %bitcast.115, f32[1,1536]{1,0:T(1,128)} %slice.168.refs_1_.gain_ref, ...), custom_call_target="tpu_custom_call", output_to_operand_aliasing={{3}: (4, {}), {4}: (5, {})} | custom-call | flops 5637144576 | bytes 11010048 | tf_op jit(solution)/shard_map/project/pallas_call | solution.py:79
  160.1 1.6 slice.211
  161.7 1.9 collective-permute-start
  163.9 0.8 reshape.204
  164.8 0.9 copy.56
  167.9 2.0 reverse_select_fusion.1
  172.2 1.6 pad.61.refs_1_.refs_4_
  173.8 45.2 %mix.2 = (f32[2,256,3072]{2,1,0:T(8,128)}, f32[2,128,3072]{2,1,0:T(8,128)}, f32[2,256,128]{2,1,0:T(8,128)}, f32[2,256,128]{2,1,0:T(8,128)}, f32[2,256,256]{2,1,0...) custom-call(f32[2,256,3584]{2,1,0:T(8,128)} %bitcast.106, ...), custom_call_target="tpu_custom_call", output_to_operand_aliasing={{6}: (10, {}), {7}: (11, {})} | custom-call | flops 6000000000 | bytes 10000000 | tf_op jit(solution)/shard_map/mix/pallas_call | solution.py:79
  219.0 39.0 %chain.4 = (bf16[6,128,512]{2,1,0:T(8,128)(2,1)}, bf16[2,2,2,4,96,1536]{5,4,3,2,1,0:T(8,128)(2,1)}, bf16[2,2,2,4,48,3584]{5,4,3,2,1,0:T(8,128)(2,1)}, bf16[2,2,2,4,48,3072]{5,4,3,2,1,0:T(8,128)(2,1)}) custom-call(f32[2,128,3072]{2,1,0:T(8,128)} %get-tuple-element.110.refs_0_, ...), custom_call_target="tpu_custom_call", output_to_operand_aliasing={{1}: (3, {}), {2}: (4, {})} | custom-call | tf_op jit(solution)/shard_map/chain/pallas_call | solution.py:79
  258.0 27.9 %project_gate.2 = (f32[512,3072]{1,0:T(8,128)}, bf16[2,2,2,4,48,3584]{5,4,3,2,1,0:T(8,128)(2,1)}, bf16[2,2,2,4,48,3072]{5,4,3,2,1,0:T(8,128)(2,1)}) custom-call(bf16[512,1536]{1,0:T(8,128)(2,1)} %get-tuple-element.108.refs_0_.normed_ref, bf16[1536,3072]{1,0:T(8,128)(2,1)} %bitcast.103, ...), custom_call_target="tpu_custom_call", output_to_operand_aliasing={{1}: (3, {}), {2}: (4, {})} | custom-call | flops 4831838208 | bytes 9437184 | tf_op jit(solution)/shard_map/project_gate/pallas_call | solution.py:79
  285.9 0.8 broadcast_in_dim.14.refs_8_.valid_ref.refs_1_
  286.7 37.7 %branch.2 = (f32[512,1536]{1,0:T(8,128)}, f32[512,3072]{1,0:T(8,128)}, f32[512,128]{1,0:T(8,128)}, bf16[2,2,2,4,48,3584]{5,4,3,2,1,0:T(8,128)(2,1)}, bf16[2,2,2,...) custom-call(f32[512,3072]{1,0:T(8,128)} %bitcast.123, ...), custom_call_target="tpu_custom_call", output_to_operand_aliasing={{3}: (10, {}), {4}: (11, {})} | custom-call | flops 4831838208 | bytes 9437184 | tf_op jit(solution)/shard_map/branch/pallas_call | solution.py:79
  324.4 22.3 %project.3 = (f32[512,3584]{1,0:T(8,128)}, f32[512,128]{1,0:T(8,128)}, bf16[512,1536]{1,0:T(8,128)(2,1)}, bf16[2,2,2,4,48,3072]{5,4,3,2,1,0:T(8,128)(2,1)}, bf16[2,2,2,4,96,1536]{5,4,3,2,1,0:T(8,128)(2,1)}) custom-call(f32[512,1536]{1,0:T(8,128)} %get-tuple-element.123.refs_0_.h_ref, ...), custom_call_target="tpu_custom_call", output_to_operand_aliasing={{3}: (4, {}), {4}: (5, {})} | custom-call | flops 5637144576 | bytes 11010048 | tf_op jit(solution)/shard_map/project/pallas_call | solution.py:79
  346.7 1.0 slice.216
  347.7 5.0 collective-permute-start.1
  354.7 0.7 pad.65.refs_1_.refs_4_
  355.4 41.2 %mix.3 = (f32[2,256,3072]{2,1,0:T(8,128)}, f32[2,128,3072]{2,1,0:T(8,128)}, f32[2,256,128]{2,1,0:T(8,128)}, f32[2,256,128]{2,1,0:T(8,128)}, f32[2,256,256]{2,1,0...) custom-call(f32[2,256,3584]{2,1,0:T(8,128)} %bitcast.111, ...), custom_call_target="tpu_custom_call", output_to_operand_aliasing={{6}: (9, {}), {7}: (10, {})} | custom-call | flops 6000000000 | bytes 10000000 | tf_op jit(solution)/shard_map/mix/pallas_call | solution.py:79
  396.6 10.7 project_gate.3.gate_ref
  407.3 20.6 %chain.5 = (bf16[6,128,512]{2,1,0:T(8,128)(2,1)}, bf16[2,2,2,4,96,1536]{5,4,3,2,1,0:T(8,128)(2,1)}) custom-call(f32[2,128,3072]{2,1,0:T(8,128)} %get-tuple-element.136.refs_0_, f32[2,8,3072]{2,1,0:T(8,128)} %get-tuple-element.137.refs_1_.decay_ref, bf16[2,2,2,4,96,1536]{5,4,3,2,1,0:T(8,128)(2,1)} %get-tuple-element.138.refs_2_), custom_call_target="tpu_custom_call", output_to_operand_aliasing={{1}: (2, {})} | custom-call | tf_op jit(solution)/shard_map/chain/pallas_call | solution.py:79
  427.9 23.5 %branch.3 = (f32[512,1536]{1,0:T(8,128)}, f32[512,3072]{1,0:T(8,128)}, f32[512,128]{1,0:T(8,128)}) custom-call(f32[512,3072]{1,0:T(8,128)} %bitcast.122, f32[512,3072]{1,0:T(8,128)} %project_gate.3.gate_ref, f32[512,256]{1,0:T(8,128)} %bitcast.136, f32[512,128]{1,0:T(8,128)} %bitcast.140, bf16[1,6,128,512]{3,2,1,0:T(8,128)(2,1)} %bitcast.132, ...), custom_call_target="tpu_custom_call" | custom-call | flops 4831838208 | bytes 9437184 | tf_op jit(solution)/shard_map/branch/pallas_call | solution.py:47
  451.4 34.6 %unbranch.2 = (f32[512,3072]{1,0:T(8,128)}, f32[512,128]{1,0:T(8,128)}, f32[8,3072]{1,0:T(8,128)}, bf16[3072,1536]{1,0:T(8,128)(2,1)}) custom-call(f32[512,1536]{1,0:T(8,128)} %bitcast.124, f32[512,128]{1,0:T(8,128)} %broadcast_in_dim.14.refs_8_.valid_ref.refs_1_, f32[512,3072]{1,0:T(8,128)} %get-tuple-element.142.mixture_ref, ...), custom_call_target="tpu_custom_call" | custom-call | flops 9663676416 | bytes 18874368 | tf_op jit(solution)/shard_map/unbranch/pallas_call | solution.py:47
  486.1 17.3 %ungate.2 = (f32[512,3072]{1,0:T(8,128)}, bf16[512,3072]{1,0:T(8,128)(2,1)}, f32[1,128,3072]{2,1,0:T(8,128)}) custom-call(f32[512,3072]{1,0:T(8,128)} %get-tuple-element.144.back_ref, f32[512,3072]{1,0:T(8,128)} %get-tuple-element.142.mixture_ref, f32[512,3072]{1,0:T(8,128)} %project_gate.3.gate_ref, f32[512,128]{1,0:T(8,128)} %get-tuple-element.143.inverse_ref, ...), custom_call_target="tpu_custom_call" | custom-call | flops 1000000000 | bytes 20000000 | tf_op jit(solution)/shard_map/ungate/pallas_call | solution.py:47
  503.4 17.6 %unproject_gate.2 = (f32[512,1536]{1,0:T(8,128)}, bf16[1536,3072]{1,0:T(8,128)(2,1)}) custom-call(bf16[512,3072]{1,0:T(8,128)(2,1)} %get-tuple-element.149.grads_ref, bf16[1536,3072]{1,0:T(8,128)(2,1)} %bitcast.100, bf16[512,1536]{1,0:T(8,128)(2,1)} %get-tuple-element.132.normed_ref), custom_call_target="tpu_custom_call" | custom-call | flops 9663676416 | bytes 18874368 | tf_op jit(solution)/shard_map/unproject_gate/pallas_call | solution.py:47
  521.0 37.6 %chain.6 = bf16[6,128,512]{2,1,0:T(8,128)(2,1)} custom-call(f32[1,128,3072]{2,1,0:T(8,128)} %get-tuple-element.147.local_ref, f32[2,8,3072]{2,1,0:T(8,128)} %get-tuple-element.137.refs_1_.decay_ref), custom_call_target="tpu_custom_call" | custom-call | tf_op jit(solution)/shard_map/chain/pallas_call | solution.py:47
  558.6 1.3 concatenate.26.refs_10_
  559.9 2.5 concatenate.27.refs_11_
  562.4 128.8 %unmix.2 = (bf16[2,256,3584]{2,1,0:T(8,128)(2,1)}, f32[2,8,3328]{2,1,0:T(8,128)}, f32[2,8,3328]{2,1,0:T(8,128)}, f32[2,8,128]{2,1,0:T(8,128)}, f32[48,3072]{1,0:T(8,128)}, /*index=5*/f32[96,1536]{1,0:T(8,128)}) custom-call(f32[2,256,3584]{2,1,0:T(8,128)} %bitcast.113, f32[2,8,3328]{2,1,0:T(8,128)} %pad.65.refs_1_.refs_4_, f32[8,3328]{1,0:T(8,128)} %pad.66.refs_2_.refs_5_, ...), custom_call_target="tpu_custom_call" | custom-call | flops 20000000000 | bytes 20000000 | tf_op jit(solution)/shard_map/unmix/pallas_call | solution.py:79
  691.2 1.0 slice.252
  692.1 1.3 collective-permute-start.2
  693.4 1.3 concatenate.28.refs_10_
  695.5 1.0 reduce_sum.37
  696.6 0.9 slice.196
  698.2 0.7 pad_convert_fusion.1.late_ref
  698.9 25.8 %unproject.2 = (f32[512,1536]{1,0:T(8,128)}, f32[8,1536]{1,0:T(8,128)}, bf16[1536,3584]{1,0:T(8,128)(2,1)}) custom-call(bf16[512,3584]{1,0:T(8,128)(2,1)} %bitcast.168, f32[2,8,3584]{2,1,0:T(8,128)} %pad_convert_fusion.1.late_ref, bf16[1536,3584]{1,0:T(8,128)(2,1)} %bitcast.98, bf16[512,1536]{1,0:T(8,128)(2,1)} %get-tuple-element.132.normed_ref, ...), custom_call_target="tpu_custom_call" | custom-call | flops 11274289152 | bytes 22020096 | tf_op jit(solution)/shard_map/unproject/pallas_call | solution.py:47
  724.7 80.0 %unbranch.3 = (f32[512,3072]{1,0:T(8,128)}, f32[512,128]{1,0:T(8,128)}, f32[8,3072]{1,0:T(8,128)}, bf16[3072,1536]{1,0:T(8,128)(2,1)}, f32[48,3584]{1,0:T(8,128)}) custom-call(f32[512,1536]{1,0:T(8,128)} %get-tuple-element.155.refs_0_.g_ref, f32[512,128]{1,0:T(8,128)} %broadcast_in_dim.14.refs_8_.valid_ref.refs_1_, ...), custom_call_target="tpu_custom_call" | custom-call | flops 9663676416 | bytes 18874368 | tf_op jit(solution)/shard_map/unbranch/pallas_call | solution.py:79
  804.7 17.3 %ungate.3 = (f32[512,3072]{1,0:T(8,128)}, bf16[512,3072]{1,0:T(8,128)(2,1)}, f32[1,128,3072]{2,1,0:T(8,128)}) custom-call(f32[512,3072]{1,0:T(8,128)} %get-tuple-element.159.back_ref, f32[512,3072]{1,0:T(8,128)} %get-tuple-element.156.refs_2_.mixture_ref, f32[512,3072]{1,0:T(8,128)} %get-tuple-element.116.refs_1_.refs_3_.gate_ref, ...), custom_call_target="tpu_custom_call" | custom-call | flops 1000000000 | bytes 20000000 | tf_op jit(solution)/shard_map/ungate/pallas_call | solution.py:47
  822.0 17.5 %unproject_gate.3 = (f32[512,1536]{1,0:T(8,128)}, bf16[1536,3072]{1,0:T(8,128)(2,1)}) custom-call(bf16[512,3072]{1,0:T(8,128)(2,1)} %get-tuple-element.164.grads_ref, bf16[1536,3072]{1,0:T(8,128)(2,1)} %bitcast.104, bf16[512,1536]{1,0:T(8,128)(2,1)} %get-tuple-element.108.refs_0_.normed_ref), custom_call_target="tpu_custom_call" | custom-call | flops 9663676416 | bytes 18874368 | tf_op jit(solution)/shard_map/unproject_gate/pallas_call | solution.py:47
  839.5 28.0 %chain.7 = bf16[6,128,512]{2,1,0:T(8,128)(2,1)} custom-call(f32[1,128,3072]{2,1,0:T(8,128)} %get-tuple-element.162.local_ref, f32[2,8,3072]{2,1,0:T(8,128)} %get-tuple-element.111.refs_1_.decay_ref), custom_call_target="tpu_custom_call" | custom-call | tf_op jit(solution)/shard_map/chain/pallas_call | solution.py:47
  867.5 2.4 concatenate.29.refs_11_
  869.9 129.2 %unmix.3 = (bf16[2,256,3584]{2,1,0:T(8,128)(2,1)}, f32[2,8,3328]{2,1,0:T(8,128)}, f32[2,8,3328]{2,1,0:T(8,128)}, f32[2,8,128]{2,1,0:T(8,128)}, f32[48,3072]{1,0:T(8,128)}, /*index=5*/f32[96,1536]{1,0:T(8,128)}) custom-call(f32[2,256,3584]{2,1,0:T(8,128)} %bitcast.108, f32[2,8,3328]{2,1,0:T(8,128)} %pad.61.refs_1_.refs_4_, f32[8,3328]{1,0:T(8,128)} %pad.62.refs_2_.refs_5_, ...), custom_call_target="tpu_custom_call" | custom-call | flops 20000000000 | bytes 20000000 | tf_op jit(solution)/shard_map/unmix/pallas_call | solution.py:79
  999.1 0.8 reduce_sum.38
  999.9 1.0 slice.251
  1000.8 1.3 collective-permute-start.3
  1002.1 1.0 reduce_sum.36
  1003.2 0.9 slice.195
  1004.2 2.2 pad_maximum_fusion.1
  1007.1 0.8 slice.192
  1008.3 0.7 pad_convert_fusion.late_ref
  1009.0 25.4 %unproject.3 = (f32[512,1536]{1,0:T(8,128)}, f32[8,1536]{1,0:T(8,128)}, bf16[1536,3584]{1,0:T(8,128)(2,1)}) custom-call(bf16[512,3584]{1,0:T(8,128)(2,1)} %bitcast.167, f32[2,8,3584]{2,1,0:T(8,128)} %pad_convert_fusion.late_ref, bf16[1536,3584]{1,0:T(8,128)(2,1)} %bitcast.120, bf16[512,1536]{1,0:T(8,128)(2,1)} %get-tuple-element.108.refs_0_.normed_ref, ...), custom_call_target="tpu_custom_call" | custom-call | flops 11274289152 | bytes 22020096 | tf_op jit(solution)/shard_map/unproject/pallas_call | solution.py:47
  1034.4 0.8 slice.191
  1035.7 0.8 copy.52
  1036.5 75.1 %reduce.17 = (f32[48,3584]{1,0:T(8,128)}, f32[16,128]{1,0:T(8,128)}, f32[8,128]{1,0:T(8,128)}) custom-call(bf16[2,2,2,4,48,3584]{5,4,3,2,1,0:T(8,128)(2,1)} %bitcast.118, f32[2,2,2,4,16,128]{5,4,3,2,1,0:T(8,128)} %bitcast.142, f32[8,128]{1,0:T(8,128)} %pad.74.refs_2_), custom_call_target="tpu_custom_call" | custom-call | tf_op jit(solution)/shard_map/reduce/pallas_call | solution.py:1197
  1111.6 0.8 reshape.236
  1113.6 1.1 slice.201
  1116.8 1.6 pad_maximum_fusion
  1118.4 1.1 copy-done.2
  1119.5 1.0 copy-done.3
  1120.5 3.4 reverse_select_fusion
  (102 shorter events, 15.8 us)
Async XLA Ops:
  0.6 4.0 slice-start
  0.7 4.9 copy-start.11
  0.7 5.0 copy-start.16
  0.7 5.0 copy-start.15
  0.7 135.8 %copy-start.10 = (s32[2]{0:T(128)S(1)}, s32[2]{0:T(128)}, u32[]{:S(2)}) copy-start(s32[2]{0:T(128)} %param.13) | copy-start | bytes 28
  0.7 137.7 %copy-start = (f32[2,256,1536]{2,1,0:T(8,128)S(1)}, f32[2,256,1536]{2,1,0:T(8,128)}, u32[]{:S(2)}) copy-start(f32[2,256,1536]{2,1,0:T(8,128)} %param.11) | copy-start | bytes 9437188
  140.4 25.5 %copy-start.12 = (f32[2,48]{1,0:T(2,128)S(1)}, f32[2,48]{1,0:T(2,128)}, u32[]{:S(2)}) copy-start(f32[2,48]{1,0:T(2,128)} %param.19) | copy-start | bytes 1156
  140.4 25.5 %copy-start.13 = (f32[2,48]{1,0:T(2,128)S(1)}, f32[2,48]{1,0:T(2,128)}, u32[]{:S(2)}) copy-start(f32[2,48]{1,0:T(2,128)} %param.20) | copy-start | bytes 1156
  140.4 26.8 %copy-start.14 = (f32[2,48]{1,0:T(2,128)S(1)}, f32[2,48]{1,0:T(2,128)}, u32[]{:S(2)}) copy-start(f32[2,48]{1,0:T(2,128)} %param.21) | copy-start | bytes 1156
  140.4 27.6 %copy-start.1 = (f32[2,256,1536]{2,1,0:T(8,128)S(1)}, f32[2,256,1536]{2,1,0:T(8,128)}, u32[]{:S(2)}) copy-start(f32[2,256,1536]{2,1,0:T(8,128)} %param.12) | copy-start | bytes 9437188
  161.7 10.5 collective-permute-start
  347.7 7.0 collective-permute-start.1
  503.4 55.2 %copy-start.5 = (bf16[6,128,512]{2,1,0:T(8,128)(2,1)S(1)}, bf16[6,128,512]{2,1,0:T(8,128)(2,1)}, u32[]{:S(2)}) copy-start(bf16[6,128,512]{2,1,0:T(8,128)(2,1)} %get-tuple-element.139) | copy-start | bytes 2359300
  562.4 131.1 %copy-start.4 = (bf16[6,128,512]{2,1,0:T(8,128)(2,1)S(1)}, bf16[6,128,512]{2,1,0:T(8,128)(2,1)}, u32[]{:S(2)}) copy-start(bf16[6,128,512]{2,1,0:T(8,128)(2,1)} %get-tuple-element.119) | copy-start | bytes 2359300
  692.1 6.0 collective-permute-start.2
  869.9 134.2 %copy-start.6 = (f32[48,3584]{1,0:T(8,128)S(1)}, f32[48,3584]{1,0:T(8,128)}, u32[]{:S(2)}) copy-start(f32[48,3584]{1,0:T(8,128)} %get-tuple-element.184) | copy-start | bytes 2064388
  869.9 134.3 %copy-start.9 = (f32[96,1536]{1,0:T(8,128)S(1)}, f32[96,1536]{1,0:T(8,128)}, u32[]{:S(2)}) copy-start(f32[96,1536]{1,0:T(8,128)} %get-tuple-element.186) | copy-start | bytes 1769476
  999.1 7.3 copy-start.7
  1000.8 7.4 collective-permute-start.3
  1036.5 80.2 %copy-start.8 = (f32[48,3072]{1,0:T(8,128)S(1)}, f32[48,3072]{1,0:T(8,128)}, u32[]{:S(2)}) copy-start(f32[48,3072]{1,0:T(8,128)} %get-tuple-element.181) | copy-start | bytes 1769476
  1116.7 2.8 copy-start.2
  1116.7 3.8 copy-start.3

commit v3 on v2

--- a/solution.py
+++ b/solution.py
@@ -21,12 +21,11 @@
 
 LANES = 128
 TAIL = 3584
-BLK = 256
+BLK = 512
+MAPS = 2 * NSTATE
 NB = INNER // BLK
 COLS = 512
 PER = BLK // HEADDIM
-CHAIN = 512
-PARTS = CHAIN // BLK
 
 f32 = jnp.float32
 bf16 = jnp.bfloat16
@@ -36,12 +35,12 @@
 
 def launch(
     kernel, name, grid, in_specs, out_specs, out_shape, args, scratch=(), cost=None, carry=None, identity=None,
-    along=False, remote=False,
+    relay=False,
 ):
     options = {"compiler_params": params()}
     if cost is not None:
         options["cost_estimate"] = pl.CostEstimate(flops=cost[0], bytes_accessed=cost[1], transcendentals=cost[2])
-    if carry is not None or remote:
+    if carry is not None or relay:
         options["compiler_params"] = params(collective_id=identity, has_side_effects=True)
     if carry is None:
         return pl.pallas_call(
@@ -60,7 +59,7 @@
         step, total = 0, 1
         for axis, extent in enumerate(grid):
             step, total = step * extent + pl.program_id(axis), total * extent
-        ticks = carry.ticks(groups[1], groups[3], refs[at:], along)
+        ticks = carry.ticks(groups[1], groups[3], refs[at:], relay)
         plan = {}
         for number, tick in enumerate(ticks[:-1]):
             plan.setdefault(number * total // (len(ticks) - 1), []).append(tick)
@@ -147,6 +146,57 @@
     return pltpu.roll(columns, lax.rem(LANES - PER * block, LANES), 1)
 
 
+def fold(array):
+    return functools.reduce(jnp.add, [array[:, at : at + LANES] for at in range(0, array.shape[1], LANES)])
+
+
+def expander(block):
+    head = lax.broadcasted_iota(jnp.int32, (LANES, BLK), 0)
+    mine = lax.broadcasted_iota(jnp.int32, (LANES, BLK), 1) // HEADDIM + block * PER
+    return (head == mine).astype(bf16)
+
+
+def stack_halves(scratch, arrays):
+    length = arrays[0].shape[0]
+    for number, array in enumerate(arrays):
+        high, low = halves(array)
+        scratch[2 * number * length : (2 * number + 1) * length, :] = high
+        scratch[(2 * number + 1) * length : (2 * number + 2) * length, :] = low
+
+
+def spread_all(scratch, block, length):
+    wide = dot(scratch[...], expander(block))
+    return [
+        wide[at : at + length] + wide[at + length : at + 2 * length] for at in range(0, wide.shape[0], 2 * length)
+    ]
+
+
+def split_rows(cum_t, minus, plus):
+    rows, length = HEADS, cum_t.shape[1]
+    first = cum_t[:rows].astype(bf16).astype(f32)
+    rest = cum_t[:rows] - first
+    second = rest.astype(bf16).astype(f32)
+    third = rest - second
+    index = lax.broadcasted_iota(jnp.int32, (rows, 16, length), 1)
+    wide = lambda array: jnp.broadcast_to(array[:, None, :], (rows, 16, length))
+
+    def pick(offset, sign, ones):
+        found = jnp.where(jnp.logical_and(index >= ones, index < ones + 3), 1.0, 0.0)
+        for number, part in enumerate((first, second, third)):
+            found = jnp.where(index == offset + number, wide(sign * part), found)
+        return found.astype(bf16).reshape(rows * 16, length)
+
+    minus[...] = pick(0, -1.0, 3)
+    plus[...] = pick(3, 1.0, 0)
+
+
+def head_pairs(array, pair):
+    columns = array[:, pair * LANES : (pair + 1) * LANES]
+    lane = lax.broadcasted_iota(jnp.int32, columns.shape, 1)
+    zero = jnp.zeros_like(columns)
+    return jnp.where(lane < HEADDIM, columns, zero), jnp.where(lane < HEADDIM, zero, columns)
+
+
 def load_extended(scratch, edge_ref, rows_ref):
     scratch[0:8, :] = edge_ref[0]
     scratch[8:, :] = rows_ref[0]
@@ -165,12 +215,88 @@
     return first >= second
 
 
-def project_kernel(h_ref, gain_ref, w_ref, proj_ref, raw_ref, normed_ref):
+class Along:
+    def __init__(self, steps, pieces, shape, kind):
+        self.steps, self.pieces, self.shape, self.kind = steps, pieces, shape, kind
+        self.scratch = [
+            pltpu.VMEM((pieces + 1,) + shape, kind),
+            pltpu.VMEM((pieces,) + shape, kind),
+            pltpu.SemaphoreType.DMA((pieces,)),
+            pltpu.SemaphoreType.DMA((pieces,)),
+        ]
+
+    def bind(self, landed, sent, send_sems, recv_sems):
+        self.landed, self.sent, self.send_sems, self.recv_sems = landed, sent, send_sems, recv_sems
+        self.me, last = lax.axis_index("seq"), lax.axis_size("seq") - 1
+        ahead, behind = self.me < last, self.me > 0
+        self.sends, self.receives = (ahead, behind) if self.steps > 0 else (behind, ahead)
+
+    def peer(self, steps):
+        return (lax.axis_index("dp"), self.me + steps)
+
+    def greet(self):
+        barrier = pltpu.get_barrier_semaphore()
+
+        @pl.when(self.receives)
+        def _():
+            pl.semaphore_signal(barrier, inc=1, device_id=self.peer(-self.steps), device_id_type=pl.DeviceIdType.MESH)
+
+        @pl.when(self.sends)
+        def _():
+            pl.semaphore_wait(barrier, 1)
+
+    def open(self):
+        self.landed[self.pieces] = jnp.zeros(self.shape, self.kind)
+
+        @pl.when(jnp.logical_not(self.receives))
+        def _():
+            for piece in range(self.pieces):
+                self.landed[piece] = jnp.zeros(self.shape, self.kind)
+
+    def copy(self, piece):
+        return pltpu.make_async_remote_copy(
+            src_ref=self.sent.at[piece],
+            dst_ref=self.landed.at[piece],
+            send_sem=self.send_sems.at[piece],
+            recv_sem=self.recv_sems.at[piece],
+            device_id=self.peer(self.steps),
+            device_id_type=pl.DeviceIdType.MESH,
+        )
+
+    def take(self, piece):
+        @pl.when(self.receives)
+        def _():
+            self.copy(piece).wait_recv()
+
+    def give(self, piece, value):
+        @pl.when(self.sends)
+        def _():
+            self.sent[piece] = value()
+            self.copy(piece).start()
+
+    def grow(self, piece, local, decay):
+        self.take(piece)
+        self.give(piece, lambda: (decay * self.landed[piece].astype(f32) + local).astype(bf16))
+
+    def close(self):
+        @pl.when(self.sends)
+        def _():
+            for piece in range(self.pieces):
+                self.copy(piece).wait_send()
+
+
+def project_kernel(edge, alone, h_ref, gain_ref, w_ref, proj_ref, raw_ref, normed_ref, edge_ref, *flow):
     step = pl.program_id(0)
     total = h_ref.shape[0]
+    length = total // SLOTS
+    edge.bind(*flow)
 
     @pl.when(step == 0)
     def _():
+        if alone:
+            edge.greet()
+        edge.open()
+
         def one(rows):
             h = h_ref[rows, :]
             inverse = lax.rsqrt(jnp.mean(h * h, axis=-1, keepdims=True) + epsilon)
@@ -180,16 +306,24 @@
 
     product = dot(normed_ref[...], w_ref[...])
     proj_ref[...] = product
+    for slot in range(SLOTS):
+        edge.give(step * SLOTS + slot, lambda slot=slot: product[(slot + 1) * length - 8 : (slot + 1) * length])
 
     @pl.when(step == pl.num_programs(0) - 1)
     def _():
         raw_ref[...] = product[:, COLS - 2 * LANES : COLS - LANES]
+        for piece in range(edge.pieces):
+            edge.take(piece)
+            number, slot = divmod(piece, SLOTS)
+            edge_ref[slot, :, number * COLS : (number + 1) * COLS] = edge.landed[piece]
+        edge.close()
 
 
 def project(h, gain_row, weight, carry=None, identity=None):
     total = h.shape[0]
+    edge = Along(1, SLOTS * (TAIL // COLS), (8, COLS), f32)
     return launch(
-        project_kernel,
+        functools.partial(project_kernel, edge, carry is None),
         "project",
         (TAIL // COLS,),
         [
@@ -201,16 +335,159 @@
             pl.BlockSpec((total, COLS), lambda n: (0, n)),
             pl.BlockSpec((total, LANES), lambda n: (0, 0)),
             pl.BlockSpec((total, D), lambda n: (0, 0)),
+            pl.BlockSpec((SLOTS, 8, TAIL), lambda n: (0, 0, 0)),
         ],
         [
             jax.ShapeDtypeStruct((total, TAIL), f32),
             jax.ShapeDtypeStruct((total, LANES), f32),
             jax.ShapeDtypeStruct((total, D), bf16),
+            jax.ShapeDtypeStruct((SLOTS, 8, TAIL), f32),
         ],
         (h, gain_row, weight),
+        scratch=edge.scratch,
         cost=(2 * total * D * TAIL, 2 * D * TAIL, 0),
         carry=carry,
         identity=identity,
+        relay=True,
+    )
+
+
+def mix_kernel(
+    relay, alone, count, rows_ref, edge_ref, taps_ref, maps_ref, maps_edge_ref, maps_taps_ref, raw_ref, heads_ref, skip_ref,
+    y_ref, state_ref, cum_ref, step_ref, act_ref, decay_ref,
+    extended, maps_extended, inner, minus, plus, input_t, scales, local, decay, *flow,
+):
+    slot, block = pl.program_id(0), pl.program_id(1)
+    number = slot * NB + block
+    length = rows_ref.shape[1]
+    relay.bind(*flow)
+
+    @pl.when(number == 0)
+    def _():
+        if alone:
+            relay.greet()
+        relay.open()
+
+    def grow(piece):
+        relay.grow(piece, local[piece], decay[piece, 0:1, :])
+
+    due = number - 1 - 2 * relay.me
+
+    @pl.when(jnp.logical_and(due >= 0, due < NB))
+    def _():
+        grow(due)
+
+    @pl.when(block == 0)
+    def _():
+        load_extended(maps_extended, maps_edge_ref, maps_ref)
+        convolved = convolve(maps_extended, maps_taps_ref[...], length)
+        maps = convolved * sigmoid(convolved)
+        act_ref[0] = maps
+        products = dot_halves(halves(maps[:, NSTATE:]), halves(maps[:, :NSTATE]), dot_nt)
+        input_t[0], input_t[1] = halves(maps[:, :NSTATE].T)
+        causal = lower(length)
+        inner[...] = jnp.where(causal, products, 0.0)
+        size = softplus(raw_ref[0] + heads_ref[0:1, :])
+        decay = -size * jnp.exp(heads_ref[1:2, :])
+        cum = dot_exact(causal.astype(f32), decay)
+        cum_ref[0] = cum
+        step_ref[0] = size
+        split_rows(cum.T, minus, plus)
+        stack_halves(scales, [size, jnp.exp(cum[length - 1 :, :] - cum)])
+
+    load_extended(extended, edge_ref, rows_ref)
+    convolved = convolve(extended, taps_ref[...], length)
+    values = convolved * sigmoid(convolved)
+    wide_step, remaining = spread_all(scales, block, length)
+    stepped = values * wide_step
+    low = stepped.astype(bf16)
+    parts = []
+    for pair in range(PER // 2):
+        members = head_pairs(low, pair)
+        pieces = []
+        for first in range(0, length, LANES):
+            end = first + LANES
+            weights = []
+            for j in range(2):
+                rows = pl.ds(pl.multiple_of((block * PER + 2 * pair + j) * 16, 16), 16)
+                change = dot_tn(plus[rows, first:end], minus[rows, :end])
+                weights.append((inner[first:end, :end] * jnp.exp(jnp.minimum(change, 0.0))).astype(bf16))
+            pieces.append(
+                dot(jnp.concatenate(weights, axis=1), jnp.concatenate([member[:end] for member in members], axis=0))
+            )
+        parts.append(jnp.concatenate(pieces, axis=0))
+    y_ref[0] = jnp.concatenate(parts, axis=1) + skip_ref[...] * values
+    final = heads_first(cum_ref[0][length - 8 :, :], block)
+    rate = jnp.broadcast_to(spread(jnp.exp(final))[7:], (8, BLK))
+    decay_ref[0, 0] = rate
+
+    @pl.when(slot < count)
+    def _():
+        local[number] = dot_halves((input_t[0], input_t[1]), halves(stepped * remaining))
+        decay[number] = rate
+
+    @pl.when(number == SLOTS * NB - 1)
+    def _():
+        for piece in range(relay.pieces):
+            @pl.when(jnp.logical_or(piece >= NB, piece > due))
+            def _():
+                grow(piece)
+
+            state_ref[piece] = relay.landed[piece]
+        relay.close()
+
+
+def mix(proj, edge, taps, raw, heads, skip_row, count, carry=None, identity=None):
+    length = proj.shape[1]
+    relay = Along(1, count * NB, (NSTATE, BLK), bf16)
+    return launch(
+        functools.partial(mix_kernel, relay, carry is None, count),
+        "mix",
+        (SLOTS, NB),
+        [
+            pl.BlockSpec((1, length, BLK), lambda s, b: (s, 0, b)),
+            pl.BlockSpec((1, 8, BLK), lambda s, b: (s, 0, b)),
+            pl.BlockSpec((8, BLK), lambda s, b: (0, b)),
+            pl.BlockSpec((1, length, MAPS), lambda s, b: (s, 0, INNER // MAPS)),
+            pl.BlockSpec((1, 8, MAPS), lambda s, b: (s, 0, INNER // MAPS)),
+            pl.BlockSpec((8, MAPS), lambda s, b: (0, INNER // MAPS)),
+            pl.BlockSpec((1, length, LANES), lambda s, b: (s, 0, 0)),
+            pl.BlockSpec((8, LANES), lambda s, b: (0, 0)),
+            pl.BlockSpec((1, BLK), lambda s, b: (0, b)),
+        ],
+        [
+            pl.BlockSpec((1, length, BLK), lambda s, b: (s, 0, b)),
+            pl.BlockSpec((count * NB, NSTATE, BLK), lambda s, b: (0, 0, 0)),
+            pl.BlockSpec((1, length, LANES), lambda s, b: (s, 0, 0)),
+            pl.BlockSpec((1, length, LANES), lambda s, b: (s, 0, 0)),
+            pl.BlockSpec((1, length, MAPS), lambda s, b: (s, 0, 0)),
+            pl.BlockSpec((1, 1, 8, BLK), lambda s, b: (s, b, 0, 0)),
+        ],
+        [
+            jax.ShapeDtypeStruct((SLOTS, length, INNER), f32),
+            jax.ShapeDtypeStruct((count * NB, NSTATE, BLK), bf16),
+            jax.ShapeDtypeStruct((SLOTS, length, LANES), f32),
+            jax.ShapeDtypeStruct((SLOTS, length, LANES), f32),
+            jax.ShapeDtypeStruct((SLOTS, length, MAPS), f32),
+            jax.ShapeDtypeStruct((SLOTS, NB, 8, BLK), f32),
+        ],
+        (proj, edge, taps, proj, edge, taps, raw, heads, skip_row),
+        scratch=[
+            pltpu.VMEM((length + 8, BLK), f32),
+            pltpu.VMEM((length + 8, MAPS), f32),
+            pltpu.VMEM((length, length), f32),
+            pltpu.VMEM((16 * HEADS, length), bf16),
+            pltpu.VMEM((16 * HEADS, length), bf16),
+            pltpu.VMEM((2, NSTATE, length), bf16),
+            pltpu.VMEM((4 * length, LANES), bf16),
+            pltpu.VMEM((count * NB, NSTATE, BLK), f32),
+            pltpu.VMEM((count * NB, 8, BLK), f32),
+        ]
+        + relay.scratch,
+        cost=(6 * 10**9, 10**7, 10**7),
+        carry=carry,
+        identity=identity,
+        relay=True,
     )
 
 
@@ -234,101 +511,6 @@
     )
 
 
-def mix_kernel(
-    rows_ref, edge_ref, taps_ref, maps_ref, maps_edge_ref, maps_taps_ref, raw_ref, heads_ref, skip_ref,
-    y_ref, state_ref, cum_ref, step_ref, act_ref, decay_ref,
-    extended, inner, cum_t, input_t,
-):
-    block = pl.program_id(1)
-    length = rows_ref.shape[1]
-
-    @pl.when(block == 0)
-    def _():
-        load_extended(extended, maps_edge_ref, maps_ref)
-        convolved = convolve(extended, maps_taps_ref[...], length)
-        maps = convolved * sigmoid(convolved)
-        act_ref[0] = maps
-        products = dot_halves(halves(maps[:, NSTATE:]), halves(maps[:, :NSTATE]), dot_nt)
-        input_t[0], input_t[1] = halves(maps[:, :NSTATE].T)
-        causal = lower(length)
-        inner[...] = jnp.where(causal, products, 0.0)
-        size = softplus(raw_ref[0] + heads_ref[0:1, :])
-        decay = -size * jnp.exp(heads_ref[1:2, :])
-        cum = dot_exact(causal.astype(f32), decay)
-        cum_ref[0] = cum
-        step_ref[0] = size
-        cum_t[...] = cum.T
-
-    load_extended(extended, edge_ref, rows_ref)
-    convolved = convolve(extended, taps_ref[...], length)
-    values = convolved * sigmoid(convolved)
-    cum = heads_first(cum_ref[0], block)
-    stepped = values * spread(heads_first(step_ref[0], block))
-    low = stepped.astype(bf16)
-    parts = []
-    for j in range(PER):
-        row = cum_t[pl.ds(block * PER + j, 1), :]
-        column = cum[:, j : j + 1]
-        pieces = []
-        for first in range(0, length, LANES):
-            end = first + LANES
-            decays = jnp.exp(jnp.minimum(column[first:end] - row[:, :end], 0.0))
-            weights = (inner[first:end, :end] * decays).astype(bf16)
-            pieces.append(dot(weights, low[:end, j * HEADDIM : (j + 1) * HEADDIM]))
-        parts.append(jnp.concatenate(pieces, axis=0))
-    y_ref[0] = jnp.concatenate(parts, axis=1) + skip_ref[...] * values
-    final = cum[length - 1 :, :]
-    remaining = jnp.exp(final - cum)
-    state_ref[0] = dot_halves((input_t[0], input_t[1]), halves(stepped * spread(remaining)))
-    decay_ref[0] = jnp.broadcast_to(spread(jnp.exp(final)), (8, BLK))
-
-
-def mix(proj, edge, taps, raw, heads, skip_row, carry=None, identity=None):
-    length = proj.shape[1]
-    return launch(
-        mix_kernel,
-        "mix",
-        (SLOTS, NB),
-        [
-            pl.BlockSpec((1, length, BLK), lambda s, b: (s, 0, b)),
-            pl.BlockSpec((1, 8, BLK), lambda s, b: (s, 0, b)),
-            pl.BlockSpec((8, BLK), lambda s, b: (0, b)),
-            pl.BlockSpec((1, length, BLK), lambda s, b: (s, 0, NB)),
-            pl.BlockSpec((1, 8, BLK), lambda s, b: (s, 0, NB)),
-            pl.BlockSpec((8, BLK), lambda s, b: (0, NB)),
-            pl.BlockSpec((1, length, LANES), lambda s, b: (s, 0, 0)),
-            pl.BlockSpec((8, LANES), lambda s, b: (0, 0)),
-            pl.BlockSpec((1, BLK), lambda s, b: (0, b)),
-        ],
-        [
-            pl.BlockSpec((1, length, BLK), lambda s, b: (s, 0, b)),
-            pl.BlockSpec((1, NSTATE, BLK), lambda s, b: (s, 0, b)),
-            pl.BlockSpec((1, length, LANES), lambda s, b: (s, 0, 0)),
-            pl.BlockSpec((1, length, LANES), lambda s, b: (s, 0, 0)),
-            pl.BlockSpec((1, length, BLK), lambda s, b: (s, 0, 0)),
-            pl.BlockSpec((1, 8, BLK), lambda s, b: (s, 0, b)),
-        ],
-        [
-            jax.ShapeDtypeStruct((SLOTS, length, INNER), f32),
-            jax.ShapeDtypeStruct((SLOTS, NSTATE, INNER), f32),
-            jax.ShapeDtypeStruct((SLOTS, length, LANES), f32),
-            jax.ShapeDtypeStruct((SLOTS, length, LANES), f32),
-            jax.ShapeDtypeStruct((SLOTS, length, BLK), f32),
-            jax.ShapeDtypeStruct((SLOTS, 8, INNER), f32),
-        ],
-        (proj, edge, taps, proj, edge, taps, raw, heads, skip_row),
-        scratch=[
-            pltpu.VMEM((length + 8, BLK), f32),
-            pltpu.VMEM((length, length), f32),
-            pltpu.VMEM((LANES, length), f32),
-            pltpu.VMEM((2, NSTATE, length), bf16),
-        ],
-        cost=(6 * 10**9, 10**7, 10**7),
-        carry=carry,
-        identity=identity,
-    )
-
-
 def branch_kernel(
     y_ref, gate_ref, act_ref, cum_ref, state_ref, gain_ref, w_ref, h_ref, valid_ref,
     out_ref, mixture_ref, inverse_ref,
@@ -355,7 +537,7 @@
         gated = mixture * gate * sigmoid(gate)
         mixture_ref[span, :] = mixture
         square = gated * gated
-        squares[span, :] += square[:, :LANES] + square[:, LANES:]
+        squares[span, :] += fold(square)
         gated_low[span, :] = (gated * gain_ref[...]).astype(bf16)
     total[...] += dot(gated_low[...], w_ref[...])
 
@@ -381,9 +563,9 @@
         [
             pl.BlockSpec((rows, BLK), lambda b: (0, b)),
             pl.BlockSpec((rows, BLK), lambda b: (0, b)),
-            pl.BlockSpec((rows, BLK), lambda b: (0, 0)),
+            pl.BlockSpec((rows, MAPS), lambda b: (0, 0)),
             pl.BlockSpec((rows, LANES), lambda b: (0, 0)),
-            pl.BlockSpec((count, 1, NSTATE, BLK), lambda b: (0, b // PARTS, 0, b % PARTS)),
+            pl.BlockSpec((count, 1, NSTATE, BLK), lambda b: (0, b, 0, 0)),
             pl.BlockSpec((1, BLK), lambda b: (0, b)),
             pl.BlockSpec((BLK, D), lambda b: (b, 0)),
             pl.BlockSpec((rows, D), lambda b: (0, 0)),
@@ -438,7 +620,7 @@
         norm_low[span, :] = (unit * gain_ref[...]).astype(bf16)
         gain_out_ref[0:1, :] += jnp.sum(back * unit, axis=0, keepdims=True)
         product = gated * back * gain_ref[...]
-        mean_ref[span, :] += product[:, :LANES] + product[:, LANES:]
+        mean_ref[span, :] += fold(product)
 
     for_rows(rows, 128, one)
     w_out_ref[...] = dot_tn(norm_low[...], low[...]).astype(bf16)
@@ -515,7 +697,7 @@
         dgate_ref[span, :] = (grad * mixture * curve * (1.0 + gate * (1.0 - curve))).astype(bf16)
         if slot < state_ref.shape[0]:
             grown = spread(jnp.exp(heads_first(cum_ref[span, :], block)))
-            state_ref[slot] = dot_halves((output_t[slot, 0], output_t[slot, 1]), halves(dy * grown))
+            state_ref[slot, 0] = dot_halves((output_t[slot, 0], output_t[slot, 1]), halves(dy * grown))
 
 
 def ungate(back, mixture, gate, inverse, mean, gain_row, act, cum, count, carry=None, identity=None):
@@ -532,18 +714,18 @@
             pl.BlockSpec((rows, LANES), lambda b: (0, 0)),
             pl.BlockSpec((rows, LANES), lambda b: (0, 0)),
             pl.BlockSpec((1, BLK), lambda b: (0, b)),
-            pl.BlockSpec((rows, BLK), lambda b: (0, 0)),
+            pl.BlockSpec((rows, MAPS), lambda b: (0, 0)),
             pl.BlockSpec((rows, LANES), lambda b: (0, 0)),
         ],
         [
             pl.BlockSpec((rows, BLK), lambda b: (0, b)),
             pl.BlockSpec((rows, BLK), lambda b: (0, b)),
-            pl.BlockSpec((count, NSTATE, BLK), lambda b: (0, 0, b)),
+            pl.BlockSpec((count, 1, NSTATE, BLK), lambda b: (0, b, 0, 0)),
         ],
         [
             jax.ShapeDtypeStruct((rows, INNER), f32),
             jax.ShapeDtypeStruct((rows, INNER), bf16),
-            jax.ShapeDtypeStruct((count, NSTATE, INNER), f32),
+            jax.ShapeDtypeStruct((count, NB, NSTATE, BLK), f32),
         ],
         (back, mixture, gate, inverse, mean, gain_row, act, cum),
         scratch=[pltpu.VMEM((count, 2, NSTATE, length), bf16)],
@@ -554,37 +736,64 @@
 
 
 def unmix_kernel(
-    rows_ref, edge_ref, taps_ref, maps_ref, maps_edge_ref, maps_taps_ref, raw_ref, heads_ref, skip_ref,
-    dy_ref, state_ref, later_ref, cum_ref, step_ref, act_ref,
-    grads_ref, edge_out_ref, taps_out_ref, heads_out_ref,
-    extended, inner, d_inner, cum_t, grad_ext, d_maps, d_cum, d_step, over_rows, sums,
+    relay, edge, alone, count, rows_ref, edge_ref, taps_ref, maps_ref, maps_edge_ref, maps_taps_ref, raw_ref, heads_ref, skip_ref,
+    dy_ref, state_ref, local_ref, decay_ref, cum_ref, step_ref, act_ref,
+    grads_ref, late_ref, taps_out_ref, heads_out_ref,
+    extended, maps_extended, inner, d_inner, minus, plus, scales, grad_ext, maps_grad_ext, d_maps, d_cum, d_step, over_rows, sums, *flow,
 ):
-    block = pl.program_id(1)
+    turn, block = pl.program_id(0), pl.program_id(1)
+    slot = SLOTS - 1 - turn
     length = rows_ref.shape[1]
-    count = state_ref.shape[0]
-
-    def conv_back(gradient, taps):
-        grad_ext[8 : 8 + length, :] = gradient
-        back = taps[0:1] * grad_ext[3 : 3 + length + 8, :]
+    relay.bind(*flow[:4])
+    edge.bind(*flow[4:])
+    reached = slot < count
+    piece = jnp.where(reached, slot * NB + block, relay.pieces)
+    number = turn * (NB + 1) + block
+
+    @pl.when(number == 0)
+    def _():
+        if alone:
+            relay.greet()
+        relay.open()
+        edge.open()
+
+    def grow(member):
+        its_slot, its_block = member // NB, lax.rem(member, NB)
+        relay.grow(member, local_ref[its_slot, its_block], decay_ref[its_slot, its_block, 0:1, :])
+
+    due = number - jnp.minimum(2 * (lax.axis_size("seq") - 1 - relay.me), NB)
+
+    @pl.when(jnp.logical_and(due >= 0, due < NB))
+    def _():
+        grow(due)
+
+    if count == SLOTS:
+        @pl.when(jnp.logical_and(turn == 0, block < NB))
+        def _():
+            grow(NB + block)
+
+    def conv_back(gradient, taps, given, padded):
+        padded[8 : 8 + length, :] = gradient
+        back = taps[0:1] * padded[3 : 3 + length + 8, :]
         for k in range(1, CONV):
-            back = back + taps[k : k + 1] * grad_ext[3 - k : 3 - k + length + 8, :]
-        edge_out_ref[0] = back[:8]
-        grads_ref[0] = back[8:].astype(bf16)
+            back = back + taps[k : k + 1] * padded[3 - k : 3 - k + length + 8, :]
         lines = [
-            jnp.sum(gradient * extended[5 + k : 5 + k + length, :], axis=0, keepdims=True)
-            for k in range(CONV)
+            jnp.sum(gradient * given[5 + k : 5 + k + length, :], axis=0, keepdims=True) for k in range(CONV)
         ]
-        lines.append(jnp.zeros((8 - CONV, BLK), f32))
-        taps_out_ref[0] = jnp.concatenate(lines, axis=0)
+        lines.append(jnp.zeros((8 - CONV, gradient.shape[1]), f32))
+        return back[:8], back[8:].astype(bf16), jnp.concatenate(lines, axis=0)
 
     @pl.when(block == 0)
     def _():
-        grad_ext[0:8, :] = jnp.zeros((8, BLK), f32)
-        grad_ext[8 + length :, :] = jnp.zeros((8, BLK), f32)
+        for padded in (grad_ext, maps_grad_ext):
+            padded[0:8, :] = jnp.zeros((8, padded.shape[1]), f32)
+            padded[8 + length :, :] = jnp.zeros((8, padded.shape[1]), f32)
         maps = act_ref[0]
         products = dot_halves(halves(maps[:, :NSTATE]), halves(maps[:, NSTATE:]), dot_nt)
         inner[...] = jnp.where(lower(length).T, products, 0.0)
-        cum_t[...] = cum_ref[0].T
+        cum = cum_ref[0]
+        split_rows(cum.T, minus, plus)
+        stack_halves(scales, [step_ref[0], jnp.exp(cum[length - 1 :, :] - cum), jnp.exp(cum)])
         d_inner[...] = jnp.zeros_like(d_inner)
         d_maps[...] = jnp.zeros_like(d_maps)
         d_cum[...] = jnp.zeros_like(d_cum)
@@ -598,56 +807,66 @@
         convolved = convolve(extended, taps_ref[...], length)
         curve = sigmoid(convolved)
         values = convolved * curve
-        cum = heads_first(cum_ref[0], block)
-        size = spread(heads_first(step_ref[0], block))
+        size, remaining, grown = spread_all(scales, block, length)
         stepped = values * size
         low = stepped.astype(bf16)
         dy = dy_ref[0]
         dy_low = dy.astype(bf16)
-        lane = lax.broadcasted_iota(jnp.int32, (1, LANES), 1)
+        dy_t = dy.T.astype(bf16)
         parts = []
-        for j in range(PER):
-            head = block * PER + j
-            row = cum_t[pl.ds(head, 1), :]
-            column = cum[:, j : j + 1]
-            dy_head = dy_low[:, j * HEADDIM : (j + 1) * HEADDIM]
-            low_head = low[:, j * HEADDIM : (j + 1) * HEADDIM]
+        moved_all = {first: [] for first in range(0, length, LANES)}
+        for pair in range(PER // 2):
+            low_pair = head_pairs(low, pair)
+            dy_pair = head_pairs(dy_low, pair)
+            dy_pair_t = dy_t[pair * LANES : (pair + 1) * LANES, :]
             pieces = []
-            row_sums = []
-            column_sums = None
+            column_sums = [None, None]
             for first in range(0, length, LANES):
                 end = first + LANES
-                decays = jnp.exp(jnp.minimum(row[:, first:] - column[first:end], 0.0))
+                weights = []
                 products = inner[first:end, first:]
-                weights = (products * decays).astype(bf16)
-                grads = dot_nt(low_head[first:end], dy_head[first:]) * decays
-                d_inner[first:end, first:] += grads
-                pieces.append(dot(weights, dy_head[first:]))
-                moved = grads * products
-                row_sums.append(jnp.sum(moved, axis=1, keepdims=True))
-                found = jnp.sum(moved, axis=0, keepdims=True)
-                if first:
-                    found = jnp.concatenate([jnp.zeros((1, first), f32), found], axis=1)
-                column_sums = found if column_sums is None else column_sums + found
+                grads_sum = None
+                for j in range(2):
+                    rows = pl.ds(pl.multiple_of((block * PER + 2 * pair + j) * 16, 16), 16)
+                    change = dot_tn(minus[rows, first:end], plus[rows, first:])
+                    decays = jnp.exp(jnp.minimum(change, 0.0))
+                    weights.append((products * decays).astype(bf16))
+                    grads = dot(low_pair[j][first:end], dy_pair_t[:, first:]) * decays
+                    grads_sum = grads if grads_sum is None else grads_sum + grads
+                    moved = (grads * products).astype(bf16)
+                    moved_all[first].append(moved)
+                    found = jnp.sum(moved.astype(f32), axis=0, keepdims=True)
+                    if first:
+                        found = jnp.concatenate([jnp.zeros((1, first), f32), found], axis=1)
+                    column_sums[j] = found if column_sums[j] is None else column_sums[j] + found
+                d_inner[first:end, first:] += grads_sum
+                pieces.append(
+                    dot(jnp.concatenate(weights, axis=1), jnp.concatenate([part[first:] for part in dy_pair], axis=0))
+                )
             parts.append(jnp.concatenate(pieces, axis=0))
-            over_rows[pl.ds(head, 1), :] = column_sums
-            d_cum[...] -= jnp.where(lane == head, jnp.concatenate(row_sums, axis=0), 0.0)
-        d_stepped = jnp.concatenate(parts, axis=1)
+            for j in range(2):
+                over_rows[pl.ds(block * PER + 2 * pair + j, 1), :] = column_sums[j]
+        intra = jnp.concatenate(parts, axis=1)
+        for first, moved in moved_all.items():
+            span = length - first
+            head = lax.broadcasted_iota(jnp.int32, (PER * span, LANES), 0) // span + block * PER
+            chosen = (lax.broadcasted_iota(jnp.int32, (PER * span, LANES), 1) == head).astype(bf16)
+            d_cum[first : first + LANES, :] -= dot(jnp.concatenate(moved, axis=1), chosen)
         which = lax.broadcasted_iota(jnp.int32, (BLK, LANES), 0) // HEADDIM + block * PER
         chosen = which == lax.broadcasted_iota(jnp.int32, (BLK, LANES), 1)
         member = chosen.astype(f32)
         member_low = chosen.astype(bf16)
-        state = state_ref[0, 0]
-        later = later_ref[0, 0]
+        state = jnp.where(reached, state_ref[0, 0].astype(f32), 0.0).astype(bf16)
+        later = relay.landed[piece]
         maps = act_ref[0]
-        remaining = spread(jnp.exp(cum[length - 1 :, :] - cum))
-        grown = spread(jnp.exp(cum))
         from_later = dot_member(maps[:, :NSTATE], later) * remaining
-        d_stepped = d_stepped + from_later
+        d_stepped = intra + from_later
         left = stepped * remaining
         grown_dy = dy * grown
         used = stepped * from_later
-        d_cum[...] += dot_member(grown_dy * dot_member(maps[:, NSTATE:], state) - used, member_low)
+        d_cum[...] += dot_member(
+            grown_dy * dot_member(maps[:, NSTATE:], state) - used, member_low
+        )
         d_maps[:, :NSTATE] += dot_nt(left.astype(bf16), later)
         d_maps[:, NSTATE:] += dot_nt(grown_dy.astype(bf16), state)
         d_step[...] += dot_member(d_stepped * values, member_low)
@@ -662,22 +881,27 @@
         )
         sums[...] += dot_exact(lines, member)
         d_values = d_stepped * size + skip_ref[...] * dy
-        conv_back(d_values * curve * (1.0 + convolved * (1.0 - curve)), taps_ref[...])
+        before, grads_ref[0], taps_out_ref[0] = conv_back(
+            d_values * curve * (1.0 + convolved * (1.0 - curve)), taps_ref[...], extended, grad_ext
+        )
+        edge.give(number, lambda: before)
 
     @pl.when(block == NB)
     def _():
-        load_extended(extended, maps_edge_ref, maps_ref)
-        convolved = convolve(extended, maps_taps_ref[...], length)
+        load_extended(maps_extended, maps_edge_ref, maps_ref)
+        convolved = convolve(maps_extended, maps_taps_ref[...], length)
         curve = sigmoid(convolved)
         maps = act_ref[0]
-        d_both = jnp.where(lower(length).T, d_inner[...], 0.0)
-        d_input = d_maps[:, :NSTATE] + dot_halves(halves(d_both), halves(maps[:, NSTATE:]))
-        d_output = d_maps[:, NSTATE:] + dot_halves(halves(d_both.T), halves(maps[:, :NSTATE]))
+        masked = jnp.where(lower(length).T, d_inner[...], 0.0)
+        d_input = d_maps[:, :NSTATE] + dot_halves(halves(masked), halves(maps[:, NSTATE:]))
+        d_output = d_maps[:, NSTATE:] + dot_halves(halves(masked.T), halves(maps[:, :NSTATE]))
         d_both = jnp.concatenate([d_input, d_output], axis=1)
-        conv_back(d_both * curve * (1.0 + convolved * (1.0 - curve)), maps_taps_ref[...])
-
-    @pl.when(block == NB + 1)
-    def _():
+        before, inside, lines = conv_back(
+            d_both * curve * (1.0 + convolved * (1.0 - curve)), maps_taps_ref[...], maps_extended, maps_grad_ext
+        )
+        rest = jnp.zeros((8, BLK - MAPS), f32)
+        edge.give(number, lambda: jnp.concatenate([before, rest], axis=1))
+        taps_out_ref[0] = jnp.concatenate([lines, rest], axis=1)
         final = cum_ref[0][length - 1 :, :]
         at_end = sums[0:1, :] + jnp.exp(final) * sums[2:3, :]
         d_total = d_cum[...] + over_rows[...].T
@@ -687,7 +911,8 @@
         rate = jnp.exp(heads_ref[1:2, :])
         size = step_ref[0]
         d_raw = (d_step[...] - d_decay * rate) * sigmoid(raw_ref[0] + heads_ref[0:1, :])
-        grads_ref[0] = jnp.concatenate([d_raw, jnp.zeros_like(d_raw)], axis=1).astype(bf16)
+        d_raw_low = d_raw.astype(bf16)
+        grads_ref[0] = jnp.concatenate([inside, d_raw_low, jnp.zeros_like(d_raw_low)], axis=1)
         heads_out_ref[0] = jnp.concatenate(
             [
                 jnp.sum(d_raw, axis=0, keepdims=True),
@@ -698,60 +923,80 @@
             axis=0,
         )
 
-
-def unmix(proj, edge, taps, raw, heads, skip_row, dy, state, later, cum, size, act, carry=None, identity=None):
+    @pl.when(number == SLOTS * (NB + 1) - 1)
+    def _():
+        relay.close()
+        for given in range(edge.pieces):
+            edge.take(given)
+            its_turn, its_block = divmod(given, NB + 1)
+            late_ref[SLOTS - 1 - its_turn, :, its_block * BLK : (its_block + 1) * BLK] = edge.landed[given]
+        edge.close()
+
+
+def unmix(proj, edge, taps, raw, heads, skip_row, dy, state, local, decay, cum, size, act, count, carry=None, identity=None):
     length = proj.shape[1]
+    relay = Along(-1, count * NB, (NSTATE, BLK), bf16)
+    border = Along(-1, SLOTS * (NB + 1), (8, BLK), f32)
+    of = lambda s: SLOTS - 1 - s
+    known = lambda s: jnp.minimum(of(s), count - 1)
     inside = lambda b: jnp.minimum(b, NB - 1)
-    upto = lambda b: jnp.minimum(b, NB)
     return launch(
-        unmix_kernel,
+        functools.partial(unmix_kernel, relay, border, carry is None, count),
         "unmix",
-        (SLOTS, NB + 2),
-        [
-            pl.BlockSpec((1, length, BLK), lambda s, b: (s, 0, inside(b))),
-            pl.BlockSpec((1, 8, BLK), lambda s, b: (s, 0, inside(b))),
+        (SLOTS, NB + 1),
+        [
+            pl.BlockSpec((1, length, BLK), lambda s, b: (of(s), 0, inside(b))),
+            pl.BlockSpec((1, 8, BLK), lambda s, b: (of(s), 0, inside(b))),
             pl.BlockSpec((8, BLK), lambda s, b: (0, inside(b))),
-            pl.BlockSpec((1, length, BLK), lambda s, b: (s, 0, NB)),
-            pl.BlockSpec((1, 8, BLK), lambda s, b: (s, 0, NB)),
-            pl.BlockSpec((8, BLK), lambda s, b: (0, NB)),
-            pl.BlockSpec((1, length, LANES), lambda s, b: (s, 0, 0)),
+            pl.BlockSpec((1, length, MAPS), lambda s, b: (of(s), 0, INNER // MAPS)),
+            pl.BlockSpec((1, 8, MAPS), lambda s, b: (of(s), 0, INNER // MAPS)),
+            pl.BlockSpec((8, MAPS), lambda s, b: (0, INNER // MAPS)),
+            pl.BlockSpec((1, length, LANES), lambda s, b: (of(s), 0, 0)),
             pl.BlockSpec((8, LANES), lambda s, b: (0, 0)),
             pl.BlockSpec((1, BLK), lambda s, b: (0, inside(b))),
-            pl.BlockSpec((1, length, BLK), lambda s, b: (s, 0, inside(b))),
-            pl.BlockSpec((1, 1, NSTATE, BLK), lambda s, b: (s, inside(b) // PARTS, 0, inside(b) % PARTS)),
-            pl.BlockSpec((1, 1, NSTATE, BLK), lambda s, b: (s, inside(b) // PARTS, 0, inside(b) % PARTS)),
-            pl.BlockSpec((1, length, LANES), lambda s, b: (s, 0, 0)),
-            pl.BlockSpec((1, length, LANES), lambda s, b: (s, 0, 0)),
-            pl.BlockSpec((1, length, BLK), lambda s, b: (s, 0, 0)),
-        ],
-        [
-            pl.BlockSpec((1, length, BLK), lambda s, b: (s, 0, b)),
-            pl.BlockSpec((1, 8, BLK), lambda s, b: (s, 0, upto(b))),
-            pl.BlockSpec((1, 8, BLK), lambda s, b: (s, 0, upto(b))),
-            pl.BlockSpec((1, 8, LANES), lambda s, b: (s, 0, 0)),
+            pl.BlockSpec((1, length, BLK), lambda s, b: (of(s), 0, inside(b))),
+            pl.BlockSpec((1, 1, NSTATE, BLK), lambda s, b: (known(s), inside(b), 0, 0)),
+            pl.BlockSpec((count, NB, NSTATE, BLK), lambda s, b: (0, 0, 0, 0)),
+            pl.BlockSpec((SLOTS, NB, 8, BLK), lambda s, b: (0, 0, 0, 0)),
+            pl.BlockSpec((1, length, LANES), lambda s, b: (of(s), 0, 0)),
+            pl.BlockSpec((1, length, LANES), lambda s, b: (of(s), 0, 0)),
+            pl.BlockSpec((1, length, MAPS), lambda s, b: (of(s), 0, 0)),
+        ],
+        [
+            pl.BlockSpec((1, length, BLK), lambda s, b: (of(s), 0, b)),
+            pl.BlockSpec((SLOTS, 8, TAIL), lambda s, b: (0, 0, 0)),
+            pl.BlockSpec((1, 8, BLK), lambda s, b: (of(s), 0, b)),
+            pl.BlockSpec((1, 8, LANES), lambda s, b: (of(s), 0, 0)),
         ],
         [
             jax.ShapeDtypeStruct((SLOTS, length, TAIL), bf16),
-            jax.ShapeDtypeStruct((SLOTS, 8, CONVCH), f32),
-            jax.ShapeDtypeStruct((SLOTS, 8, CONVCH), f32),
+            jax.ShapeDtypeStruct((SLOTS, 8, TAIL), f32),
+            jax.ShapeDtypeStruct((SLOTS, 8, TAIL), f32),
             jax.ShapeDtypeStruct((SLOTS, 8, LANES), f32),
         ],
-        (proj, edge, taps, proj, edge, taps, raw, heads, skip_row, dy, state, later, cum, size, act),
+        (proj, edge, taps, proj, edge, taps, raw, heads, skip_row, dy, state, local, decay, cum, size, act),
         scratch=[
             pltpu.VMEM((length + 8, BLK), f32),
+            pltpu.VMEM((length + 8, MAPS), f32),
             pltpu.VMEM((length, length), f32),
             pltpu.VMEM((length, length), f32),
-            pltpu.VMEM((LANES, length), f32),
+            pltpu.VMEM((16 * HEADS, length), bf16),
+            pltpu.VMEM((16 * HEADS, length), bf16),
+            pltpu.VMEM((6 * length, LANES), bf16),
             pltpu.VMEM((length + 16, BLK), f32),
+            pltpu.VMEM((length + 16, MAPS), f32),
             pltpu.VMEM((length, 2 * NSTATE), f32),
             pltpu.VMEM((length, LANES), f32),
             pltpu.VMEM((length, LANES), f32),
             pltpu.VMEM((LANES, length), f32),
             pltpu.VMEM((8, LANES), f32),
-        ],
+        ]
+        + relay.scratch
+        + border.scratch,
         cost=(2 * 10**10, 2 * 10**7, 10**7),
         carry=carry,
         identity=identity,
+        relay=True,
     )
 
 
@@ -1206,105 +1451,6 @@
         compiler_params=params(collective_id=identity, has_side_effects=True),
     )(*exchange.args)
     return exchange.results(found)
-
-
-def chain_kernel(steps, last, alone, local_ref, decay_ref, state_ref, landed, send_ref, send_sems, recv_sems):
-    dp, me = lax.axis_index("dp"), lax.axis_index("seq")
-    number = pl.program_id(0)
-    total = landed.shape[0]
-    receives = me > 0 if steps > 0 else me < last
-    sends = me < last if steps > 0 else me > 0
-
-    def make(part):
-        return pltpu.make_async_remote_copy(
-            src_ref=send_ref.at[part],
-            dst_ref=landed.at[part],
-            send_sem=send_sems.at[part],
-            recv_sem=recv_sems.at[part],
-            device_id=(dp, me + steps),
-            device_id_type=MESH,
-        )
-
-    if alone:
-        @pl.when(number == 0)
-        def _():
-            chain_greet(steps, last, pltpu.get_barrier_semaphore())
-
-    @pl.when(jnp.logical_and(number < total, receives))
-    def _():
-        make(number).wait_recv()
-        state_ref[0] = landed[number]
-
-    @pl.when(jnp.logical_and(number < total, jnp.logical_not(receives)))
-    def _():
-        state_ref[0] = jnp.zeros(state_ref.shape[1:], bf16)
-
-    @pl.when(jnp.logical_and(number < total, sends))
-    def _():
-        decay = decay_ref[0, 0:1, :]
-        send_ref[number] = (decay * state_ref[0].astype(f32) + local_ref[0]).astype(bf16)
-        make(number).start()
-
-    @pl.when(jnp.logical_and(number == total, sends))
-    def _():
-        for part in range(total):
-            make(part).wait_send()
-
-
-def chain_greet(steps, last, barrier):
-    dp, me = lax.axis_index("dp"), lax.axis_index("seq")
-    receives = me > 0 if steps > 0 else me < last
-    sends = me < last if steps > 0 else me > 0
-
-    @pl.when(receives)
-    def _():
-        pl.semaphore_signal(barrier, inc=1, device_id=(dp, me - steps), device_id_type=MESH)
-
-    @pl.when(sends)
-    def _():
-        pl.semaphore_wait(barrier, 1)
-
-
-def chained(local, decay, slots, steps, identity, carry=None):
-    pieces = INNER // CHAIN
-    total = slots * pieces
-    last = lax.axis_size("seq") - 1
-    piece = lambda n: jnp.minimum(n, total - 1)
-    return launch(
-        functools.partial(chain_kernel, steps, last, carry is None),
-        "chain",
-        (total + 1,),
-        [
-            pl.BlockSpec((1, NSTATE, CHAIN), lambda n: (piece(n) // pieces, 0, piece(n) % pieces)),
-            pl.BlockSpec((1, 8, CHAIN), lambda n: (piece(n) // pieces, 0, piece(n) % pieces)),
-        ],
-        [pl.BlockSpec((1, NSTATE, CHAIN), lambda n: (piece(n), 0, 0))],
-        [jax.ShapeDtypeStruct((total, NSTATE, CHAIN), bf16)],
-        (local, decay),
-        scratch=[
-            pltpu.VMEM((total, NSTATE, CHAIN), bf16),
-            pltpu.VMEM((total, NSTATE, CHAIN), bf16),
-            pltpu.SemaphoreType.DMA((total,)),
-            pltpu.SemaphoreType.DMA((total,)),
-        ],
-        carry=carry,
-        identity=identity,
-        along=True,
-        remote=True,
-    )
-
-
-def passed_along(value, steps):
-    count = lax.axis_size("seq")
-    initial, last = (max(0, -steps), min(count, count - steps))
-    return lax.ppermute(value, "seq", [(source, source + steps) for source in range(initial, last)])
-
-
-def all_slots(state):
-    missing = SLOTS - state.shape[0]
-    if missing:
-        state = jnp.concatenate([state, jnp.zeros((missing,) + state.shape[1:], state.dtype)], axis=0)
-    return state
 
 
 def spaced(first, last, weights):
@@ -1411,7 +1557,7 @@
     for layer in range(LAYERS):
         gain_row = norm_all[layer].reshape(1, D)
         gate_row = gate_all[layer].reshape(1, INNER)
-        taps = padded_rows(conv_all[layer], 8)
+        taps = jnp.pad(conv_all[layer], ((0, 8 - CONV), (0, TAIL - CONVCH)))
         heads = padded_rows(
             jnp.pad(
                 jnp.stack([dt_bias[layer], a_log[layer]]), ((0, 0), (0, LANES - HEADS))
@@ -1421,19 +1567,20 @@
         skip_row = jnp.repeat(d_skip[layer], HEADDIM).reshape(1, INNER)
         base = 1 + 3 * layer
         more = tail_done[layer + 1] if layer + 1 < LAYERS else out_done[layer]
-        marks = spaced(tail_done[layer], out_done[layer], (1, 3, 2)) + spaced(out_done[layer], more, (1, 2))
-        proj, raw, normed, *_ = project(h, gain_row, whole(base), run(marks[0]), next(ids))
+        marks = spaced(tail_done[layer], more, (16, 30, 11, 30) if layer + 1 < LAYERS else (18, 30, 11, 0))
+        marks[1] = max(marks[1], gate_done[layer])
+        marks[2] = max(marks[2], out_done[layer])
+        proj, raw, normed, edge, *_ = project(h, gain_row, whole(base), run(marks[0]), next(ids))
         cube = proj.reshape(SLOTS, length, TAIL)
         raw = raw.reshape(SLOTS, length, LANES)
-        edge = passed_along(cube[:, length - (CONV - 1) :, :CONVCH], 1)
-        edge = jnp.pad(edge, ((0, 0), (8 - (CONV - 1), 0), (0, 0)))
-        y, local, cum, size, act, decay, *_ = mix(cube, edge, taps, raw, heads, skip_row, run(marks[1]), next(ids))
-        state, *_ = chained(local, decay, count, 1, next(ids), run(marks[2]))
-        state = state.reshape(count, -1, NSTATE, CHAIN)
-        gate, *_ = project_gate(normed, whole(base + 1), run(marks[3]), next(ids))
+        y, state, cum, size, act, decay, *_ = mix(
+            cube, edge, taps, raw, heads, skip_row, count, run(marks[1]), next(ids)
+        )
+        state = state.reshape(count, NB, NSTATE, BLK)
+        gate, *_ = project_gate(normed, whole(base + 1), run(marks[2]), next(ids))
         flat = lambda array: array.reshape(rows, -1)
         h_next, mixture, inverse, *_ = branch(
-            flat(y), gate, flat(act), flat(cum), state, gate_row, whole(base + 2), h, valid, run(marks[4]), next(ids)
+            flat(y), gate, flat(act), flat(cum), state, gate_row, whole(base + 2), h, valid, run(marks[3]), next(ids)
         )
         kept.append(
             (h, gain_row, gate_row, taps, heads, skip_row, proj, gate, raw, normed, edge, cum, size, act,
@@ -1452,7 +1599,7 @@
     def summing(arrays):
         if not ours or arrays[0] is None:
             return None
-        return Reduce([cut(array) for array in arrays], [(3, 2)] * len(arrays))
+        return Reduce([cut(array) for array in arrays], [(3, 4)] * len(arrays), 2)
 
     for layer in reversed(range(LAYERS)):
         (h, gain_row, gate_row, taps, heads, skip_row, proj, gate, raw, normed, edge, cum, size, act,
@@ -1467,20 +1614,16 @@
             totals[layer + 1][0] = sums[0][0]
         dy, grads, local = ungate(back, mixture, gate, inverse, mean, gate_row, flat(act), flat(cum), count)
         back, partial_gate = unproject_gate(grads, weight_gate, normed)
-        later, *_ = chained(local, decay, count, -1, next(ids))
-        later = later.reshape(count, -1, NSTATE, CHAIN)
-        grads, edge_grad, grad_taps, grad_heads, *sums = unmix(
-            cube, edge, taps, raw, heads, skip_row, shaped(dy), all_slots(state), all_slots(later),
-            cum, size, act, summing([partial_gate, partial_out]), next(ids),
+        grads, late, grad_taps, grad_heads, *sums = unmix(
+            cube, edge, taps, raw, heads, skip_row, shaped(dy), state, local, decay, cum, size, act, count,
+            summing([partial_gate, partial_out]), next(ids),
         )
         if ours:
             totals[layer][1], totals[layer][2] = sums[0]
-        late = passed_along(edge_grad[:, 8 - (CONV - 1) :].astype(bf16), -1).astype(f32)
-        late = jnp.pad(late, ((0, 0), (8 - (CONV - 1), 0), (0, TAIL - CONVCH)))
         g, grad_norm, waiting = unproject(flat(grads), late, weight_tail, normed, h, g, gain_row, back)
         partials[layer] = (waiting, partial_gate, partial_out)
         small[layer] = (
-            grad_norm[0], jnp.sum(grad_taps, axis=0)[:CONV], grad_gate[0],
+            grad_norm[0], jnp.sum(grad_taps, axis=0)[:CONV, :CONVCH], grad_gate[0],
             jnp.sum(grad_heads, axis=0)[:3, :HEADS],
         )
     grad_hidden = ordered(g.reshape(SLOTS, length, D))

time: 1140 us -> 945 us (0.83); the launches traced: 1120 us -> 942 us
  Pallas kernels: 1050 us -> 890 us
  local copies, waits for them, and re-layouts: 44.7 us -> 32.2 us
    pallas_call x11 -> x8, Pallas kernels: 255 us -> 158 us  [launch(): pl.pallas_call(kernel, name=name, grid=grid, in_specs=in_specs, out_specs...]
    pallas_call x11 -> x10, Pallas kernels: 591 us -> 532 us  [launch(): pl.pallas_call(wrapped, name=name, grid=grid, in_specs=list(in_specs) + c...]
  transfers between devices with their start and end apart: 4 -> 0, of which waited for: 1 -> 0; matrix products, arithmetic and copies ran while one was open for 2% -> 0% of each run, Pallas kernels for 0% -> 0%
where the time goes in v3:
time: 945 us; the launch traced here: 942 us
  Pallas kernels  890 us (94%)
  local copies, waits for them, and re-layouts  32.2 us (3%)
  other arithmetic  17.5 us (2%)
    pallas_call x10, Pallas kernels, launch(): pl.pallas_call(wrapped, name=name, grid=grid, in_specs=list(in_specs) + c...  532 us
    pallas_call x2, Pallas kernels, alone(): pl.pallas_call(kernel, name=name, grid=(1,), in_specs=exchange.in_specs,...  200 us
    pallas_call x8, Pallas kernels, launch(): pl.pallas_call(kernel, name=name, grid=grid, in_specs=in_specs, out_specs...  158 us

profile of v3, /device:TPU:0, one launch (start us, length us, event | category | flops | bytes accessed | tf_op | source)
XLA Modules:
  0.0 941.8 jit_solution(17008630112109876960)
XLA Ops:
  0.7 0.9 rev.16
  1.6 0.8 fusion.5
  2.3 0.8 fusion.6
  3.1 0.8 slice_bitcast_fusion.6
  3.9 1.3 fusion.7
  6.5 0.7 broadcast_select_fusion
  7.2 0.8 reshape.193
  8.0 0.8 pad_maximum_fusion.5
  8.8 0.6 pad_bitcast_fusion.1.refs_0_
  9.4 0.6 pad.41.refs_7_
  10.0 0.6 pad.44.refs_7_
  10.7 0.7 reshape_reshape.32.refs_8_
  11.4 0.7 reshape_reshape.31.refs_8_
  12.1 0.8 broadcast_in_dim.14.refs_8_.valid_ref.refs_1_
  13.0 1.9 slice_bitcast_fusion
  14.9 1.9 slice_bitcast_fusion.1
  16.8 0.9 fusion.1
  17.7 2.0 reverse_select_fusion.1
  19.7 1.1 copy-done.1
  20.7 1.9 reverse_select_fusion.3
  22.6 127.3 %gather.1 = (bf16[2,2,2,4,16,128]{5,4,3,2,1,0:T(8,128)(2,1)}, bf16[2,2,2,4,48,3584]{5,4,3,2,1,0:T(8,128)(2,1)}, bf16[2,2,2,4,48,3072]{5,4,3,2,1,0:T(8,128)(2,1)}, bf16[2,2,2,4,96,1536]{5,4,3,2,1,0:T(8,128)(2,1)}) custom-call(bf16[16,128]{1,0:T(8,128)(2,1)} %pad_bitcast_fusion.1.refs_0_, bf16[48,3584]{1,0:T(8,128)(2,1)} %get-tuple-element.193.refs_1_, ...), custom_call_target="tpu_custom_call" | custom-call | tf_op jit(solution)/shard_map/gather/pallas_call | solution.py:1442
  149.9 0.9 copy.53
  151.2 0.7 slice.172.gain_ref
  151.9 0.7 slice.163.refs_5_.gain_ref
  152.6 0.2 slice.193
  153.1 0.7 slice.166.refs_1_.gain_ref
  153.9 0.7 slice.154.refs_1_.gain_ref
  154.7 0.6 pad.39.refs_2_.refs_5_
  155.3 0.6 pad.42.refs_2_.refs_5_
  155.9 20.4 %project.2 = (f32[512,3584]{1,0:T(8,128)}, f32[512,128]{1,0:T(8,128)}, bf16[512,1536]{1,0:T(8,128)(2,1)}, f32[2,8,3584]{2,1,0:T(8,128)}, bf16[2,2,2,4,48,3072]{5...) custom-call(f32[512,1536]{1,0:T(8,128)} %bitcast.111, ...), custom_call_target="tpu_custom_call", output_to_operand_aliasing={{4}: (4, {}), {5}: (5, {})} | custom-call | flops 5637144576 | bytes 11010048 | tf_op jit(solution)/shard_map/project/pallas_call | solution.py:78
  176.4 49.1 %mix.2 = (f32[2,256,3072]{2,1,0:T(8,128)}, bf16[6,128,512]{2,1,0:T(8,128)(2,1)}, f32[2,256,128]{2,1,0:T(8,128)}, f32[2,256,128]{2,1,0:T(8,128)}, f32[2,256,256]{...) custom-call(f32[2,256,3584]{2,1,0:T(8,128)} %bitcast.103, ...), custom_call_target="tpu_custom_call", output_to_operand_aliasing={{6}: (10, {}), {7}: (11, {})} | custom-call | flops 6000000000 | bytes 10000000 | tf_op jit(solution)/shard_map/mix/pallas_call | solution.py:78
  225.5 43.7 %project_gate.2 = (f32[512,3072]{1,0:T(8,128)}, bf16[2,2,2,4,96,1536]{5,4,3,2,1,0:T(8,128)(2,1)}, bf16[2,2,2,4,48,3584]{5,4,3,2,1,0:T(8,128)(2,1)}, bf16[2,2,2,4,48,3072]{5,4,3,2,1,0:T(8,128)(2,1)}) custom-call(bf16[512,1536]{1,0:T(8,128)(2,1)} %get-tuple-element.108.refs_0_.normed_ref, ...), custom_call_target="tpu_custom_call", output_to_operand_aliasing={{1}: (3, {}), {2}: (4, {})} | custom-call | flops 4831838208 | bytes 9437184 | tf_op jit(solution)/shard_map/project_gate/pallas_call | solution.py:78
  269.3 50.4 %branch.2 = (f32[512,1536]{1,0:T(8,128)}, f32[512,3072]{1,0:T(8,128)}, f32[512,128]{1,0:T(8,128)}, bf16[2,2,2,4,48,3584]{5,4,3,2,1,0:T(8,128)(2,1)}, bf16[2,2,2,...) custom-call(f32[512,3072]{1,0:T(8,128)} %bitcast.119, ...), custom_call_target="tpu_custom_call", output_to_operand_aliasing={{3}: (11, {}), {4}: (12, {})} | custom-call | flops 4831838208 | bytes 9437184 | tf_op jit(solution)/shard_map/branch/pallas_call | solution.py:78
  319.7 26.6 %project.3 = (f32[512,3584]{1,0:T(8,128)}, f32[512,128]{1,0:T(8,128)}, bf16[512,1536]{1,0:T(8,128)(2,1)}, f32[2,8,3584]{2,1,0:T(8,128)}, bf16[2,2,2,4,48,3072]{5...) custom-call(f32[512,1536]{1,0:T(8,128)} %get-tuple-element.119.refs_0_.h, ...), custom_call_target="tpu_custom_call", output_to_operand_aliasing={{4}: (4, {}), {5}: (5, {})} | custom-call | flops 5637144576 | bytes 11010048 | tf_op jit(solution)/shard_map/project/pallas_call | solution.py:78
  346.3 42.8 %mix.3 = (f32[2,256,3072]{2,1,0:T(8,128)}, bf16[6,128,512]{2,1,0:T(8,128)(2,1)}, f32[2,256,128]{2,1,0:T(8,128)}, f32[2,256,128]{2,1,0:T(8,128)}, f32[2,256,256]{...) custom-call(f32[2,256,3584]{2,1,0:T(8,128)} %bitcast.107, ...), custom_call_target="tpu_custom_call", output_to_operand_aliasing={{6}: (9, {}), {7}: (10, {})} | custom-call | flops 6000000000 | bytes 10000000 | tf_op jit(solution)/shard_map/mix/pallas_call | solution.py:78
  389.1 11.6 %project_gate.3 = (f32[512,3072]{1,0:T(8,128)}, bf16[2,2,2,4,96,1536]{5,4,3,2,1,0:T(8,128)(2,1)}) custom-call(bf16[512,1536]{1,0:T(8,128)(2,1)} %get-tuple-element.129.refs_0_.normed_ref, bf16[1536,3072]{1,0:T(8,128)(2,1)} %bitcast.97, bf16[2,2,2,4,96,1536]{5,4,3,2,1,0:T(8,128)(2,1)} %get-tuple-element.131.refs_2_), custom_call_target="tpu_custom_call", output_to_operand_aliasing={{1}: (2, {})} | custom-call | flops 4831838208 | bytes 9437184 | tf_op jit(solution)/shard_map/project_gate/pallas_call | solution.py:78
  400.7 20.2 %branch.3 = (f32[512,1536]{1,0:T(8,128)}, f32[512,3072]{1,0:T(8,128)}, f32[512,128]{1,0:T(8,128)}) custom-call(f32[512,3072]{1,0:T(8,128)} %bitcast.118, f32[512,3072]{1,0:T(8,128)} %get-tuple-element.132.gate_ref, f32[512,256]{1,0:T(8,128)} %bitcast.124, f32[512,128]{1,0:T(8,128)} %bitcast.130, bf16[1,6,128,512]{3,2,1,0:T(8,128)(2,1)} %bitcast.136, ...), custom_call_target="tpu_custom_call" | custom-call | flops 4831838208 | bytes 9437184 | tf_op jit(solution)/shard_map/branch/pallas_call | solution.py:46
  420.9 23.1 %unbranch.2 = (f32[512,3072]{1,0:T(8,128)}, f32[512,128]{1,0:T(8,128)}, f32[8,3072]{1,0:T(8,128)}, bf16[3072,1536]{1,0:T(8,128)(2,1)}) custom-call(f32[512,1536]{1,0:T(8,128)} %bitcast.120, f32[512,128]{1,0:T(8,128)} %broadcast_in_dim.14.refs_8_.valid_ref.refs_1_, f32[512,3072]{1,0:T(8,128)} %get-tuple-element.138.mixture_ref, ...), custom_call_target="tpu_custom_call" | custom-call | flops 9663676416 | bytes 18874368 | tf_op jit(solution)/shard_map/unbranch/pallas_call | solution.py:46
  444.0 14.1 %ungate.2 = (f32[512,3072]{1,0:T(8,128)}, bf16[512,3072]{1,0:T(8,128)(2,1)}, f32[1,6,128,512]{3,2,1,0:T(8,128)}) custom-call(f32[512,3072]{1,0:T(8,128)} %get-tuple-element.140.back_ref, f32[512,3072]{1,0:T(8,128)} %get-tuple-element.138.mixture_ref, f32[512,3072]{1,0:T(8,128)} %get-tuple-element.132.gate_ref, f32[512,128]{1,0:T(8,128)} %get-tuple-element.139.inverse_ref, ...), custom_call_target="tpu_custom_call" | custom-call | flops 1000000000 | bytes 20000000 | tf_op jit(solution)/shard_map/ungate/pallas_call | solution.py:46
  458.1 0.9 slice.178
  459.0 17.5 %unproject_gate.2 = (f32[512,1536]{1,0:T(8,128)}, bf16[1536,3072]{1,0:T(8,128)(2,1)}) custom-call(bf16[512,3072]{1,0:T(8,128)(2,1)} %get-tuple-element.146.grads_ref, bf16[1536,3072]{1,0:T(8,128)(2,1)} %bitcast.98, bf16[512,1536]{1,0:T(8,128)(2,1)} %get-tuple-element.129.refs_0_.normed_ref), custom_call_target="tpu_custom_call" | custom-call | flops 9663676416 | bytes 18874368 | tf_op jit(solution)/shard_map/unproject_gate/pallas_call | solution.py:46
  476.5 109.2 %unmix.2 = (bf16[2,256,3584]{2,1,0:T(8,128)(2,1)}, f32[2,8,3584]{2,1,0:T(8,128)}, f32[2,8,3584]{2,1,0:T(8,128)}, f32[2,8,128]{2,1,0:T(8,128)}, f32[48,3072]{1,0:T(8,128)}, /*index=5*/f32[96,1536]{1,0:T(8,128)}) custom-call(f32[2,256,3584]{2,1,0:T(8,128)} %bitcast.109, f32[2,8,3584]{2,1,0:T(8,128)} %get-tuple-element.124.refs_1_.refs_4_, ...), custom_call_target="tpu_custom_call" | custom-call | flops 20000000000 | bytes 20000000 | tf_op jit(solution)/shard_map/unmix/pallas_call | solution.py:78
  585.7 25.4 %unproject.2 = (f32[512,1536]{1,0:T(8,128)}, f32[8,1536]{1,0:T(8,128)}, bf16[1536,3584]{1,0:T(8,128)(2,1)}) custom-call(bf16[512,3584]{1,0:T(8,128)(2,1)} %bitcast.161, f32[2,8,3584]{2,1,0:T(8,128)} %get-tuple-element.150.late_ref, bf16[1536,3584]{1,0:T(8,128)(2,1)} %bitcast.100, bf16[512,1536]{1,0:T(8,128)(2,1)} %get-tuple-element.129.refs_0_.normed_ref, ...), custom_call_target="tpu_custom_call" | custom-call | flops 11274289152 | bytes 22020096 | tf_op jit(solution)/shard_map/unproject/pallas_call | solution.py:46
  611.1 70.3 %unbranch.3 = (f32[512,3072]{1,0:T(8,128)}, f32[512,128]{1,0:T(8,128)}, f32[8,3072]{1,0:T(8,128)}, bf16[3072,1536]{1,0:T(8,128)(2,1)}, f32[48,3584]{1,0:T(8,128)}) custom-call(f32[512,1536]{1,0:T(8,128)} %get-tuple-element.152.refs_0_.g_ref, f32[512,128]{1,0:T(8,128)} %broadcast_in_dim.14.refs_8_.valid_ref.refs_1_, ...), custom_call_target="tpu_custom_call" | custom-call | flops 9663676416 | bytes 18874368 | tf_op jit(solution)/shard_map/unbranch/pallas_call | solution.py:78
  681.5 14.2 %ungate.3 = (f32[512,3072]{1,0:T(8,128)}, bf16[512,3072]{1,0:T(8,128)(2,1)}, f32[1,6,128,512]{3,2,1,0:T(8,128)}) custom-call(f32[512,3072]{1,0:T(8,128)} %get-tuple-element.156.back_ref, f32[512,3072]{1,0:T(8,128)} %get-tuple-element.153.refs_2_.mixture_ref, f32[512,3072]{1,0:T(8,128)} %get-tuple-element.112.refs_1_.refs_3_.gate_ref, ...), custom_call_target="tpu_custom_call" | custom-call | flops 1000000000 | bytes 20000000 | tf_op jit(solution)/shard_map/ungate/pallas_call | solution.py:46
  695.7 0.8 slice.174
  696.5 0.9 slice.177
  697.9 17.5 %unproject_gate.3 = (f32[512,1536]{1,0:T(8,128)}, bf16[1536,3072]{1,0:T(8,128)(2,1)}) custom-call(bf16[512,3072]{1,0:T(8,128)(2,1)} %get-tuple-element.162.grads_ref, bf16[1536,3072]{1,0:T(8,128)(2,1)} %bitcast.102, bf16[512,1536]{1,0:T(8,128)(2,1)} %get-tuple-element.108.refs_0_.normed_ref), custom_call_target="tpu_custom_call" | custom-call | flops 9663676416 | bytes 18874368 | tf_op jit(solution)/shard_map/unproject_gate/pallas_call | solution.py:46
  715.3 107.4 %unmix.3 = (bf16[2,256,3584]{2,1,0:T(8,128)(2,1)}, f32[2,8,3584]{2,1,0:T(8,128)}, f32[2,8,3584]{2,1,0:T(8,128)}, f32[2,8,128]{2,1,0:T(8,128)}, f32[48,3072]{1,0:T(8,128)}, /*index=5*/f32[96,1536]{1,0:T(8,128)}) custom-call(f32[2,256,3584]{2,1,0:T(8,128)} %bitcast.105, f32[2,8,3584]{2,1,0:T(8,128)} %get-tuple-element.103.refs_1_.refs_4_, ...), custom_call_target="tpu_custom_call" | custom-call | flops 20000000000 | bytes 20000000 | tf_op jit(solution)/shard_map/unmix/pallas_call | solution.py:78
  822.7 25.6 %unproject.3 = (f32[512,1536]{1,0:T(8,128)}, f32[8,1536]{1,0:T(8,128)}, bf16[1536,3584]{1,0:T(8,128)(2,1)}) custom-call(bf16[512,3584]{1,0:T(8,128)(2,1)} %bitcast.162, f32[2,8,3584]{2,1,0:T(8,128)} %get-tuple-element.166.late_ref, bf16[1536,3584]{1,0:T(8,128)(2,1)} %bitcast.116, bf16[512,1536]{1,0:T(8,128)(2,1)} %get-tuple-element.108.refs_0_.normed_ref, ...), custom_call_target="tpu_custom_call" | custom-call | flops 11274289152 | bytes 22020096 | tf_op jit(solution)/shard_map/unproject/pallas_call | solution.py:46
  848.3 9.0 reverse_select_fusion
  857.3 0.6 pad.46.refs_2_
  857.9 0.8 slice.173
  859.6 0.8 copy.50
  860.4 73.1 %reduce.17 = (f32[48,3584]{1,0:T(8,128)}, f32[16,128]{1,0:T(8,128)}, f32[8,128]{1,0:T(8,128)}) custom-call(bf16[2,2,2,4,48,3584]{5,4,3,2,1,0:T(8,128)(2,1)} %bitcast.114, f32[2,2,2,4,16,128]{5,4,3,2,1,0:T(8,128)} %bitcast.132, f32[8,128]{1,0:T(8,128)} %pad.46.refs_2_), custom_call_target="tpu_custom_call" | custom-call | tf_op jit(solution)/shard_map/reduce/pallas_call | solution.py:1442
  933.6 0.8 reshape.228
  934.4 0.6 slice.204
  935.0 0.6 slice.202
  935.7 0.7 reshape.229
  936.3 0.7 reshape.230
  937.0 0.6 fusion.4
  937.6 1.1 pad_maximum_fusion.1
  938.7 1.1 slice.183
  939.9 1.6 pad_maximum_fusion
  (66 shorter events, 2.7 us)
Async XLA Ops:
  0.6 17.0 %copy-start = (f32[2,256,1536]{2,1,0:T(8,128)S(1)}, f32[2,256,1536]{2,1,0:T(8,128)}, u32[]{:S(2)}) copy-start(f32[2,256,1536]{2,1,0:T(8,128)} %param.12) | copy-start | bytes 9437188
  12.1 4.7 slice-start
  17.7 3.0 copy-start.1
  681.5 14.2 %copy-start.9 = (f32[2,8,128]{2,1,0:T(8,128)S(1)}, f32[2,8,128]{2,1,0:T(8,128)}, u32[]{:S(2)}) copy-start(f32[2,8,128]{2,1,0:T(8,128)} %get-tuple-element.177) | copy-start | bytes 24580
  681.5 16.1 %copy-start.7 = (f32[2,8,3584]{2,1,0:T(8,128)S(1)}, f32[2,8,3584]{2,1,0:T(8,128)}, u32[]{:S(2)}) copy-start(f32[2,8,3584]{2,1,0:T(8,128)} %get-tuple-element.173) | copy-start | bytes 688132
  681.5 16.2 %copy-start.2 = (f32[48,3584]{1,0:T(8,128)S(1)}, f32[48,3584]{1,0:T(8,128)}, u32[]{:S(2)}) copy-start(f32[48,3584]{1,0:T(8,128)} %get-tuple-element.182) | copy-start | bytes 2064388
  681.5 16.3 %copy-start.4 = (f32[48,3072]{1,0:T(8,128)S(1)}, f32[48,3072]{1,0:T(8,128)}, u32[]{:S(2)}) copy-start(f32[48,3072]{1,0:T(8,128)} %get-tuple-element.181) | copy-start | bytes 1769476
  848.3 9.0 copy-start.10
  848.3 9.6 %copy-start.8 = (f32[2,8,3584]{2,1,0:T(8,128)S(1)}, f32[2,8,3584]{2,1,0:T(8,128)}, u32[]{:S(2)}) copy-start(f32[2,8,3584]{2,1,0:T(8,128)} %get-tuple-element.172) | copy-start | bytes 688132
  860.4 77.2 %copy-start.5 = (f32[96,1536]{1,0:T(8,128)S(1)}, f32[96,1536]{1,0:T(8,128)}, u32[]{:S(2)}) copy-start(f32[96,1536]{1,0:T(8,128)} %get-tuple-element.184) | copy-start | bytes 1769476
  860.4 77.2 %copy-start.6 = (f32[96,1536]{1,0:T(8,128)S(1)}, f32[96,1536]{1,0:T(8,128)}, u32[]{:S(2)}) copy-start(f32[96,1536]{1,0:T(8,128)} %get-tuple-element.183) | copy-start | bytes 1769476
  933.5 6.3 copy-start.3

commit v4 on v3

--- a/solution.py
+++ b/solution.py
@@ -30,7 +30,7 @@
 f32 = jnp.float32
 bf16 = jnp.bfloat16
 epsilon = 1e-05
-VMEM_LIMIT = 58 << 20
+VMEM_LIMIT = 60 << 20
 
 
 def launch(
@@ -593,143 +593,137 @@
     )
 
 
-def unbranch_kernel(
-    g_ref, valid_ref, mixture_ref, gate_ref, inverse_ref, gain_ref, w_ref,
-    back_ref, mean_ref, gain_out_ref, w_out_ref,
-    low, norm_low,
+def turn_kernel(
+    g_ref, valid_ref, mixture_ref, gate_ref, inverse_ref, gain_ref, w_ref, act_ref, cum_ref, normed_ref, w_gate_ref,
+    gain_out_ref, w_out_ref, dy_ref, state_ref, back_ref, w_gate_out_ref,
+    low, norm_low, held, mean, output_t, turned,
 ):
-    block = pl.program_id(0)
+    step = pl.program_id(0)
     rows = g_ref.shape[0]
-
-    @pl.when(block == 0)
+    length = rows // SLOTS
+    count = state_ref.shape[0]
+
+    @pl.when(step == 0)
     def _():
         def one(span):
             low[span, :] = (valid_ref[span, 0:1] * g_ref[span, :]).astype(bf16)
 
         for_rows(rows, 32, one)
-        mean_ref[...] = jnp.zeros_like(mean_ref)
-
-    back_ref[...] = dot_nt(low[...], w_ref[...])
-    gain_out_ref[...] = jnp.zeros_like(gain_out_ref)
-
-    def one(span):
-        gate = gate_ref[span, :]
-        gated = mixture_ref[span, :] * gate * sigmoid(gate)
-        back = back_ref[span, :]
-        unit = gated * inverse_ref[span, 0:1]
-        norm_low[span, :] = (unit * gain_ref[...]).astype(bf16)
-        gain_out_ref[0:1, :] += jnp.sum(back * unit, axis=0, keepdims=True)
-        product = gated * back * gain_ref[...]
-        mean_ref[span, :] += fold(product)
-
-    for_rows(rows, 128, one)
-    w_out_ref[...] = dot_tn(norm_low[...], low[...]).astype(bf16)
-
-    @pl.when(block == NB - 1)
-    def _():
-        mean_ref[...] = jnp.broadcast_to(
-            jnp.sum(mean_ref[...], axis=-1, keepdims=True) / INNER, mean_ref.shape
-        )
-
-
-def unbranch(g, valid, mixture, gate, inverse, gain_row, weight, carry=None, identity=None):
+        mean[...] = jnp.zeros_like(mean)
+        turned[...] = normed_ref[...].T
+        for slot in range(count):
+            span = slice(slot * length, (slot + 1) * length)
+            output_t[slot, 0], output_t[slot, 1] = halves(act_ref[span, NSTATE:].T)
+
+    @pl.when(step < NB)
+    def _():
+        held[step] = dot_nt(low[...], w_ref[...])
+        gain_out_ref[...] = jnp.zeros_like(gain_out_ref)
+
+        def one(span):
+            gate = gate_ref[span, :]
+            gated = mixture_ref[span, :] * gate * sigmoid(gate)
+            back = held[step, span, :]
+            unit = gated * inverse_ref[span, 0:1]
+            norm_low[span, :] = (unit * gain_ref[...]).astype(bf16)
+            gain_out_ref[0:1, :] += jnp.sum(back * unit, axis=0, keepdims=True)
+            mean[span, :] += fold(gated * back * gain_ref[...])
+
+        for_rows(rows, 128, one)
+        w_out_ref[...] = dot_tn(norm_low[...], low[...]).astype(bf16)
+
+    @pl.when(step == NB - 1)
+    def _():
+        mean[...] = jnp.broadcast_to(jnp.sum(mean[...], axis=-1, keepdims=True) / INNER, mean.shape)
+
+    @pl.when(jnp.logical_and(step >= NB, step < 2 * NB))
+    def _():
+        block = step - NB
+        for slot in range(SLOTS):
+            span = slice(slot * length, (slot + 1) * length)
+            gate = gate_ref[span, :]
+            curve = sigmoid(gate)
+            mixture = mixture_ref[span, :]
+            swish = gate * curve
+            inverse = inverse_ref[span, 0:1]
+            back = held[block, span, :] * gain_ref[...]
+            pull = inverse * inverse * inverse * mean[span, 0:1]
+            grad = inverse * back - (mixture * swish) * pull
+            dy = grad * swish
+            dy_ref[span, :] = dy
+            held[block, span, :] = grad * mixture * curve * (1.0 + gate * (1.0 - curve))
+            if slot < count:
+                grown = spread(jnp.exp(heads_first(cum_ref[span, :], block)))
+                state_ref[slot, 0] = dot_halves((output_t[slot, 0], output_t[slot, 1]), halves(dy * grown))
+
+    @pl.when(step >= 2 * NB)
+    def _():
+        grads = held[step - 2 * NB].astype(bf16)
+        w_gate_out_ref[...] = dot(turned[...], grads).astype(bf16)
+        product = dot_nt(grads, w_gate_ref[...])
+
+        @pl.when(step == 2 * NB)
+        def _():
+            back_ref[...] = product
+
+        @pl.when(step > 2 * NB)
+        def _():
+            back_ref[...] += product
+
+
+def turn(
+    g, valid, mixture, gate, inverse, gain_row, weight, act, cum, normed, weight_gate, count, carry=None, identity=None
+):
     rows = g.shape[0]
+    length = rows // SLOTS
+    first = lambda n: jnp.minimum(n, NB - 1)
+    second = lambda n: jnp.clip(n - NB, 0, NB - 1)
+    third = lambda n: jnp.maximum(n - 2 * NB, 0)
+    both = lambda n: jnp.where(n < NB, n, second(n))
+    once = dict(pipeline_mode=pl.Buffered(1))
     return launch(
-        unbranch_kernel,
-        "unbranch",
-        (NB,),
-        [
-            pl.BlockSpec((rows, D), lambda b: (0, 0)),
-            pl.BlockSpec((rows, LANES), lambda b: (0, 0)),
-            pl.BlockSpec((rows, BLK), lambda b: (0, b)),
-            pl.BlockSpec((rows, BLK), lambda b: (0, b)),
-            pl.BlockSpec((rows, LANES), lambda b: (0, 0)),
-            pl.BlockSpec((1, BLK), lambda b: (0, b)),
-            pl.BlockSpec((BLK, D), lambda b: (b, 0)),
-        ],
-        [
-            pl.BlockSpec((rows, BLK), lambda b: (0, b)),
-            pl.BlockSpec((rows, LANES), lambda b: (0, 0)),
-            pl.BlockSpec((8, BLK), lambda b: (0, b)),
-            pl.BlockSpec((BLK, D), lambda b: (b, 0)),
-        ],
-        [
-            jax.ShapeDtypeStruct((rows, INNER), f32),
-            jax.ShapeDtypeStruct((rows, LANES), f32),
+        turn_kernel,
+        "turn",
+        (3 * NB,),
+        [
+            pl.BlockSpec((rows, D), lambda n: (0, 0), **once),
+            pl.BlockSpec((rows, LANES), lambda n: (0, 0), **once),
+            pl.BlockSpec((rows, BLK), lambda n: (0, both(n))),
+            pl.BlockSpec((rows, BLK), lambda n: (0, both(n))),
+            pl.BlockSpec((rows, LANES), lambda n: (0, 0), **once),
+            pl.BlockSpec((1, BLK), lambda n: (0, both(n))),
+            pl.BlockSpec((BLK, D), lambda n: (first(n), 0)),
+            pl.BlockSpec((rows, MAPS), lambda n: (0, 0), **once),
+            pl.BlockSpec((rows, LANES), lambda n: (0, 0), **once),
+            pl.BlockSpec((rows, D), lambda n: (0, 0), **once),
+            pl.BlockSpec((D, BLK), lambda n: (0, third(n))),
+        ],
+        [
+            pl.BlockSpec((8, BLK), lambda n: (0, first(n))),
+            pl.BlockSpec((BLK, D), lambda n: (first(n), 0)),
+            pl.BlockSpec((rows, BLK), lambda n: (0, second(n))),
+            pl.BlockSpec((count, 1, NSTATE, BLK), lambda n: (0, second(n), 0, 0)),
+            pl.BlockSpec((rows, D), lambda n: (0, 0)),
+            pl.BlockSpec((D, BLK), lambda n: (0, third(n))),
+        ],
+        [
             jax.ShapeDtypeStruct((8, INNER), f32),
             jax.ShapeDtypeStruct((INNER, D), bf16),
-        ],
-        (g, valid, mixture, gate, inverse, gain_row, weight),
-        scratch=[pltpu.VMEM((rows, D), bf16), pltpu.VMEM((rows, BLK), bf16)],
-        cost=(4 * rows * D * INNER, 4 * D * INNER, 10**6),
-        carry=carry,
-        identity=identity,
-    )
-
-
-def ungate_kernel(
-    back_ref, mixture_ref, gate_ref, inverse_ref, mean_ref, gain_ref, act_ref, cum_ref,
-    dy_ref, dgate_ref, state_ref,
-    output_t,
-):
-    block = pl.program_id(0)
-    rows = back_ref.shape[0]
-    length = rows // SLOTS
-
-    @pl.when(block == 0)
-    def _():
-        for slot in range(state_ref.shape[0]):
-            span = slice(slot * length, (slot + 1) * length)
-            output_t[slot, 0], output_t[slot, 1] = halves(act_ref[span, NSTATE:].T)
-
-    for slot in range(SLOTS):
-        span = slice(slot * length, (slot + 1) * length)
-        gate = gate_ref[span, :]
-        curve = sigmoid(gate)
-        mixture = mixture_ref[span, :]
-        swish = gate * curve
-        inverse = inverse_ref[span, 0:1]
-        back = back_ref[span, :] * gain_ref[...]
-        pull = inverse * inverse * inverse * mean_ref[span, 0:1]
-        grad = inverse * back - (mixture * swish) * pull
-        dy = grad * swish
-        dy_ref[span, :] = dy
-        dgate_ref[span, :] = (grad * mixture * curve * (1.0 + gate * (1.0 - curve))).astype(bf16)
-        if slot < state_ref.shape[0]:
-            grown = spread(jnp.exp(heads_first(cum_ref[span, :], block)))
-            state_ref[slot, 0] = dot_halves((output_t[slot, 0], output_t[slot, 1]), halves(dy * grown))
-
-
-def ungate(back, mixture, gate, inverse, mean, gain_row, act, cum, count, carry=None, identity=None):
-    rows = back.shape[0]
-    length = rows // SLOTS
-    return launch(
-        ungate_kernel,
-        "ungate",
-        (NB,),
-        [
-            pl.BlockSpec((rows, BLK), lambda b: (0, b)),
-            pl.BlockSpec((rows, BLK), lambda b: (0, b)),
-            pl.BlockSpec((rows, BLK), lambda b: (0, b)),
-            pl.BlockSpec((rows, LANES), lambda b: (0, 0)),
-            pl.BlockSpec((rows, LANES), lambda b: (0, 0)),
-            pl.BlockSpec((1, BLK), lambda b: (0, b)),
-            pl.BlockSpec((rows, MAPS), lambda b: (0, 0)),
-            pl.BlockSpec((rows, LANES), lambda b: (0, 0)),
-        ],
-        [
-            pl.BlockSpec((rows, BLK), lambda b: (0, b)),
-            pl.BlockSpec((rows, BLK), lambda b: (0, b)),
-            pl.BlockSpec((count, 1, NSTATE, BLK), lambda b: (0, b, 0, 0)),
-        ],
-        [
             jax.ShapeDtypeStruct((rows, INNER), f32),
-            jax.ShapeDtypeStruct((rows, INNER), bf16),
             jax.ShapeDtypeStruct((count, NB, NSTATE, BLK), f32),
-        ],
-        (back, mixture, gate, inverse, mean, gain_row, act, cum),
-        scratch=[pltpu.VMEM((count, 2, NSTATE, length), bf16)],
-        cost=(10**9, 2 * 10**7, 10**7),
+            jax.ShapeDtypeStruct((rows, D), f32),
+            jax.ShapeDtypeStruct((D, INNER), bf16),
+        ],
+        (g, valid, mixture, gate, inverse, gain_row, weight, act, cum, normed, weight_gate),
+        scratch=[
+            pltpu.VMEM((rows, D), bf16),
+            pltpu.VMEM((rows, BLK), bf16),
+            pltpu.VMEM((NB, rows, BLK), f32),
+            pltpu.VMEM((rows, LANES), f32),
+            pltpu.VMEM((count, 2, NSTATE, length), bf16),
+            pltpu.VMEM((D, rows), bf16),
+        ],
+        cost=(8 * rows * D * INNER, 8 * D * INNER, 10**7),
         carry=carry,
         identity=identity,
     )
@@ -1000,46 +994,6 @@
     )
 
 
-def unproject_gate_kernel(grads_ref, w_ref, normed_ref, back_ref, w_out_ref, turned):
-    step = pl.program_id(0)
-
-    @pl.when(step == 0)
-    def _():
-        turned[...] = normed_ref[...].T
-
-    w_out_ref[...] = dot(turned[...], grads_ref[...]).astype(bf16)
-    product = dot_nt(grads_ref[...], w_ref[...])
-
-    @pl.when(step == 0)
-    def _():
-        back_ref[...] = product
-
-    @pl.when(step > 0)
-    def _():
-        back_ref[...] += product
-
-
-def unproject_gate(grads, weight, normed, carry=None, identity=None):
-    rows = normed.shape[0]
-    return launch(
-        unproject_gate_kernel,
-        "unproject_gate",
-        (INNER // COLS,),
-        [
-            pl.BlockSpec((rows, COLS), lambda n: (0, n)),
-            pl.BlockSpec((D, COLS), lambda n: (0, n)),
-            pl.BlockSpec((rows, D), lambda n: (0, 0)),
-        ],
-        [pl.BlockSpec((rows, D), lambda n: (0, 0)), pl.BlockSpec((D, COLS), lambda n: (0, n))],
-        [jax.ShapeDtypeStruct((rows, D), f32), jax.ShapeDtypeStruct((D, INNER), bf16)],
-        (grads, weight, normed),
-        scratch=[pltpu.VMEM((D, rows), bf16)],
-        cost=(4 * rows * D * INNER, 4 * D * INNER, 0),
-        carry=carry,
-        identity=identity,
-    )
-
-
 def unproject_kernel(
     grads_ref, late_ref, w_ref, normed_ref, h_ref, g_ref, gain_ref, back_ref,
     out_ref, gain_out_ref, w_out_ref,
@@ -1607,13 +1561,12 @@
         cube = proj.reshape(SLOTS, length, TAIL)
         flat = lambda array: array.reshape(rows, -1)
         shaped = lambda array: array.reshape(SLOTS, length, -1)
-        back, mean, grad_gate, partial_out, *sums = unbranch(
-            g, valid, mixture, gate, inverse, gate_row, weight_out, summing([waiting]), next(ids)
+        grad_gate, partial_out, dy, local, back, partial_gate, *sums = turn(
+            g, valid, mixture, gate, inverse, gate_row, weight_out, flat(act), flat(cum), normed, weight_gate, count,
+            summing([waiting]), next(ids),
         )
         if waiting is not None and ours:
             totals[layer + 1][0] = sums[0][0]
-        dy, grads, local = ungate(back, mixture, gate, inverse, mean, gate_row, flat(act), flat(cum), count)
-        back, partial_gate = unproject_gate(grads, weight_gate, normed)
         grads, late, grad_taps, grad_heads, *sums = unmix(
             cube, edge, taps, raw, heads, skip_row, shaped(dy), state, local, decay, cum, size, act, count,
             summing([partial_gate, partial_out]), next(ids),

time: 945 us -> 918 us (0.971)
  Pallas kernels: 890 us -> 864 us
    pallas_call x8 -> x4, Pallas kernels: 158 us -> 120 us  [launch(): pl.pallas_call(kernel, name=name, grid=grid, in_specs=in_specs, out_specs...]
    pallas_call x10, Pallas kernels: 532 us -> 543 us  [launch(): pl.pallas_call(wrapped, name=name, grid=grid, in_specs=list(in_specs) + c...]
where the time goes in v4:
time: 918 us; the launch traced here: 914 us
  Pallas kernels  864 us (94%)
  local copies, waits for them, and re-layouts  32.3 us (4%)
  other arithmetic  15.3 us (2%)
    pallas_call x10, Pallas kernels, launch(): pl.pallas_call(wrapped, name=name, grid=grid, in_specs=list(in_specs) + c...  543 us
    pallas_call x2, Pallas kernels, alone(): pl.pallas_call(kernel, name=name, grid=(1,), in_specs=exchange.in_specs,...  200 us
    pallas_call x4, Pallas kernels, launch(): pl.pallas_call(kernel, name=name, grid=grid, in_specs=in_specs, out_specs...  120 us

profile of v4, /device:TPU:0, one launch (start us, length us, event | category | flops | bytes accessed | tf_op | source)
XLA Modules:
  0.0 913.9 jit_solution(11557281536552073421)
XLA Ops:
  0.7 0.9 rev.16
  1.6 0.8 fusion.5
  2.3 0.8 fusion.6
  3.1 0.8 slice_bitcast_fusion.6
  3.9 1.3 fusion.7
  6.5 0.7 broadcast_select_fusion
  7.2 0.8 reshape.193
  8.0 0.8 pad_maximum_fusion.5
  8.8 0.6 pad_bitcast_fusion.1.refs_0_
  9.4 0.6 pad.41.refs_7_
  10.0 0.6 pad.44.refs_7_
  10.7 0.7 reshape_reshape.32.refs_8_
  11.4 0.7 reshape_reshape.31.refs_8_
  12.1 0.8 broadcast_in_dim.14.refs_8_.valid_ref.refs_1_
  13.0 1.9 slice_bitcast_fusion
  14.9 1.9 slice_bitcast_fusion.1
  16.8 0.9 fusion.1
  17.7 2.0 reverse_select_fusion.1
  19.7 1.1 copy-done.1
  20.7 1.9 reverse_select_fusion.3
  22.6 127.6 %gather.1 = (bf16[2,2,2,4,16,128]{5,4,3,2,1,0:T(8,128)(2,1)}, bf16[2,2,2,4,48,3584]{5,4,3,2,1,0:T(8,128)(2,1)}, bf16[2,2,2,4,48,3072]{5,4,3,2,1,0:T(8,128)(2,1)}, bf16[2,2,2,4,96,1536]{5,4,3,2,1,0:T(8,128)(2,1)}) custom-call(bf16[16,128]{1,0:T(8,128)(2,1)} %pad_bitcast_fusion.1.refs_0_, bf16[48,3584]{1,0:T(8,128)(2,1)} %get-tuple-element.181.refs_1_, ...), custom_call_target="tpu_custom_call" | custom-call | tf_op jit(solution)/shard_map/gather/pallas_call | solution.py:1396
  150.2 0.9 copy.53
  151.2 0.2 reshape.232
  151.4 0.2 slice_reduce_fusion
  151.5 0.7 slice.172.gain_ref
  152.2 0.7 slice.163.refs_5_
  153.0 0.2 slice.193
  153.2 0.2 reshape.198
  153.4 0.7 slice.166.refs_1_.gain_ref
  154.2 0.7 slice.154.refs_1_.gain_ref
  155.0 0.7 pad.39.refs_2_.refs_5_
  155.7 0.7 pad.42.refs_2_.refs_5_
  156.3 20.9 %project.2 = (f32[512,3584]{1,0:T(8,128)}, f32[512,128]{1,0:T(8,128)}, bf16[512,1536]{1,0:T(8,128)(2,1)}, f32[2,8,3584]{2,1,0:T(8,128)}, bf16[2,2,2,4,48,3072]{5...) custom-call(f32[512,1536]{1,0:T(8,128)} %bitcast.111, ...), custom_call_target="tpu_custom_call", output_to_operand_aliasing={{4}: (4, {}), {5}: (5, {})} | custom-call | flops 5637144576 | bytes 11010048 | tf_op jit(solution)/shard_map/project/pallas_call | solution.py:78
  177.3 49.5 %mix.2 = (f32[2,256,3072]{2,1,0:T(8,128)}, bf16[6,128,512]{2,1,0:T(8,128)(2,1)}, f32[2,256,128]{2,1,0:T(8,128)}, f32[2,256,128]{2,1,0:T(8,128)}, f32[2,256,256]{...) custom-call(f32[2,256,3584]{2,1,0:T(8,128)} %bitcast.103, ...), custom_call_target="tpu_custom_call", output_to_operand_aliasing={{6}: (10, {}), {7}: (11, {})} | custom-call | flops 6000000000 | bytes 10000000 | tf_op jit(solution)/shard_map/mix/pallas_call | solution.py:78
  226.8 45.3 %project_gate.2 = (f32[512,3072]{1,0:T(8,128)}, bf16[2,2,2,4,96,1536]{5,4,3,2,1,0:T(8,128)(2,1)}, bf16[2,2,2,4,48,3584]{5,4,3,2,1,0:T(8,128)(2,1)}, bf16[2,2,2,4,48,3072]{5,4,3,2,1,0:T(8,128)(2,1)}) custom-call(bf16[512,1536]{1,0:T(8,128)(2,1)} %get-tuple-element.102.refs_0_.refs_9_.normed_ref, ...), custom_call_target="tpu_custom_call", output_to_operand_aliasing={{1}: (3, {}), {2}: (4, {})} | custom-call | flops 4831838208 | bytes 9437184 | tf_op jit(solution)/shard_map/project_gate/pallas_call | solution.py:78
  272.1 49.2 %branch.2 = (f32[512,1536]{1,0:T(8,128)}, f32[512,3072]{1,0:T(8,128)}, f32[512,128]{1,0:T(8,128)}, bf16[2,2,2,4,48,3584]{5,4,3,2,1,0:T(8,128)(2,1)}, bf16[2,2,2,...) custom-call(f32[512,3072]{1,0:T(8,128)} %bitcast.118, ...), custom_call_target="tpu_custom_call", output_to_operand_aliasing={{3}: (11, {}), {4}: (12, {})} | custom-call | flops 4831838208 | bytes 9437184 | tf_op jit(solution)/shard_map/branch/pallas_call | solution.py:78
  321.3 26.4 %project.3 = (f32[512,3584]{1,0:T(8,128)}, f32[512,128]{1,0:T(8,128)}, bf16[512,1536]{1,0:T(8,128)(2,1)}, f32[2,8,3584]{2,1,0:T(8,128)}, bf16[2,2,2,4,48,3072]{5...) custom-call(f32[512,1536]{1,0:T(8,128)} %get-tuple-element.113.refs_0_.h, ...), custom_call_target="tpu_custom_call", output_to_operand_aliasing={{4}: (4, {}), {5}: (5, {})} | custom-call | flops 5637144576 | bytes 11010048 | tf_op jit(solution)/shard_map/project/pallas_call | solution.py:78
  347.7 42.8 %mix.3 = (f32[2,256,3072]{2,1,0:T(8,128)}, bf16[6,128,512]{2,1,0:T(8,128)(2,1)}, f32[2,256,128]{2,1,0:T(8,128)}, f32[2,256,128]{2,1,0:T(8,128)}, f32[2,256,256]{...) custom-call(f32[2,256,3584]{2,1,0:T(8,128)} %bitcast.107, ...), custom_call_target="tpu_custom_call", output_to_operand_aliasing={{6}: (9, {}), {7}: (10, {})} | custom-call | flops 6000000000 | bytes 10000000 | tf_op jit(solution)/shard_map/mix/pallas_call | solution.py:78
  390.5 11.6 %project_gate.3 = (f32[512,3072]{1,0:T(8,128)}, bf16[2,2,2,4,96,1536]{5,4,3,2,1,0:T(8,128)(2,1)}) custom-call(bf16[512,1536]{1,0:T(8,128)(2,1)} %get-tuple-element.123.refs_0_.normed_ref, bf16[1536,3072]{1,0:T(8,128)(2,1)} %bitcast.95, bf16[2,2,2,4,96,1536]{5,4,3,2,1,0:T(8,128)(2,1)} %get-tuple-element.125.refs_2_), custom_call_target="tpu_custom_call", output_to_operand_aliasing={{1}: (2, {})} | custom-call | flops 4831838208 | bytes 9437184 | tf_op jit(solution)/shard_map/project_gate/pallas_call | solution.py:78
  402.2 20.2 %branch.3 = (f32[512,1536]{1,0:T(8,128)}, f32[512,3072]{1,0:T(8,128)}, f32[512,128]{1,0:T(8,128)}) custom-call(f32[512,3072]{1,0:T(8,128)} %bitcast.117, f32[512,3072]{1,0:T(8,128)} %get-tuple-element.126.gate_ref, f32[512,256]{1,0:T(8,128)} %bitcast.133, f32[512,128]{1,0:T(8,128)} %bitcast.145, bf16[1,6,128,512]{3,2,1,0:T(8,128)(2,1)} %bitcast.127, ...), custom_call_target="tpu_custom_call" | custom-call | flops 4831838208 | bytes 9437184 | tf_op jit(solution)/shard_map/branch/pallas_call | solution.py:46
  422.4 48.5 %turn.2 = (f32[8,3072]{1,0:T(8,128)}, bf16[3072,1536]{1,0:T(8,128)(2,1)}, f32[512,3072]{1,0:T(8,128)}, f32[1,6,128,512]{3,2,1,0:T(8,128)}, f32[512,1536]{1,0:T(8,128)}, /*index=5*/bf16[1536,3072]{1,0:T(8,128)(2,1)}) custom-call(f32[512,1536]{1,0:T(8,128)} %bitcast.119, f32[512,128]{1,0:T(8,128)} %broadcast_in_dim.14.refs_8_.valid_ref.refs_1_, ...), custom_call_target="tpu_custom_call" | custom-call | flops 19327352832 | bytes 37748736 | tf_op jit(solution)/shard_map/turn/pallas_call | solution.py:46
  470.9 109.3 %unmix.2 = (bf16[2,256,3584]{2,1,0:T(8,128)(2,1)}, f32[2,8,3584]{2,1,0:T(8,128)}, f32[2,8,3584]{2,1,0:T(8,128)}, f32[2,8,128]{2,1,0:T(8,128)}, f32[48,3072]{1,0:T(8,128)}, /*index=5*/f32[96,1536]{1,0:T(8,128)}) custom-call(f32[2,256,3584]{2,1,0:T(8,128)} %bitcast.109, f32[2,8,3584]{2,1,0:T(8,128)} %get-tuple-element.118.refs_1_.refs_4_, ...), custom_call_target="tpu_custom_call" | custom-call | flops 20000000000 | bytes 20000000 | tf_op jit(solution)/shard_map/unmix/pallas_call | solution.py:78
  580.2 25.5 %unproject.2 = (f32[512,1536]{1,0:T(8,128)}, f32[8,1536]{1,0:T(8,128)}, bf16[1536,3584]{1,0:T(8,128)(2,1)}) custom-call(bf16[512,3584]{1,0:T(8,128)(2,1)} %bitcast.161, f32[2,8,3584]{2,1,0:T(8,128)} %get-tuple-element.141.late_ref, bf16[1536,3584]{1,0:T(8,128)(2,1)} %bitcast.100, bf16[512,1536]{1,0:T(8,128)(2,1)} %get-tuple-element.123.refs_0_.normed_ref, ...), custom_call_target="tpu_custom_call" | custom-call | flops 11274289152 | bytes 22020096 | tf_op jit(solution)/shard_map/unproject/pallas_call | solution.py:46
  605.6 80.7 %turn.3 = (f32[8,3072]{1,0:T(8,128)}, bf16[3072,1536]{1,0:T(8,128)(2,1)}, f32[512,3072]{1,0:T(8,128)}, f32[1,6,128,512]{3,2,1,0:T(8,128)}, f32[512,1536]{1,0:T(8...) custom-call(f32[512,1536]{1,0:T(8,128)} %get-tuple-element.143.refs_0_.g_ref, ...), custom_call_target="tpu_custom_call" | custom-call | flops 19327352832 | bytes 37748736 | tf_op jit(solution)/shard_map/turn/pallas_call | solution.py:78
  686.3 107.7 %unmix.3 = (bf16[2,256,3584]{2,1,0:T(8,128)(2,1)}, f32[2,8,3584]{2,1,0:T(8,128)}, f32[2,8,3584]{2,1,0:T(8,128)}, f32[2,8,128]{2,1,0:T(8,128)}, f32[48,3072]{1,0:T(8,128)}, /*index=5*/f32[96,1536]{1,0:T(8,128)}) custom-call(f32[2,256,3584]{2,1,0:T(8,128)} %bitcast.105, f32[2,8,3584]{2,1,0:T(8,128)} %get-tuple-element.97.refs_1_.refs_4_, ...), custom_call_target="tpu_custom_call" | custom-call | flops 20000000000 | bytes 20000000 | tf_op jit(solution)/shard_map/unmix/pallas_call | solution.py:78
  794.0 25.7 %unproject.3 = (f32[512,1536]{1,0:T(8,128)}, f32[8,1536]{1,0:T(8,128)}, bf16[1536,3584]{1,0:T(8,128)(2,1)}) custom-call(bf16[512,3584]{1,0:T(8,128)(2,1)} %bitcast.162, f32[2,8,3584]{2,1,0:T(8,128)} %get-tuple-element.154.late_ref, bf16[1536,3584]{1,0:T(8,128)(2,1)} %bitcast.116, bf16[512,1536]{1,0:T(8,128)(2,1)} %get-tuple-element.102.refs_0_.refs_9_.normed_ref, ...), custom_call_target="tpu_custom_call" | custom-call | flops 11274289152 | bytes 22020096 | tf_op jit(solution)/shard_map/unproject/pallas_call | solution.py:46
  819.7 6.8 reverse_select_fusion
  826.6 0.6 pad.46.refs_2_
  827.2 0.8 slice.173
  828.0 0.8 slice.174
  828.8 0.9 slice.177
  829.7 0.9 slice.178
  831.7 0.1 reshape.225
  831.8 0.8 copy.50
  832.6 72.7 %reduce.17 = (f32[48,3584]{1,0:T(8,128)}, f32[16,128]{1,0:T(8,128)}, f32[8,128]{1,0:T(8,128)}) custom-call(bf16[2,2,2,4,48,3584]{5,4,3,2,1,0:T(8,128)(2,1)} %bitcast.114, f32[2,2,2,4,16,128]{5,4,3,2,1,0:T(8,128)} %bitcast.123, f32[8,128]{1,0:T(8,128)} %pad.46.refs_2_), custom_call_target="tpu_custom_call" | custom-call | tf_op jit(solution)/shard_map/reduce/pallas_call | solution.py:1396
  905.3 0.9 reshape.228
  906.2 0.6 slice.204
  906.8 0.6 slice.202
  907.5 0.7 reshape.229
  908.1 0.7 reshape.230
  908.8 0.6 fusion.4
  909.4 1.1 pad_maximum_fusion.1
  910.5 1.2 slice.183
  912.0 1.6 pad_maximum_fusion
  (64 shorter events, 2.0 us)
Async XLA Ops:
  0.6 17.0 %copy-start = (f32[2,256,1536]{2,1,0:T(8,128)S(1)}, f32[2,256,1536]{2,1,0:T(8,128)}, u32[]{:S(2)}) copy-start(f32[2,256,1536]{2,1,0:T(8,128)} %param.12) | copy-start | bytes 9437188
  12.1 4.7 slice-start
  17.7 3.0 copy-start.1
  794.0 25.7 %copy-start.2 = (f32[512,1536]{1,0:T(8,128)S(1)}, f32[512,1536]{1,0:T(8,128)}, u32[]{:S(2)}) copy-start(f32[512,1536]{1,0:T(8,128)} %get-tuple-element.131) | copy-start | bytes 9437188
  819.7 6.8 copy-start.11
  819.7 6.8 copy-start.10
  819.7 11.1 %copy-start.9 = (f32[2,8,3584]{2,1,0:T(8,128)S(1)}, f32[2,8,3584]{2,1,0:T(8,128)}, u32[]{:S(2)}) copy-start(f32[2,8,3584]{2,1,0:T(8,128)} %get-tuple-element.160) | copy-start | bytes 688132
  819.7 11.1 %copy-start.8 = (f32[2,8,3584]{2,1,0:T(8,128)S(1)}, f32[2,8,3584]{2,1,0:T(8,128)}, u32[]{:S(2)}) copy-start(f32[2,8,3584]{2,1,0:T(8,128)} %get-tuple-element.161) | copy-start | bytes 688132
  832.6 76.8 %copy-start.6 = (f32[96,1536]{1,0:T(8,128)S(1)}, f32[96,1536]{1,0:T(8,128)}, u32[]{:S(2)}) copy-start(f32[96,1536]{1,0:T(8,128)} %get-tuple-element.172) | copy-start | bytes 1769476
  832.6 76.8 %copy-start.7 = (f32[96,1536]{1,0:T(8,128)S(1)}, f32[96,1536]{1,0:T(8,128)}, u32[]{:S(2)}) copy-start(f32[96,1536]{1,0:T(8,128)} %get-tuple-element.171) | copy-start | bytes 1769476
  905.3 6.4 copy-start.5
  905.3 6.5 copy-start.3
  910.5 1.4 copy-start.4

commit v5 on v4

--- a/solution.py
+++ b/solution.py
@@ -35,7 +35,7 @@
 
 def launch(
     kernel, name, grid, in_specs, out_specs, out_shape, args, scratch=(), cost=None, carry=None, identity=None,
-    relay=False,
+    relay=False, points=1,
 ):
     options = {"compiler_params": params()}
     if cost is not None:
@@ -43,6 +43,8 @@
     if carry is not None or relay:
         options["compiler_params"] = params(collective_id=identity, has_side_effects=True)
     if carry is None:
+        if points > 1:
+            kernel = functools.partial(kernel, lambda point, keep=None: None)
         return pl.pallas_call(
             kernel, name=name, grid=grid, in_specs=in_specs, out_specs=out_specs, out_shape=out_shape,
             scratch_shapes=list(scratch), **options,
@@ -62,14 +64,23 @@
         ticks = carry.ticks(groups[1], groups[3], refs[at:], relay)
         plan = {}
         for number, tick in enumerate(ticks[:-1]):
-            plan.setdefault(number * total // (len(ticks) - 1), []).append(tick)
-        for moment, members in plan.items():
-            @pl.when(step == moment)
-            def _(members=members):
-                for member in members:
-                    member()
-
-        kernel(*groups[0], *groups[2], *groups[4])
+            moment, point = divmod(number * total * points // (len(ticks) - 1), points)
+            plan.setdefault((moment, point), []).append(tick)
+
+        def pump(point, keep=None):
+            for (moment, at_point), members in plan.items():
+                if at_point == point and (keep is None or keep(moment)):
+                    @pl.when(step == moment)
+                    def _(members=members):
+                        for member in members:
+                            member()
+
+        own = (*groups[0], *groups[2], *groups[4])
+        if points > 1:
+            kernel(pump, *own)
+        else:
+            pump(0)
+            kernel(*own)
 
         @pl.when(step == total - 1)
         def _():
@@ -730,11 +741,12 @@
 
 
 def unmix_kernel(
-    relay, edge, alone, count, rows_ref, edge_ref, taps_ref, maps_ref, maps_edge_ref, maps_taps_ref, raw_ref, heads_ref, skip_ref,
+    relay, edge, alone, count, pump, rows_ref, edge_ref, taps_ref, maps_ref, maps_edge_ref, maps_taps_ref, raw_ref, heads_ref, skip_ref,
     dy_ref, state_ref, local_ref, decay_ref, cum_ref, step_ref, act_ref,
     grads_ref, late_ref, taps_out_ref, heads_out_ref,
     extended, maps_extended, inner, d_inner, minus, plus, scales, grad_ext, maps_grad_ext, d_maps, d_cum, d_step, over_rows, sums, *flow,
 ):
+    pump(0)
     turn, block = pl.program_id(0), pl.program_id(1)
     slot = SLOTS - 1 - turn
     length = rows_ref.shape[1]
@@ -840,6 +852,7 @@
             parts.append(jnp.concatenate(pieces, axis=0))
             for j in range(2):
                 over_rows[pl.ds(block * PER + 2 * pair + j, 1), :] = column_sums[j]
+            pump(1 + pair, lambda moment: moment % (NB + 1) < NB)
         intra = jnp.concatenate(parts, axis=1)
         for first, moved in moved_all.items():
             span = length - first
@@ -882,6 +895,8 @@
 
     @pl.when(block == NB)
     def _():
+        for point in range(1, 1 + PER // 2):
+            pump(point, lambda moment: moment % (NB + 1) == NB)
         load_extended(maps_extended, maps_edge_ref, maps_ref)
         convolved = convolve(maps_extended, maps_taps_ref[...], length)
         curve = sigmoid(convolved)
@@ -991,21 +1006,28 @@
         carry=carry,
         identity=identity,
         relay=True,
+        points=1 + PER // 2,
     )
 
 
 def unproject_kernel(
-    grads_ref, late_ref, w_ref, normed_ref, h_ref, g_ref, gain_ref, back_ref,
+    grads_ref, late_ref, w_ref, normed_ref, h_far, g_far, gain_ref, back_far,
     out_ref, gain_out_ref, w_out_ref,
-    total, turned, mended,
+    total, turned, mended, h_ref, g_ref, back_ref, sems,
 ):
     step = pl.program_id(0)
     rows = h_ref.shape[0]
+    copies = [
+        pltpu.make_async_copy(far, near, sems.at[number])
+        for number, (far, near) in enumerate(((h_far, h_ref), (g_far, g_ref), (back_far, back_ref)))
+    ]
     length = rows // SLOTS
 
     @pl.when(step == 0)
     def _():
-        total[...] = back_ref[...]
+        for copy in copies:
+            copy.start()
+        total[...] = jnp.zeros_like(total)
         turned[...] = normed_ref[...].T
 
     mended[...] = grads_ref[...]
@@ -1018,12 +1040,14 @@
 
     @pl.when(step == pl.num_programs(0) - 1)
     def _():
+        for copy in copies:
+            copy.wait()
         gain_out_ref[...] = jnp.zeros_like(gain_out_ref)
 
         def one(span):
             h = h_ref[span, :]
             inverse = lax.rsqrt(jnp.mean(h * h, axis=-1, keepdims=True) + epsilon)
-            back = total[span, :]
+            back = total[span, :] + back_ref[span, :]
             unit = h * inverse
             gain_out_ref[0:1, :] += jnp.sum(back * unit, axis=0, keepdims=True)
             wanted = back * gain_ref[...]
@@ -1044,10 +1068,10 @@
             pl.BlockSpec((SLOTS, 8, COLS), lambda n: (0, 0, n)),
             pl.BlockSpec((D, COLS), lambda n: (0, n)),
             pl.BlockSpec((rows, D), lambda n: (0, 0)),
-            pl.BlockSpec((rows, D), lambda n: (0, 0)),
-            pl.BlockSpec((rows, D), lambda n: (0, 0)),
+            pl.BlockSpec(memory_space=pl.ANY),
+            pl.BlockSpec(memory_space=pl.ANY),
             pl.BlockSpec((1, D), lambda n: (0, 0)),
-            pl.BlockSpec((rows, D), lambda n: (0, 0)),
+            pl.BlockSpec(memory_space=pl.ANY),
         ],
         [
             pl.BlockSpec((rows, D), lambda n: (0, 0)),
@@ -1064,6 +1088,10 @@
             pltpu.VMEM((rows, D), f32),
             pltpu.VMEM((D, rows), bf16),
             pltpu.VMEM((rows, COLS), bf16),
+            pltpu.VMEM((rows, D), f32),
+            pltpu.VMEM((rows, D), f32),
+            pltpu.VMEM((rows, D), f32),
+            pltpu.SemaphoreType.DMA((3,)),
         ],
         cost=(4 * rows * D * TAIL, 4 * D * TAIL, 0),
         carry=carry,
@@ -1585,7 +1613,7 @@
     head_sums = jnp.pad(stacked[3].reshape(-1, HEADS), ((0, 8 - 3 * LAYERS), (0, LANES - HEADS)))
     if ours:
         totals[0][0], mine, head_sums = alone(
-            Reduce([cut(waiting), shares], [(3, 2), (1, 1)], heads=head_sums), "reduce", next(ids)
+            Reduce([cut(waiting), shares], [(3, 4), (1, 1)], heads=head_sums), "reduce", next(ids)
         )
     else:
         totals = [

time: 918 us -> 908 us (0.989)
  Pallas kernels: 864 us -> 851 us
where the time goes in v5:
time: 908 us; the launch traced here: 901 us
  Pallas kernels  851 us (94%)
  local copies, waits for them, and re-layouts  32.3 us (4%)
  other arithmetic  15.3 us (2%)
    pallas_call x10, Pallas kernels, launch(): pl.pallas_call(wrapped, name=name, grid=grid, in_specs=list(in_specs) + c...  539 us
    pallas_call x2, Pallas kernels, alone(): pl.pallas_call(kernel, name=name, grid=(1,), in_specs=exchange.in_specs,...  196 us
    pallas_call x4, Pallas kernels, launch(): pl.pallas_call(kernel, name=name, grid=grid, in_specs=in_specs, out_specs...  115 us

profile of v5, /device:TPU:0, one launch (start us, length us, event | category | flops | bytes accessed | tf_op | source)
XLA Modules:
  0.0 900.9 jit_solution(7347781095162318543)
XLA Ops:
  0.7 0.9 rev.16
  1.6 0.8 fusion.5
  2.3 0.8 fusion.6
  3.1 0.8 slice_bitcast_fusion.6
  3.9 1.3 fusion.7
  6.5 0.7 broadcast_select_fusion
  7.2 0.8 reshape.193
  8.0 0.8 pad_maximum_fusion.5
  8.8 0.6 pad_bitcast_fusion.1.refs_0_
  9.4 0.6 pad.41.refs_7_
  10.0 0.6 pad.44.refs_7_
  10.7 0.7 reshape_reshape.32.refs_8_
  11.4 0.7 reshape_reshape.31.refs_8_
  12.1 0.8 broadcast_in_dim.14.refs_8_.valid_ref.refs_1_
  13.0 1.9 slice_bitcast_fusion
  14.9 1.9 slice_bitcast_fusion.1
  16.8 0.9 fusion.1
  17.7 2.0 reverse_select_fusion.1
  19.7 1.1 copy-done.1
  20.7 1.9 reverse_select_fusion.3
  22.6 127.6 %gather.1 = (bf16[2,2,2,4,16,128]{5,4,3,2,1,0:T(8,128)(2,1)}, bf16[2,2,2,4,48,3584]{5,4,3,2,1,0:T(8,128)(2,1)}, bf16[2,2,2,4,48,3072]{5,4,3,2,1,0:T(8,128)(2,1)}, bf16[2,2,2,4,96,1536]{5,4,3,2,1,0:T(8,128)(2,1)}) custom-call(bf16[16,128]{1,0:T(8,128)(2,1)} %pad_bitcast_fusion.1.refs_0_, bf16[48,3584]{1,0:T(8,128)(2,1)} %get-tuple-element.181.refs_1_, ...), custom_call_target="tpu_custom_call" | custom-call | tf_op jit(solution)/shard_map/gather/pallas_call | solution.py:1424
  150.2 0.9 copy.53
  151.2 0.2 reshape.232
  151.4 0.2 slice_reduce_fusion
  151.5 0.7 slice.172.gain_ref
  152.2 0.7 slice.163.refs_5_
  153.0 0.2 slice.193
  153.2 0.2 reshape.198
  153.4 0.7 slice.166.refs_1_.gain_ref
  154.2 0.7 slice.154.refs_1_.gain_ref
  155.0 0.7 pad.39.refs_2_.refs_5_
  155.7 0.7 pad.42.refs_2_.refs_5_
  156.3 20.1 %project.2 = (f32[512,3584]{1,0:T(8,128)}, f32[512,128]{1,0:T(8,128)}, bf16[512,1536]{1,0:T(8,128)(2,1)}, f32[2,8,3584]{2,1,0:T(8,128)}, bf16[2,2,2,4,48,3072]{5...) custom-call(f32[512,1536]{1,0:T(8,128)} %bitcast.111, ...), custom_call_target="tpu_custom_call", output_to_operand_aliasing={{4}: (4, {}), {5}: (5, {})} | custom-call | flops 5637144576 | bytes 11010048 | tf_op jit(solution)/shard_map/project/pallas_call | solution.py:89
  176.5 48.9 %mix.2 = (f32[2,256,3072]{2,1,0:T(8,128)}, bf16[6,128,512]{2,1,0:T(8,128)(2,1)}, f32[2,256,128]{2,1,0:T(8,128)}, f32[2,256,128]{2,1,0:T(8,128)}, f32[2,256,256]{...) custom-call(f32[2,256,3584]{2,1,0:T(8,128)} %bitcast.103, ...), custom_call_target="tpu_custom_call", output_to_operand_aliasing={{6}: (10, {}), {7}: (11, {})} | custom-call | flops 6000000000 | bytes 10000000 | tf_op jit(solution)/shard_map/mix/pallas_call | solution.py:89
  225.4 42.7 %project_gate.2 = (f32[512,3072]{1,0:T(8,128)}, bf16[2,2,2,4,96,1536]{5,4,3,2,1,0:T(8,128)(2,1)}, bf16[2,2,2,4,48,3584]{5,4,3,2,1,0:T(8,128)(2,1)}, bf16[2,2,2,4,48,3072]{5,4,3,2,1,0:T(8,128)(2,1)}) custom-call(bf16[512,1536]{1,0:T(8,128)(2,1)} %get-tuple-element.102.refs_0_.refs_9_.normed_ref, ...), custom_call_target="tpu_custom_call", output_to_operand_aliasing={{1}: (3, {}), {2}: (4, {})} | custom-call | flops 4831838208 | bytes 9437184 | tf_op jit(solution)/shard_map/project_gate/pallas_call | solution.py:89
  268.1 48.1 %branch.2 = (f32[512,1536]{1,0:T(8,128)}, f32[512,3072]{1,0:T(8,128)}, f32[512,128]{1,0:T(8,128)}, bf16[2,2,2,4,48,3584]{5,4,3,2,1,0:T(8,128)(2,1)}, bf16[2,2,2,...) custom-call(f32[512,3072]{1,0:T(8,128)} %bitcast.118, ...), custom_call_target="tpu_custom_call", output_to_operand_aliasing={{3}: (11, {}), {4}: (12, {})} | custom-call | flops 4831838208 | bytes 9437184 | tf_op jit(solution)/shard_map/branch/pallas_call | solution.py:89
  316.3 25.0 %project.3 = (f32[512,3584]{1,0:T(8,128)}, f32[512,128]{1,0:T(8,128)}, bf16[512,1536]{1,0:T(8,128)(2,1)}, f32[2,8,3584]{2,1,0:T(8,128)}, bf16[2,2,2,4,48,3072]{5...) custom-call(f32[512,1536]{1,0:T(8,128)} %get-tuple-element.113.refs_0_.h, ...), custom_call_target="tpu_custom_call", output_to_operand_aliasing={{4}: (4, {}), {5}: (5, {})} | custom-call | flops 5637144576 | bytes 11010048 | tf_op jit(solution)/shard_map/project/pallas_call | solution.py:89
  341.3 42.9 %mix.3 = (f32[2,256,3072]{2,1,0:T(8,128)}, bf16[6,128,512]{2,1,0:T(8,128)(2,1)}, f32[2,256,128]{2,1,0:T(8,128)}, f32[2,256,128]{2,1,0:T(8,128)}, f32[2,256,256]{...) custom-call(f32[2,256,3584]{2,1,0:T(8,128)} %bitcast.107, ...), custom_call_target="tpu_custom_call", output_to_operand_aliasing={{6}: (9, {}), {7}: (10, {})} | custom-call | flops 6000000000 | bytes 10000000 | tf_op jit(solution)/shard_map/mix/pallas_call | solution.py:89
  384.2 13.4 %project_gate.3 = (f32[512,3072]{1,0:T(8,128)}, bf16[2,2,2,4,96,1536]{5,4,3,2,1,0:T(8,128)(2,1)}) custom-call(bf16[512,1536]{1,0:T(8,128)(2,1)} %get-tuple-element.123.refs_0_.normed_ref, bf16[1536,3072]{1,0:T(8,128)(2,1)} %bitcast.95, bf16[2,2,2,4,96,1536]{5,4,3,2,1,0:T(8,128)(2,1)} %get-tuple-element.125.refs_2_), custom_call_target="tpu_custom_call", output_to_operand_aliasing={{1}: (2, {})} | custom-call | flops 4831838208 | bytes 9437184 | tf_op jit(solution)/shard_map/project_gate/pallas_call | solution.py:89
  397.6 20.2 %branch.3 = (f32[512,1536]{1,0:T(8,128)}, f32[512,3072]{1,0:T(8,128)}, f32[512,128]{1,0:T(8,128)}) custom-call(f32[512,3072]{1,0:T(8,128)} %bitcast.117, f32[512,3072]{1,0:T(8,128)} %get-tuple-element.126.gate_ref, f32[512,256]{1,0:T(8,128)} %bitcast.133, f32[512,128]{1,0:T(8,128)} %bitcast.145, bf16[1,6,128,512]{3,2,1,0:T(8,128)(2,1)} %bitcast.127, ...), custom_call_target="tpu_custom_call" | custom-call | flops 4831838208 | bytes 9437184 | tf_op jit(solution)/shard_map/branch/pallas_call | solution.py:48
  417.8 48.5 %turn.2 = (f32[8,3072]{1,0:T(8,128)}, bf16[3072,1536]{1,0:T(8,128)(2,1)}, f32[512,3072]{1,0:T(8,128)}, f32[1,6,128,512]{3,2,1,0:T(8,128)}, f32[512,1536]{1,0:T(8,128)}, /*index=5*/bf16[1536,3072]{1,0:T(8,128)(2,1)}) custom-call(f32[512,1536]{1,0:T(8,128)} %bitcast.119, f32[512,128]{1,0:T(8,128)} %broadcast_in_dim.14.refs_8_.valid_ref.refs_1_, ...), custom_call_target="tpu_custom_call" | custom-call | flops 19327352832 | bytes 37748736 | tf_op jit(solution)/shard_map/turn/pallas_call | solution.py:48
  466.3 108.0 %unmix.2 = (bf16[2,256,3584]{2,1,0:T(8,128)(2,1)}, f32[2,8,3584]{2,1,0:T(8,128)}, f32[2,8,3584]{2,1,0:T(8,128)}, f32[2,8,128]{2,1,0:T(8,128)}, f32[48,3072]{1,0:T(8,128)}, /*index=5*/f32[96,1536]{1,0:T(8,128)}) custom-call(f32[2,256,3584]{2,1,0:T(8,128)} %bitcast.109, f32[2,8,3584]{2,1,0:T(8,128)} %get-tuple-element.118.refs_1_.refs_4_, ...), custom_call_target="tpu_custom_call" | custom-call | flops 20000000000 | bytes 20000000 | tf_op jit(solution)/shard_map/unmix/pallas_call | solution.py:89
  574.3 23.1 %unproject.2 = (f32[512,1536]{1,0:T(8,128)}, f32[8,1536]{1,0:T(8,128)}, bf16[1536,3584]{1,0:T(8,128)(2,1)}) custom-call(bf16[512,3584]{1,0:T(8,128)(2,1)} %bitcast.161, f32[2,8,3584]{2,1,0:T(8,128)} %get-tuple-element.141.late_ref, bf16[1536,3584]{1,0:T(8,128)(2,1)} %bitcast.100, bf16[512,1536]{1,0:T(8,128)(2,1)} %get-tuple-element.123.refs_0_.normed_ref, ...), custom_call_target="tpu_custom_call" | custom-call | flops 11274289152 | bytes 22020096 | tf_op jit(solution)/shard_map/unproject/pallas_call | solution.py:48
  597.5 82.2 %turn.3 = (f32[8,3072]{1,0:T(8,128)}, bf16[3072,1536]{1,0:T(8,128)(2,1)}, f32[512,3072]{1,0:T(8,128)}, f32[1,6,128,512]{3,2,1,0:T(8,128)}, f32[512,1536]{1,0:T(8...) custom-call(f32[512,1536]{1,0:T(8,128)} %get-tuple-element.143.refs_0_.g_far, ...), custom_call_target="tpu_custom_call" | custom-call | flops 19327352832 | bytes 37748736 | tf_op jit(solution)/shard_map/turn/pallas_call | solution.py:89
  679.7 107.3 %unmix.3 = (bf16[2,256,3584]{2,1,0:T(8,128)(2,1)}, f32[2,8,3584]{2,1,0:T(8,128)}, f32[2,8,3584]{2,1,0:T(8,128)}, f32[2,8,128]{2,1,0:T(8,128)}, f32[48,3072]{1,0:T(8,128)}, /*index=5*/f32[96,1536]{1,0:T(8,128)}) custom-call(f32[2,256,3584]{2,1,0:T(8,128)} %bitcast.105, f32[2,8,3584]{2,1,0:T(8,128)} %get-tuple-element.97.refs_1_.refs_4_, ...), custom_call_target="tpu_custom_call" | custom-call | flops 20000000000 | bytes 20000000 | tf_op jit(solution)/shard_map/unmix/pallas_call | solution.py:89
  787.0 23.5 %unproject.3 = (f32[512,1536]{1,0:T(8,128)}, f32[8,1536]{1,0:T(8,128)}, bf16[1536,3584]{1,0:T(8,128)(2,1)}) custom-call(bf16[512,3584]{1,0:T(8,128)(2,1)} %bitcast.162, f32[2,8,3584]{2,1,0:T(8,128)} %get-tuple-element.154.late_ref, bf16[1536,3584]{1,0:T(8,128)(2,1)} %bitcast.116, bf16[512,1536]{1,0:T(8,128)(2,1)} %get-tuple-element.102.refs_0_.refs_9_.normed_ref, ...), custom_call_target="tpu_custom_call" | custom-call | flops 11274289152 | bytes 22020096 | tf_op jit(solution)/shard_map/unproject/pallas_call | solution.py:48
  810.6 6.8 reverse_select_fusion
  817.5 0.6 pad.46.refs_2_
  818.0 0.8 slice.173
  818.9 0.8 slice.174
  819.7 0.9 slice.177
  820.6 0.9 slice.178
  822.5 0.1 reshape.225
  822.7 0.8 copy.50
  823.4 68.9 %reduce.17 = (f32[48,3584]{1,0:T(8,128)}, f32[16,128]{1,0:T(8,128)}, f32[8,128]{1,0:T(8,128)}) custom-call(bf16[2,2,2,4,48,3584]{5,4,3,2,1,0:T(8,128)(2,1)} %bitcast.114, f32[2,2,2,4,16,128]{5,4,3,2,1,0:T(8,128)} %bitcast.123, f32[8,128]{1,0:T(8,128)} %pad.46.refs_2_), custom_call_target="tpu_custom_call" | custom-call | tf_op jit(solution)/shard_map/reduce/pallas_call | solution.py:1424
  892.3 0.9 reshape.228
  893.2 0.6 slice.204
  893.8 0.6 slice.202
  894.5 0.7 reshape.229
  895.2 0.7 reshape.230
  895.8 0.6 fusion.4
  896.4 1.1 pad_maximum_fusion.1
  897.5 1.2 slice.183
  899.0 1.6 pad_maximum_fusion
  (64 shorter events, 2.0 us)
Async XLA Ops:
  0.6 17.0 %copy-start = (f32[2,256,1536]{2,1,0:T(8,128)S(1)}, f32[2,256,1536]{2,1,0:T(8,128)}, u32[]{:S(2)}) copy-start(f32[2,256,1536]{2,1,0:T(8,128)} %param.12) | copy-start | bytes 9437188
  12.1 4.7 slice-start
  17.7 3.0 copy-start.1
  787.0 23.5 %copy-start.2 = (f32[512,1536]{1,0:T(8,128)S(1)}, f32[512,1536]{1,0:T(8,128)}, u32[]{:S(2)}) copy-start(f32[512,1536]{1,0:T(8,128)} %get-tuple-element.131) | copy-start | bytes 9437188
  810.6 6.8 copy-start.11
  810.6 6.8 copy-start.10
  810.6 11.1 %copy-start.9 = (f32[2,8,3584]{2,1,0:T(8,128)S(1)}, f32[2,8,3584]{2,1,0:T(8,128)}, u32[]{:S(2)}) copy-start(f32[2,8,3584]{2,1,0:T(8,128)} %get-tuple-element.160) | copy-start | bytes 688132
  810.6 11.1 %copy-start.8 = (f32[2,8,3584]{2,1,0:T(8,128)S(1)}, f32[2,8,3584]{2,1,0:T(8,128)}, u32[]{:S(2)}) copy-start(f32[2,8,3584]{2,1,0:T(8,128)} %get-tuple-element.161) | copy-start | bytes 688132
  823.4 73.0 %copy-start.6 = (f32[96,1536]{1,0:T(8,128)S(1)}, f32[96,1536]{1,0:T(8,128)}, u32[]{:S(2)}) copy-start(f32[96,1536]{1,0:T(8,128)} %get-tuple-element.172) | copy-start | bytes 1769476
  823.4 73.0 %copy-start.7 = (f32[96,1536]{1,0:T(8,128)S(1)}, f32[96,1536]{1,0:T(8,128)}, u32[]{:S(2)}) copy-start(f32[96,1536]{1,0:T(8,128)} %get-tuple-element.171) | copy-start | bytes 1769476
  892.3 6.4 copy-start.5
  892.3 6.5 copy-start.3
  897.5 1.4 copy-start.4
